TPU v7x, 32 devices: a whole 2x2x4 slice. The times are simulated.
32 devices in a mesh: gx: 4 (over y, core), gy: 8 (over z, x).
Axes of the slice: x: 2, y: 2, z: 4, core: 2. Of those that a mesh axis runs over, the one named last changes fastest.
Arguments:
- volume: bfloat16 [32, 128, 2048], P('gx', 'gy'), may hold values from -6 to 6
- cotangent: bfloat16 [32, 128, 2048], P('gx', 'gy'), may hold values from -6 to 6
- weight: bfloat16 [3, 3, 3, 32, 32], replicated, may hold values from -0.21875 to 0.21875
- bias: float32 [32], replicated, may hold values from -4 to 4
Outputs:
- data_grad: bfloat16 [32, 128, 2048], P('gx', 'gy')
- filter_grad: float32 [3, 3, 3, 32, 32], replicated
- bias_grad: float32 [32], replicated
All inputs are finite; a program needn't handle non-finite values.
Results may differ from a plain program's by a relative error of at most 0.008.
Values may be sent and summed in bfloat16 or wider, within the bound.
No kernel may reach another device: no remote copies, remote signals or barrier semaphores. Data moves between devices by JAX's collectives and lax.ppermute only.
A program may use at most 128 MiB of HBM per device.

v0:
```python
import math

import jax
import jax.numpy as jnp
from jax import lax
from jax.experimental import pallas as pl
from jax.experimental.pallas import tpu as pltpu
from jax.sharding import PartitionSpec as P

C = 32
Z = 64
T = 128
ROW = 8 * T
F32 = jnp.float32
BF16 = jnp.bfloat16
VMEM_LIMIT = 48 * 1024 * 1024
VMEM = pl.BlockSpec(memory_space=pltpu.VMEM)
ANY = pl.BlockSpec(memory_space=pl.ANY)


def call(body, out_shape, scratch_shapes, flops, *args, in_specs=None, out_specs=None, aliases=None):
    traffic = sum(math.prod(a.shape) * a.dtype.itemsize for a in (*args, *jax.tree.leaves(out_shape)))
    return pl.pallas_call(
        body,
        out_shape=out_shape,
        in_specs=in_specs or [VMEM] * len(args),
        out_specs=out_specs or jax.tree.map(lambda _: VMEM, out_shape),
        scratch_shapes=scratch_shapes,
        input_output_aliases=aliases or {},
        compiler_params=pltpu.CompilerParams(vmem_limit_bytes=VMEM_LIMIT),
        cost_estimate=pl.CostEstimate(flops=flops, bytes_accessed=traffic, transcendentals=0),
    )(*args)


def like(dtype, *shape):
    return jax.ShapeDtypeStruct(shape, dtype)


def lane(shape):
    return lax.broadcasted_iota(jnp.int32, shape, len(shape) - 1)


def swap_halves(a):
    return pltpu.roll(a, T // 2, a.ndim - 1)


def halves(low, high):
    return jnp.where(lane(low.shape) < T // 2, low, high)


def exchange_halves(a, b):
    mixed = swap_halves(halves(b, a))
    return halves(a, mixed), halves(mixed, b)


def from_below(a):
    return jnp.where(lane(a.shape) % Z == 0, 0.0, pltpu.roll(a, 1, a.ndim - 1))


def from_above(a):
    return jnp.where(lane(a.shape) % Z == Z - 1, 0.0, pltpu.roll(a, T - 1, a.ndim - 1))


def tile(t):
    return slice(t * T, t * T + T)


def to_channels(rows, stage):
    rows = rows.astype(F32)
    for pair in range(C // 2):
        even, odd = exchange_halves(rows[:8, tile(pair)], rows[8:, tile(pair)])
        stage[pl.ds(pair * 16, 8), :] = even
        stage[pl.ds(pair * 16 + 8, 8), :] = odd
    return [stage[pl.ds(t, C, stride=8), :] for t in range(8)]


def going_down(first, second):
    return halves(second, swap_halves(first)).astype(BF16)


def going_up(last, second):
    return halves(swap_halves(last), second).astype(BF16)


def is_even(axis):
    return lax.axis_index(axis) % 2 == 0


def pack_body(v, g, vx, gx, even, odd, down, up, vbuf, gbuf, stage, sems):
    copies = []
    for x in (0, 7, 1, 6, 2, 3, 4, 5):
        pair = (
            pltpu.make_async_copy(v.at[x], vbuf.at[x], sems.at[0, x]),
            pltpu.make_async_copy(g.at[x], gbuf.at[x], sems.at[1, x]),
        )
        for copy in pair:
            copy.start()
        copies.append((x, pair))
    first, last = {}, {}
    for x, pair in copies:
        pair[0].wait()
        tiles = to_channels(vbuf[x], stage.at[x])
        for t in range(8):
            vx[x, :, tile(t)] = tiles[t].astype(BF16)
        down[x] = going_down(tiles[0], tiles[1])
        up[x] = going_up(tiles[7], tiles[6])
        pair[1].wait()
        tiles = to_channels(gbuf[x], stage.at[8 + x])
        for t in range(8):
            gx[x, :, tile(t)] = tiles[t].astype(BF16)
        first[x], last[x] = tiles[0], tiles[7]
    for x in range(4):
        down[8 + x] = going_down(first[x], first[x + 4])
        up[8 + x] = going_up(last[x], last[x + 4])
    low_out, high_out = is_even("gx"), jnp.logical_not(is_even("gx"))
    for when, low, high in ((low_out, odd, even), (high_out, even, odd)):

        @pl.when(when)
        def _(low=low, high=high):
            low[0:2] = vx[0:2]
            low[2] = gx[0]
            high[0:2] = vx[6:8]
            high[2] = gx[7]


def pack(volume, cotangent):
    field, face, edge = like(BF16, 8, C, ROW), like(BF16, 3, C, ROW), like(BF16, 12, C, T)
    scratch = [pltpu.VMEM((8, 16, C * Z), BF16)] * 2 + [pltpu.VMEM((16, 8 * C, T), F32), pltpu.SemaphoreType.DMA((2, 8))]
    out = (field, field, face, face, edge, edge)
    return call(pack_body, out, scratch, 2_000_000, volume, cotangent, in_specs=[ANY] * 2)


def sort(axis, even, odd, low, high):
    @pl.when(is_even(axis))
    def _():
        low[...] = odd[...]
        high[...] = even[...]

    @pl.when(jnp.logical_not(is_even(axis)))
    def _():
        low[...] = even[...]
        high[...] = odd[...]


def edges_body(down, up, xeven, xodd, even, odd, xlow, xhigh):
    sort("gx", xeven, xodd, xlow, xhigh)
    for when, to_low, to_high in ((is_even("gy"), odd, even), (jnp.logical_not(is_even("gy")), even, odd)):

        @pl.when(when)
        def _(to_low=to_low, to_high=to_high):
            to_low[2:10] = down[:8]
            to_low[12:16] = down[8:]
            to_high[2:10] = up[:8]
            to_high[12:16] = up[8:]
            for row, face, at in ((0, xlow, 0), (1, xlow, 1), (10, xhigh, 0), (11, xhigh, 1)):
                to_low[row] = going_down(face[at, :, tile(0)].astype(F32), face[at, :, tile(1)].astype(F32))
                to_high[row] = going_up(face[at, :, tile(7)].astype(F32), face[at, :, tile(6)].astype(F32))
            to_low[16] = going_down(xlow[2, :, tile(0)].astype(F32), xhigh[2, :, tile(0)].astype(F32))
            to_high[16] = going_up(xlow[2, :, tile(7)].astype(F32), xhigh[2, :, tile(7)].astype(F32))


def edges(down, up, xeven, xodd):
    edge, face = like(BF16, 17, C, T), like(BF16, 3, C, ROW)
    return call(edges_body, (edge, edge, face, face), [], 100_000, down, up, xeven, xodd)


def activation(pre, grad_out):
    sig = 1.0 / (1.0 + jnp.exp(-pre))
    return grad_out.astype(F32) * sig * (1.0 + pre * (1.0 - sig))


def below_tile(own_last, nearest):
    return halves(nearest.astype(F32), swap_halves(own_last.astype(F32))).astype(BF16)


def above_tile(own_first, nearest):
    return halves(swap_halves(own_first.astype(F32)), nearest.astype(F32)).astype(BF16)


def stack(out, i, field, below, above):
    row = i * 3 * C
    out[row : row + C, :T] = below
    out[row : row + C, T:ROW] = field[:, : 7 * T]
    out[row + C : row + 2 * C, :ROW] = field
    out[row + 2 * C : row + 3 * C, : 7 * T] = field[:, T:]
    out[row + 2 * C : row + 3 * C, 7 * T : ROW] = above


def step_z(part):
    return from_below(part[:64]) + part[64:128] + from_above(part[128:])


def volume_at(x, vx, xlow, xhigh, ylow, yhigh):
    field = xlow[x + 2] if x < 0 else xhigh[x - 8] if x > 7 else vx[x]
    return field, ylow[x + 2], yhigh[x + 2]


def front_body(vx, gx, xlow, xhigh, yeven, yodd, wf, bias, gp, wire, ylow, yhigh, cols, gps):
    sort("gy", yeven, yodd, ylow, yhigh)
    for x in range(-1, 9):
        field, low, high = volume_at(x, vx, xlow, xhigh, ylow, yhigh)
        stack(cols, x + 1, field, below_tile(field[:, tile(7)], low), above_tile(field[:, tile(0)], high))
    offset = jnp.concatenate([bias[...]] * 2, axis=0)
    total = jnp.zeros((64, T), F32)
    for q in range(4):
        both = jnp.dot(wf[...], cols[q * 192 : q * 192 + 384, :], preferred_element_type=F32)
        for t in range(8):
            grad_out = gx[2 * q : 2 * q + 2, :, tile(t)].reshape(64, T)
            grad = activation(step_z(both[:, tile(t)]) + offset, grad_out).astype(BF16)
            gp[q * 64 : q * 64 + 64, tile(t)] = grad
            grad = grad.astype(F32)
            total = total + grad
            gps[q * 192 : q * 192 + 64, tile(t)] = from_above(grad).astype(BF16)
            gps[q * 192 + 64 : q * 192 + 128, tile(t)] = grad.astype(BF16)
            gps[q * 192 + 128 : q * 192 + 192, tile(t)] = from_below(grad).astype(BF16)
    prod = jnp.zeros((384, 192), F32)
    for q in range(4):
        prod = prod + lax.dot_general(
            cols[q * 192 : q * 192 + 384, :],
            gps[q * 192 : q * 192 + 192, :],
            (((1,), (1,)), ((), ())),
            preferred_element_type=F32,
        )
    group = lane((8, T)) // C
    rows = []
    for row in range(0, 288, 8):
        a, b = prod[row : row + 8], prod[row + 96 : row + 104]
        a = jnp.concatenate([a[:, T:], jnp.zeros((8, 64), F32)], axis=1), a[:, :T]
        b = jnp.concatenate([b[:, T:], jnp.zeros((8, 64), F32)], axis=1), b[:, :T]
        near = a[1] + pltpu.roll(b[1], T - C, 1)
        far = a[0] + pltpu.roll(b[0], T - C, 1)
        rows.append((near, pltpu.roll(near, T - C, 1), pltpu.roll(far, 2 * C, 1), far))
    for i in range(27):
        near, moved, far, _ = rows[i]
        dz, at = divmod(i, 9)
        near2, moved2, far2, plain2 = rows[27 + at]
        last = pltpu.roll((near2, near2, plain2)[dz], (3 * C, C, 3 * C)[dz], 1)
        out = jnp.where(group == 0, near, jnp.where(group == 1, moved, jnp.where(group == 2, far, last)))
        wire[8 * i : 8 * i + 8] = out
    total = jnp.concatenate([total[:C] + total[C:], jnp.zeros((T - C, T), F32)], axis=0)
    total = jnp.sum(total.T, axis=0, keepdims=True)
    wire[216:] = jnp.broadcast_to(total, (8, T))


def front(vx, gx, xlow, xhigh, yeven, yodd, wf, bias):
    edge = like(BF16, 17, C, T)
    out = (like(BF16, 256, ROW), like(F32, 224, T), edge, edge)
    scratch = [pltpu.VMEM((960, ROW), BF16), pltpu.VMEM((768, ROW), BF16)]
    return call(front_body, out, scratch, 2_500_000_000, vx, gx, xlow, xhigh, yeven, yodd, wf, bias)


def ring_body(vx, xlow, xhigh, ylow, yhigh, wf, bias, faces, border, side, ring):
    for x in range(-2, 10):
        field, low, high = volume_at(x, vx, xlow, xhigh, ylow, yhigh)
        lo, hi = low.astype(F32), high.astype(F32)
        first, last = field[:, tile(0)].astype(F32), field[:, tile(7)].astype(F32)
        near = halves(lo, hi).astype(BF16)
        before = halves(swap_halves(lo), last).astype(BF16)
        after = halves(first, swap_halves(hi)).astype(BF16)
        if x <= 1 or x >= 6:
            i = x + 2 if x <= 1 else x - 2
            stack(side, i, field, below_tile(field[:, tile(7)], low), above_tile(field[:, tile(0)], high))
            for dy, part in enumerate((before, near, after)):
                side[i * 96 + dy * C : i * 96 + dy * C + C, ROW:] = part
        if -1 <= x <= 8:
            for dy, part in enumerate((before, near, after)):
                ring[(x + 1) * 96 + dy * C : (x + 1) * 96 + dy * C + C, :] = part
    offset = jnp.concatenate([bias[...]] * 2, axis=0)
    for face in range(2):
        both = jnp.dot(wf[...], side[face * 384 : face * 384 + 384, :], preferred_element_type=F32)
        mine = slice(face * C, face * C + C)
        far = (xlow, xhigh)[face]
        lo, hi = ylow[16].astype(F32), yhigh[16].astype(F32)
        corner = halves(swap_halves(lo), swap_halves(hi)) if face else halves(lo, hi)
        for t in range(9):
            pre = (step_z(both[:, tile(t)]) + offset)[mine]
            if t < 8:
                faces[face, :, tile(t)] = activation(pre, far[2, :, tile(t)]).astype(BF16)
            else:
                border[9 * face] = activation(pre, corner).astype(BF16)
    for q in range(4):
        part = jnp.dot(wf[...], ring[q * 192 : q * 192 + 384, :], preferred_element_type=F32)
        pre = step_z(part) + offset
        for side_x in range(2):
            x = 2 * q + side_x
            lo, hi = ylow[12 + x % 4].astype(F32), yhigh[12 + x % 4].astype(F32)
            grad_out = halves(lo, hi) if x < 4 else halves(swap_halves(lo), swap_halves(hi))
            border[x + 1] = activation(pre[side_x * C : side_x * C + C], grad_out).astype(BF16)


def ring(vx, xlow, xhigh, ylow, yhigh, wf, bias):
    scratch = [pltpu.VMEM((768, 9 * T), BF16), pltpu.VMEM((960, T), BF16)]
    out = (like(BF16, 2, C, ROW), like(BF16, 10, C, T))
    return call(ring_body, out, scratch, 800_000_000, vx, xlow, xhigh, ylow, yhigh, wf, bias)


def data_body(q, gp, faces, border, wd, *refs):
    data, cols, stage, block, sem = refs[-5:]
    for i in range(4):
        x = 2 * q + i - 1
        field = faces[0] if x < 0 else faces[1] if x > 7 else gp[x * C : x * C + C, :]
        near = border[x + 1]
        stack(cols, i, field, below_tile(field[:, tile(7)], near), above_tile(field[:, tile(0)], near))
    both = jnp.dot(wd[...], cols[...], preferred_element_type=F32)
    for t in range(8):
        out = step_z(both[:, tile(t)])
        for x in range(2):
            stage[x, pl.ds(t, C, stride=8), :] = out[x * C : x * C + C]
    for x in range(2):
        for pair in range(C // 2):
            low, high = exchange_halves(stage[x, pl.ds(pair * 16, 8), :], stage[x, pl.ds(pair * 16 + 8, 8), :])
            block[x, :, tile(pair)] = jnp.concatenate([low, high], axis=0).astype(BF16)
    copy = pltpu.make_async_copy(block, data.at[pl.ds(2 * q, 2)], sem)
    copy.start()
    copy.wait()


def data_piece(q, gp, faces, border, wd, before):
    scratch = [
        pltpu.VMEM((384, ROW), BF16),
        pltpu.VMEM((2, 8 * C, T), F32),
        pltpu.VMEM((2, 16, C * Z), BF16),
        pltpu.SemaphoreType.DMA,
    ]
    out = like(BF16, 8, 16, C * Z)
    args, specs, aliases = (gp, faces, border, wd), [VMEM] * 4, None
    if before is not None:
        args, specs, aliases = (*args, before), [*specs, ANY], {4: 0}
    return call(
        lambda *refs: data_body(q, *refs), out, scratch, 200_000_000, *args, in_specs=specs, out_specs=ANY, aliases=aliases
    )


def finish_body(scale, wire, filters, biases):
    for row in range(0, 288, 8):
        for dz in range(3):
            at, group = (row, dz) if row < 216 else (row - 216 + 72 * dz, 3)
            part = wire[at : at + 8]
            moved = part if group == 0 else pltpu.roll(part, T - group * C, 1)
            block, inside = divmod(row, C)
            filters[block * 3 + dz, inside : inside + 8, :] = moved[:, :C] * scale
    biases[...] = wire[216:217, :C] * scale


def finish(wire, scale):
    out = (like(F32, 27, C, C), like(F32, 1, C))
    return call(lambda *refs: finish_body(scale, *refs), out, [], 100_000, wire)


def swap(array, axis, size, odd):
    pairs = []
    for low in range(odd, size - 1, 2):
        pairs += [(low, low + 1), (low + 1, low)]
    return lax.ppermute(array, axis, pairs)


def band(strip):
    pad = [jnp.pad(strip, ((0, 0), (0, 0), (96 * x, 96 - 96 * x))) for x in range(2)]
    return jnp.stack(pad, axis=1).reshape(192, 384)


def shards(volume, cotangent, weight, bias):
    nx, ny = lax.axis_size("gx"), lax.axis_size("gy")
    wf = band(jnp.transpose(weight, (2, 4, 0, 1, 3)).reshape(3, C, 288))
    wd = band(jnp.transpose(weight[::-1, ::-1, ::-1], (2, 3, 0, 1, 4)).reshape(3, C, 288))
    offset = jnp.broadcast_to(bias[:, None], (C, T))
    vx, gx, xeven, xodd, down, up = pack(volume, cotangent)
    xodd = swap(xodd, "gx", nx, 1)
    xeven = swap(xeven, "gx", nx, 0)
    yeven, yodd, xlow, xhigh = edges(down, up, xeven, xodd)
    yodd = swap(yodd, "gy", ny, 1)
    yeven = swap(yeven, "gy", ny, 0)
    gp, wire, ylow, yhigh = front(vx, gx, xlow, xhigh, yeven, yodd, wf, offset)

    state = {}

    def border_piece(vx):
        state["ring"] = ring(vx, xlow, xhigh, ylow, yhigh, wf, offset)
        return state["ring"][0]

    def piece(q):
        def run(gp):
            state["data"] = data_piece(q, gp, *state["ring"], wd, state.get("data"))
            return state["data"]

        return run

    pieces = [(border_piece, vx, "ring")] + [(piece(q), gp, "data") for q in range(4)]
    steps = [(axis, size, 1 << b) for axis, size in (("gx", nx), ("gy", ny)) for b in range(size.bit_length() - 1)]
    for axis, size, step in steps:
        sent = wire.astype(BF16)
        work = pieces.pop(0) if pieces else None
        if work:
            sent, operand = lax.optimization_barrier((sent, work[1]))
        got = lax.ppermute(sent, axis, [(i, i ^ step) for i in range(size)])
        if work:
            work[0](operand)
            got, state[work[2]] = lax.optimization_barrier((got, state[work[2]]))
        wire = sent.astype(F32) + got.astype(F32)
    for work in pieces:
        work[0](work[1])
    scale = 1.0 / math.sqrt(8 * nx * 16 * ny * Z)
    filters, biases = finish(wire, scale)
    return state["data"], filters.reshape(3, 3, 3, C, C), biases.reshape(C)


def solution(mesh):
    in_specs = (P("gx", "gy", None), P("gx", "gy", None), P(), P())
    out_specs = (P("gx", "gy", None), P(), P())
    return jax.shard_map(shards, mesh=mesh, in_specs=in_specs, out_specs=out_specs, check_vma=False)
```

profile of v0, /device:TPU:0, one launch (start us, length us, event | category | flops | bytes accessed | tf_op | source)
XLA Modules:
  0.0 47.8 jit_solution(3440722374383930260)
XLA Ops:
  0.6 0.0 copy-start
  0.6 1.0 %copy-done = bf16[8,16,2048]{2,1,0:T(8,128)(2,1)S(1)} copy-done((bf16[8,16,2048]{2,1,0:T(8,128)(2,1)S(1)}, bf16[8,16,2048]{2,1,0:T(8,128)(2,1)}, u32[]{:S(2)}) %copy-start) | copy-done | bytes 524312
  1.7 0.0 copy-start.1
  1.7 1.0 %copy-done.1 = bf16[8,16,2048]{2,1,0:T(8,128)(2,1)S(1)} copy-done((bf16[8,16,2048]{2,1,0:T(8,128)(2,1)S(1)}, bf16[8,16,2048]{2,1,0:T(8,128)(2,1)}, u32[]{:S(2)}) %copy-start.1) | copy-done | bytes 524312
  2.7 0.0 copy-start.2
  2.7 3.8 %shard_map.67 = (bf16[8,32,1024]{2,1,0:T(8,128)(2,1)S(1)}, bf16[8,32,1024]{2,1,0:T(8,128)(2,1)S(1)}, bf16[3,32,1024]{2,1,0:T(8,128)(2,1)S(1)}, bf16[3,32,1024]{2...) custom-call(bf16[8,16,2048]{2,1,0:T(8,128)(2,1)S(1)} %copy-done, ...), custom_call_target="tpu_custom_call" | custom-call | flops 2000000 | bytes 2686976 | tf_op jit(solution)/shard_map/pallas_call | solution.py:23
  6.5 0.5 %collective-permute-start = (bf16[3,32,1024]{2,1,0:T(8,128)(2,1)S(1)}, bf16[3,32,1024]{2,1,0:T(8,128)(2,1)S(1)}, u32[]{:S(2)}, u32[]{:S(2)}) collective-permute-start(bf16[3,32,1024]{2,1,0:T(8,128)(2,1)S(1)} %get-tuple-element.46), channel_id=1, source_target_pairs={{0,8},{8,0},{16,24},{24,16},{1,9},{9,1},{17,25},{25,17},{2,10},{10... | collective-permute-start | bytes 589832 | tf_op jit(solution)/shard_map/ppermute | solution.py:354
  7.0 0.7 %collective-permute-start.1 = (bf16[3,32,1024]{2,1,0:T(8,128)(2,1)S(1)}, bf16[3,32,1024]{2,1,0:T(8,128)(2,1)S(1)}, u32[]{:S(2)}, u32[]{:S(2)}) collective-permute-start(bf16[3,32,1024]{2,1,0:T(8,128)(2,1)S(1)} %get-tuple-element.47), channel_id=1, source_target_pairs={{8,16},{16,8},{9,17},{17,9},{10,18},{18,10},{11,19},{19,11},{12,20... | collective-permute-start | bytes 589832 | tf_op jit(solution)/shard_map/ppermute | solution.py:354
  7.7 0.0 copy-done.2
  7.7 0.2 copy.12
  7.9 0.2 reshape.25
  8.1 0.1 pad_bitcast_fusion.3
  8.2 0.0 collective-permute-done.xeven
  8.2 0.0 collective-permute-done.1.xodd
  8.2 0.1 shard_map.68
  8.4 2.8 %collective-permute-start.2 = (bf16[17,32,128]{2,1,0:T(8,128)(2,1)S(1)}, bf16[17,32,128]{2,1,0:T(8,128)(2,1)S(1)}, u32[]{:S(2)}, u32[]{:S(2)}) collective-permute-start(bf16[17,32,128]{2,1,0:T(8,128)(2,1)S(1)} %get-tuple-element.50), channel_id=1, source_target_pairs={{0,1},{1,0},{2,3},{3,2},{4,5},{5,4},{6,7},{7,6},{8,9},{9,8},{10,11... | collective-permute-start | bytes 417800 | tf_op jit(solution)/shard_map/ppermute | solution.py:354
  11.1 0.7 %collective-permute-start.3 = (bf16[17,32,128]{2,1,0:T(8,128)(2,1)S(1)}, bf16[17,32,128]{2,1,0:T(8,128)(2,1)S(1)}, u32[]{:S(2)}, u32[]{:S(2)}) collective-permute-start(bf16[17,32,128]{2,1,0:T(8,128)(2,1)S(1)} %get-tuple-element.51), channel_id=1, source_target_pairs={{1,2},{2,1},{3,4},{4,3},{5,6},{6,5},{9,10},{10,9},{11,12},{12,11},... | collective-permute-start | bytes 417800 | tf_op jit(solution)/shard_map/ppermute | solution.py:354
  11.8 0.2 copy.14
  12.0 0.2 reshape.27
  12.2 0.1 pad_bitcast_fusion.1
  12.3 1.9 %collective-permute-done.2.yeven = bf16[17,32,128]{2,1,0:T(8,128)(2,1)S(1)} collective-permute-done((bf16[17,32,128]{2,1,0:T(8,128)(2,1)S(1)}, bf16[17,32,128]{2,1,0:T(8,128)(2,1)S(1)}, u32[]{:S(2)}, u32[]{:S(2)}) %collective-permute-start.2) | collective-permute-done | bytes 139296 | tf_op jit(solution)/shard_map/ppermute | solution.py:354
  14.2 0.0 collective-permute-done.3.yodd
  14.2 0.0 copy-start.3
  14.2 0.7 %copy-done.3 = f32[32]{0:T(128)S(1)} copy-done((f32[32]{0:T(128)S(1)}, f32[32]{0:T(128)}, u32[]{:S(2)}) %copy-start.3) | copy-done | bytes 152
  14.8 0.1 broadcast_in_dim.2.bias
  14.9 2.9 %shard_map.69 = (bf16[256,1024]{1,0:T(8,128)(2,1)S(1)}, f32[224,128]{1,0:T(8,128)S(1)}, bf16[17,32,128]{2,1,0:T(8,128)(2,1)S(1)}, bf16[17,32,128]{2,1,0:T(8,128)(2,1)S(1)}) custom-call(bf16[8,32,1024]{2,1,0:T(8,128)(2,1)S(1)} %get-tuple-element.54.vx, bf16[8,32,1024]{2,1,0:T(8,128)(2,1)S(1)} %get-tuple-element.43.gx, ...), custom_call_target="tpu_custom_call" | custom-call | flops 2500000000 | bytes 2801664 | tf_op jit(solution)/shard_map/pallas_call | solution.py:23
  17.8 5.2 %collective-permute-start.4 = (bf16[224,128]{1,0:T(8,128)(2,1)S(1)}, bf16[224,128]{1,0:T(8,128)(2,1)S(1)}, u32[]{:S(2)}, u32[]{:S(2)}) collective-permute-start(bf16[224,128]{1,0:T(8,128)(2,1)S(1)} %convert_element_type.51), channel_id=1, source_target_pairs={{0,8},{8,0},{16,24},{24,16},{1,9},{9,1},{17,25},{25,17},{2,10},{10... | collective-permute-start | bytes 172040 | tf_op jit(solution)/shard_map/ppermute | solution.py:395
  23.0 1.0 %shard_map.70 = (bf16[2,32,1024]{2,1,0:T(8,128)(2,1)S(1)}, bf16[10,32,128]{2,1,0:T(8,128)(2,1)S(1)}) custom-call(bf16[8,32,1024]{2,1,0:T(8,128)(2,1)S(1)} %get-tuple-element.54.vx, bf16[3,32,1024]{2,1,0:T(8,128)(2,1)S(1)} %get-tuple-element.48.xlow, bf16[3,32,1024]{2,1,0:T(8,128)(2,1)S(1)} %get-tuple-element.49.xhigh, ...), custom_call_target="tpu_custom_call" | custom-call | flops 800000000 | bytes 1572864 | tf_op jit(solution)/shard_map/pallas_call | solution.py:23
  24.1 0.0 collective-permute-done.4
  24.1 2.7 %collective-permute-start.5 = (bf16[224,128]{1,0:T(8,128)(2,1)S(1)}, bf16[224,128]{1,0:T(8,128)(2,1)S(1)}, u32[]{:S(2)}, u32[]{:S(2)}) collective-permute-start(bf16[224,128]{1,0:T(8,128)(2,1)S(1)} %add_convert_fusion.3), channel_id=1, source_target_pairs={{0,16},{8,24},{16,0},{24,8},{1,17},{9,25},{17,1},{25,9},{2,18},{10... | collective-permute-start | bytes 172040 | tf_op jit(solution)/shard_map/ppermute | solution.py:395
  26.9 1.3 %shard_map.71.refs_4_ = bf16[8,16,2048]{2,1,0:T(8,128)(2,1)} custom-call(bf16[256,1024]{1,0:T(8,128)(2,1)S(1)} %get-tuple-element.75.refs_0_, bf16[2,32,1024]{2,1,0:T(8,128)(2,1)S(1)} %get-tuple-element.63.refs_1_, bf16[10,32,128]{2,1,0:T(8,128)(2,1)S(1)} %get-tuple-element.64.refs_2_, bf16[192,384]{1,0:T(8,128)(2,1)S(1)} %bitcast.15), custom_call_target="tpu_custom_call" | custom-call | flops 200000000 | bytes 1409024 | tf_op jit(solution)/shard_map/pallas_call | solution.py:23
  28.2 1.1 %collective-permute-done.5 = bf16[224,128]{1,0:T(8,128)(2,1)S(1)} collective-permute-done((bf16[224,128]{1,0:T(8,128)(2,1)S(1)}, bf16[224,128]{1,0:T(8,128)(2,1)S(1)}, u32[]{:S(2)}, u32[]{:S(2)}) %collective-permute-start.5) | collective-permute-done | bytes 57376 | tf_op jit(solution)/shard_map/ppermute | solution.py:395
  29.2 4.9 %collective-permute-start.6 = (bf16[224,128]{1,0:T(8,128)(2,1)S(1)}, bf16[224,128]{1,0:T(8,128)(2,1)S(1)}, u32[]{:S(2)}, u32[]{:S(2)}) collective-permute-start(bf16[224,128]{1,0:T(8,128)(2,1)S(1)} %add_convert_fusion.2), channel_id=1, source_target_pairs={{0,1},{1,0},{2,3},{3,2},{4,5},{5,4},{6,7},{7,6},{8,9},{9,8},{10,11... | collective-permute-start | bytes 172040 | tf_op jit(solution)/shard_map/ppermute | solution.py:395
  34.1 1.3 %shard_map.72.refs_4_ = bf16[8,16,2048]{2,1,0:T(8,128)(2,1)} custom-call(bf16[256,1024]{1,0:T(8,128)(2,1)S(1)} %get-tuple-element.75.refs_0_, bf16[2,32,1024]{2,1,0:T(8,128)(2,1)S(1)} %get-tuple-element.63.refs_1_, bf16[10,32,128]{2,1,0:T(8,128)(2,1)S(1)} %get-tuple-element.64.refs_2_, ...), custom_call_target="tpu_custom_call", output_to_operand_aliasing={{}: (4, {})} | custom-call | flops 200000000 | bytes 1933312 | tf_op jit(solution)/shard_map/pallas_call | solution.py:23
  35.4 0.9 %collective-permute-done.6 = bf16[224,128]{1,0:T(8,128)(2,1)S(1)} collective-permute-done((bf16[224,128]{1,0:T(8,128)(2,1)S(1)}, bf16[224,128]{1,0:T(8,128)(2,1)S(1)}, u32[]{:S(2)}, u32[]{:S(2)}) %collective-permute-start.6) | collective-permute-done | bytes 57376 | tf_op jit(solution)/shard_map/ppermute | solution.py:395
  36.3 3.1 %collective-permute-start.7 = (bf16[224,128]{1,0:T(8,128)(2,1)S(1)}, bf16[224,128]{1,0:T(8,128)(2,1)S(1)}, u32[]{:S(2)}, u32[]{:S(2)}) collective-permute-start(bf16[224,128]{1,0:T(8,128)(2,1)S(1)} %add_convert_fusion.1), channel_id=1, source_target_pairs={{0,2},{1,3},{2,0},{3,1},{4,6},{5,7},{6,4},{7,5},{8,10},{9,11},{10,... | collective-permute-start | bytes 172040 | tf_op jit(solution)/shard_map/ppermute | solution.py:395
  39.4 1.3 %shard_map.73.refs_4_ = bf16[8,16,2048]{2,1,0:T(8,128)(2,1)} custom-call(bf16[256,1024]{1,0:T(8,128)(2,1)S(1)} %get-tuple-element.75.refs_0_, bf16[2,32,1024]{2,1,0:T(8,128)(2,1)S(1)} %get-tuple-element.63.refs_1_, bf16[10,32,128]{2,1,0:T(8,128)(2,1)S(1)} %get-tuple-element.64.refs_2_, ...), custom_call_target="tpu_custom_call", output_to_operand_aliasing={{}: (4, {})} | custom-call | flops 200000000 | bytes 1933312 | tf_op jit(solution)/shard_map/pallas_call | solution.py:23
  40.7 0.9 %collective-permute-done.7 = bf16[224,128]{1,0:T(8,128)(2,1)S(1)} collective-permute-done((bf16[224,128]{1,0:T(8,128)(2,1)S(1)}, bf16[224,128]{1,0:T(8,128)(2,1)S(1)}, u32[]{:S(2)}, u32[]{:S(2)}) %collective-permute-start.7) | collective-permute-done | bytes 57376 | tf_op jit(solution)/shard_map/ppermute | solution.py:395
  41.6 3.1 %collective-permute-start.8 = (bf16[224,128]{1,0:T(8,128)(2,1)S(1)}, bf16[224,128]{1,0:T(8,128)(2,1)S(1)}, u32[]{:S(2)}, u32[]{:S(2)}) collective-permute-start(bf16[224,128]{1,0:T(8,128)(2,1)S(1)} %add_convert_fusion), channel_id=1, source_target_pairs={{0,4},{1,5},{2,6},{3,7},{4,0},{5,1},{6,2},{7,3},{8,12},{9,13},{10,... | collective-permute-start | bytes 172040 | tf_op jit(solution)/shard_map/ppermute | solution.py:395
  44.7 1.3 %shard_map.74 = bf16[8,16,2048]{2,1,0:T(8,128)(2,1)} custom-call(bf16[256,1024]{1,0:T(8,128)(2,1)S(1)} %get-tuple-element.75.refs_0_, bf16[2,32,1024]{2,1,0:T(8,128)(2,1)S(1)} %get-tuple-element.63.refs_1_, bf16[10,32,128]{2,1,0:T(8,128)(2,1)S(1)} %get-tuple-element.64.refs_2_, bf16[192,384]{1,0:T(8,128)(2,1)S(1)} %bitcast.18, ...), custom_call_target="tpu_custom_call", output_to_operand_aliasing={{}: (4, {})} | custom-call | flops 200000000 | bytes 1933312 | tf_op jit(solution)/shard_map/pallas_call | solution.py:23
  46.0 0.9 %collective-permute-done.8 = bf16[224,128]{1,0:T(8,128)(2,1)S(1)} collective-permute-done((bf16[224,128]{1,0:T(8,128)(2,1)S(1)}, bf16[224,128]{1,0:T(8,128)(2,1)S(1)}, u32[]{:S(2)}, u32[]{:S(2)}) %collective-permute-start.8) | collective-permute-done | bytes 57376 | tf_op jit(solution)/shard_map/ppermute | solution.py:395
  46.9 0.9 %shard_map.75 = (f32[27,32,32]{2,1,0:T(8,128)}, f32[1,32]{1,0:T(1,128)}) custom-call(f32[224,128]{1,0:T(8,128)S(1)} %convert_add_fusion.refs_0_), custom_call_target="tpu_custom_call" | custom-call | flops 100000 | bytes 225408 | tf_op jit(solution)/shard_map/pallas_call | solution.py:23
  (11 shorter events, 0.2 us)
Async XLA Ops:
  0.6 1.0 %copy-start = (bf16[8,16,2048]{2,1,0:T(8,128)(2,1)S(1)}, bf16[8,16,2048]{2,1,0:T(8,128)(2,1)}, u32[]{:S(2)}) copy-start(bf16[8,16,2048]{2,1,0:T(8,128)(2,1)} %v.1) | copy-start | bytes 1572868
  1.7 1.0 %copy-start.1 = (bf16[8,16,2048]{2,1,0:T(8,128)(2,1)S(1)}, bf16[8,16,2048]{2,1,0:T(8,128)(2,1)}, u32[]{:S(2)}) copy-start(bf16[8,16,2048]{2,1,0:T(8,128)(2,1)} %g.1) | copy-start | bytes 1572868
  2.7 5.0 %copy-start.2 = (bf16[3,3,3,32,32]{4,3,2,1,0:T(8,128)(2,1)S(1)}, bf16[3,3,3,32,32]{4,3,2,1,0:T(8,128)(2,1)}, u32[]{:S(2)}) copy-start(bf16[3,3,3,32,32]{4,3,2,1,0:T(8,128)(2,1)} %param.6) | copy-start | bytes 165892
  6.5 1.7 %collective-permute-start = (bf16[3,32,1024]{2,1,0:T(8,128)(2,1)S(1)}, bf16[3,32,1024]{2,1,0:T(8,128)(2,1)S(1)}, u32[]{:S(2)}, u32[]{:S(2)}) collective-permute-start(bf16[3,32,1024]{2,1,0:T(8,128)(2,1)S(1)} %get-tuple-element.46), channel_id=1, source_target_pairs={{0,8},{8,0},{16,24},{24,16},{1,9},{9,1},{17,25},{25,17},{2,10},{10... | collective-permute-start | bytes 589832 | tf_op jit(solution)/shard_map/ppermute | solution.py:354
  7.0 1.2 %collective-permute-start.1 = (bf16[3,32,1024]{2,1,0:T(8,128)(2,1)S(1)}, bf16[3,32,1024]{2,1,0:T(8,128)(2,1)S(1)}, u32[]{:S(2)}, u32[]{:S(2)}) collective-permute-start(bf16[3,32,1024]{2,1,0:T(8,128)(2,1)S(1)} %get-tuple-element.47), channel_id=1, source_target_pairs={{8,16},{16,8},{9,17},{17,9},{10,18},{18,10},{11,19},{19,11},{12,20... | collective-permute-start | bytes 589832 | tf_op jit(solution)/shard_map/ppermute | solution.py:354
  8.4 5.8 %collective-permute-start.2 = (bf16[17,32,128]{2,1,0:T(8,128)(2,1)S(1)}, bf16[17,32,128]{2,1,0:T(8,128)(2,1)S(1)}, u32[]{:S(2)}, u32[]{:S(2)}) collective-permute-start(bf16[17,32,128]{2,1,0:T(8,128)(2,1)S(1)} %get-tuple-element.50), channel_id=1, source_target_pairs={{0,1},{1,0},{2,3},{3,2},{4,5},{5,4},{6,7},{7,6},{8,9},{9,8},{10,11... | collective-permute-start | bytes 417800 | tf_op jit(solution)/shard_map/ppermute | solution.py:354
  11.1 3.0 %collective-permute-start.3 = (bf16[17,32,128]{2,1,0:T(8,128)(2,1)S(1)}, bf16[17,32,128]{2,1,0:T(8,128)(2,1)S(1)}, u32[]{:S(2)}, u32[]{:S(2)}) collective-permute-start(bf16[17,32,128]{2,1,0:T(8,128)(2,1)S(1)} %get-tuple-element.51), channel_id=1, source_target_pairs={{1,2},{2,1},{3,4},{4,3},{5,6},{6,5},{9,10},{10,9},{11,12},{12,11},... | collective-permute-start | bytes 417800 | tf_op jit(solution)/shard_map/ppermute | solution.py:354
  14.2 0.7 %copy-start.3 = (f32[32]{0:T(128)S(1)}, f32[32]{0:T(128)}, u32[]{:S(2)}) copy-start(f32[32]{0:T(128)} %param.7) | copy-start | bytes 388
  17.8 6.3 %collective-permute-start.4 = (bf16[224,128]{1,0:T(8,128)(2,1)S(1)}, bf16[224,128]{1,0:T(8,128)(2,1)S(1)}, u32[]{:S(2)}, u32[]{:S(2)}) collective-permute-start(bf16[224,128]{1,0:T(8,128)(2,1)S(1)} %convert_element_type.51), channel_id=1, source_target_pairs={{0,8},{8,0},{16,24},{24,16},{1,9},{9,1},{17,25},{25,17},{2,10},{10... | collective-permute-start | bytes 172040 | tf_op jit(solution)/shard_map/ppermute | solution.py:395
  24.1 5.1 %collective-permute-start.5 = (bf16[224,128]{1,0:T(8,128)(2,1)S(1)}, bf16[224,128]{1,0:T(8,128)(2,1)S(1)}, u32[]{:S(2)}, u32[]{:S(2)}) collective-permute-start(bf16[224,128]{1,0:T(8,128)(2,1)S(1)} %add_convert_fusion.3), channel_id=1, source_target_pairs={{0,16},{8,24},{16,0},{24,8},{1,17},{9,25},{17,1},{25,9},{2,18},{10... | collective-permute-start | bytes 172040 | tf_op jit(solution)/shard_map/ppermute | solution.py:395
  29.2 7.0 %collective-permute-start.6 = (bf16[224,128]{1,0:T(8,128)(2,1)S(1)}, bf16[224,128]{1,0:T(8,128)(2,1)S(1)}, u32[]{:S(2)}, u32[]{:S(2)}) collective-permute-start(bf16[224,128]{1,0:T(8,128)(2,1)S(1)} %add_convert_fusion.2), channel_id=1, source_target_pairs={{0,1},{1,0},{2,3},{3,2},{4,5},{5,4},{6,7},{7,6},{8,9},{9,8},{10,11... | collective-permute-start | bytes 172040 | tf_op jit(solution)/shard_map/ppermute | solution.py:395
  36.3 5.3 %collective-permute-start.7 = (bf16[224,128]{1,0:T(8,128)(2,1)S(1)}, bf16[224,128]{1,0:T(8,128)(2,1)S(1)}, u32[]{:S(2)}, u32[]{:S(2)}) collective-permute-start(bf16[224,128]{1,0:T(8,128)(2,1)S(1)} %add_convert_fusion.1), channel_id=1, source_target_pairs={{0,2},{1,3},{2,0},{3,1},{4,6},{5,7},{6,4},{7,5},{8,10},{9,11},{10,... | collective-permute-start | bytes 172040 | tf_op jit(solution)/shard_map/ppermute | solution.py:395
  41.6 5.3 %collective-permute-start.8 = (bf16[224,128]{1,0:T(8,128)(2,1)S(1)}, bf16[224,128]{1,0:T(8,128)(2,1)S(1)}, u32[]{:S(2)}, u32[]{:S(2)}) collective-permute-start(bf16[224,128]{1,0:T(8,128)(2,1)S(1)} %add_convert_fusion), channel_id=1, source_target_pairs={{0,4},{1,5},{2,6},{3,7},{4,0},{5,1},{6,2},{7,3},{8,12},{9,13},{10,... | collective-permute-start | bytes 172040 | tf_op jit(solution)/shard_map/ppermute | solution.py:395
where the time goes:
time: 48 us; the launch traced here: 47.8 us
  starting transfers between devices  23.6 us (49%)
  Pallas kernels  13.9 us (29%)
  waiting for transfers between devices  5.53 us (12%)
  local copies, waits for them, and re-layouts  3.76 us (8%)
  between operations  0.85 us (2%)
    ppermute x5, starting transfers between devices, shards(): got = lax.ppermute(sent, axis, [(i, i ^ step) for i in range(size)])  19 us
    pallas_call x9, Pallas kernels, call(): pl.pallas_call(body, out_shape=out_shape, in_specs=in_specs or [VMEM] * l...  13.9 us
    ppermute x4, starting transfers between devices, swap(): return lax.ppermute(array, axis, pairs)  4.6 us
    ppermute x5, waiting for transfers between devices, shards(): got = lax.ppermute(sent, axis, [(i, i ^ step) for i in range(size)])  3.65 us
    unnamed x8, local copies, waits for them, and re-layouts  2.74 us
    ppermute x4, waiting for transfers between devices, swap(): return lax.ppermute(array, axis, pairs)  1.87 us
  transfers between devices with their start and end apart: 9, of which 5 were waited for; matrix products, arithmetic and copies ran while one was open for 2% of the time, Pallas kernels for 13%

commit v1 on v0

v1 whole, which is shorter than its diff:
```python
import math

import jax
import jax.numpy as jnp
from jax import lax
from jax.experimental import pallas as pl
from jax.experimental.pallas import tpu as pltpu
from jax.sharding import PartitionSpec as P

C = 32
Z = 64
T = 128
ROW = 8 * T
F32 = jnp.float32
BF16 = jnp.bfloat16
VMEM_LIMIT = 48 * 1024 * 1024
VMEM = pl.BlockSpec(memory_space=pltpu.VMEM)
HBM = pl.BlockSpec(memory_space=pltpu.HBM)


def call(body, out_shape, scratch_shapes, flops, *args, in_specs=None, out_specs=None, aliases=None):
    traffic = sum(math.prod(a.shape) * a.dtype.itemsize for a in (*args, *jax.tree.leaves(out_shape)))
    return pl.pallas_call(
        body,
        out_shape=out_shape,
        in_specs=in_specs or [VMEM] * len(args),
        out_specs=out_specs or jax.tree.map(lambda _: VMEM, out_shape),
        scratch_shapes=scratch_shapes,
        input_output_aliases=aliases or {},
        compiler_params=pltpu.CompilerParams(vmem_limit_bytes=VMEM_LIMIT),
        cost_estimate=pl.CostEstimate(flops=flops, bytes_accessed=traffic, transcendentals=0),
    )(*args)


def like(dtype, *shape):
    return jax.ShapeDtypeStruct(shape, dtype)


def lane(shape):
    return lax.broadcasted_iota(jnp.int32, shape, len(shape) - 1)


def swap_halves(a):
    return pltpu.roll(a, T // 2, a.ndim - 1)


def halves(low, high):
    return jnp.where(lane(low.shape) < T // 2, low, high)


def exchange_halves(a, b):
    mixed = swap_halves(halves(b, a))
    return halves(a, mixed), halves(mixed, b)


def from_below(a):
    return jnp.where(lane(a.shape) % Z == 0, 0.0, pltpu.roll(a, 1, a.ndim - 1))


def from_above(a):
    return jnp.where(lane(a.shape) % Z == Z - 1, 0.0, pltpu.roll(a, T - 1, a.ndim - 1))


def tile(t):
    return slice(t * T, t * T + T)


def to_channels(rows, stage):
    rows = rows.astype(F32)
    for pair in range(C // 2):
        even, odd = exchange_halves(rows[:8, tile(pair)], rows[8:, tile(pair)])
        stage[pl.ds(pair * 16, 8), :] = even
        stage[pl.ds(pair * 16 + 8, 8), :] = odd
    return [stage[pl.ds(t, C, stride=8), :] for t in range(8)]


def is_even(axis):
    return lax.axis_index(axis) % 2 == 0


def pack_body(v, g, vx, gx, even, odd, vbuf, gbuf, stage, sems):
    copies = []
    for x in (0, 7, 1, 2, 3, 4, 5, 6):
        copies.append((x, v, vbuf, vx, 0))
    for x in range(8):
        copies.append((x, g, gbuf, gx, 1))
    copies = [(x, out, buf, pltpu.make_async_copy(src.at[x], buf.at[x], sems.at[k, x])) for x, src, buf, out, k in copies]
    for *_, copy in copies:
        copy.start()
    for n, (x, out, buf, copy) in enumerate(copies):
        copy.wait()
        for t, part in enumerate(to_channels(buf[x], stage.at[n])):
            out[x, :, tile(t)] = part.astype(BF16)
    faces(vx, even, odd)


def faces(field, even, odd):
    for when, low, high in ((is_even("gx"), odd, even), (jnp.logical_not(is_even("gx")), even, odd)):

        @pl.when(when)
        def _(low=low, high=high):
            low[...] = field[0]
            high[...] = field[7]


def pack(volume, cotangent):
    field, face = like(BF16, 8, C, ROW), like(BF16, C, ROW)
    scratch = [pltpu.VMEM((8, 16, C * Z), BF16)] * 2 + [pltpu.VMEM((16, 8 * C, T), F32), pltpu.SemaphoreType.DMA((2, 8))]
    return call(pack_body, (field, field, face, face), scratch, 2_000_000, volume, cotangent, in_specs=[HBM] * 2)


def sort(axis, even, odd, low, high):
    @pl.when(is_even(axis))
    def _():
        low[...] = odd[...]
        high[...] = even[...]

    @pl.when(jnp.logical_not(is_even(axis)))
    def _():
        low[...] = even[...]
        high[...] = odd[...]


def edges_body(field, xeven, xodd, even, odd, xlow, xhigh):
    sort("gx", xeven, xodd, xlow, xhigh)

    def at(x, t):
        source = xlow if x < 0 else xhigh if x > 7 else field.at[x]
        return source[:, tile(t)].astype(F32)

    for when, to_low, to_high in ((is_even("gy"), odd, even), (jnp.logical_not(is_even("gy")), even, odd)):

        @pl.when(when)
        def _(to_low=to_low, to_high=to_high):
            for row in range(5):
                to_low[row] = halves(at(row + 4, 0), swap_halves(at(row - 1, 0))).astype(BF16)
                to_high[row] = halves(swap_halves(at(row - 1, 7)), at(row + 4, 7)).astype(BF16)


def edges(field, xeven, xodd):
    edge, face = like(BF16, 5, C, T), like(BF16, C, ROW)
    return call(edges_body, (edge, edge, face, face), [], 100_000, field, xeven, xodd)


def sort_edges(even, odd, near):
    for when, low, high in ((is_even("gy"), odd, even), (jnp.logical_not(is_even("gy")), even, odd)):

        @pl.when(when)
        def _(low=low, high=high):
            for row in range(5):
                a, b = low[row].astype(F32), high[row].astype(F32)
                near[row] = halves(a, b)
                near[row + 5] = halves(swap_halves(a), swap_halves(b))


def activation(pre, grad_out):
    sig = 1.0 / (1.0 + jnp.exp(-pre))
    return grad_out.astype(F32) * sig * (1.0 + pre * (1.0 - sig))


def stack(out, i, field, near):
    row = i * 3 * C
    out[row : row + C, :T] = halves(near, swap_halves(field[:, tile(7)].astype(F32))).astype(BF16)
    out[row : row + C, T:] = field[:, : 7 * T]
    out[row + C : row + 2 * C, :] = field[...]
    out[row + 2 * C : row + 3 * C, : 7 * T] = field[:, T:]
    out[row + 2 * C : row + 3 * C, 7 * T :] = halves(swap_halves(field[:, tile(0)].astype(F32)), near).astype(BF16)


def step_z(part):
    return from_below(part[:64]) + part[64:128] + from_above(part[128:])


def field_at(x, field, xlow, xhigh):
    return xlow if x < 0 else xhigh if x > 7 else field.at[x]


def front_body(vx, gx, xlow, xhigh, yeven, yodd, wf, bias, gp, even, odd, wire, near, cols, gps):
    sort_edges(yeven, yodd, near)
    for x in range(-1, 9):
        stack(cols, x + 1, field_at(x, vx, xlow, xhigh), near[x + 1])
    offset = jnp.concatenate([bias[...]] * 2, axis=0)
    total = jnp.zeros((64, T), F32)
    for q in range(4):
        both = jnp.dot(wf[...], cols[q * 192 : q * 192 + 384, :], preferred_element_type=F32)
        for t in range(8):
            grad_out = gx[2 * q : 2 * q + 2, :, tile(t)].reshape(64, T)
            grad = activation(step_z(both[:, tile(t)]) + offset, grad_out).astype(BF16)
            gp[2 * q : 2 * q + 2, :, tile(t)] = grad.reshape(2, C, T)
            grad = grad.astype(F32)
            total = total + grad
            gps[q * 192 : q * 192 + 64, tile(t)] = from_above(grad).astype(BF16)
            gps[q * 192 + 64 : q * 192 + 128, tile(t)] = grad.astype(BF16)
            gps[q * 192 + 128 : q * 192 + 192, tile(t)] = from_below(grad).astype(BF16)
    faces(gp, even, odd)
    prod = jnp.zeros((384, 192), F32)
    for q in range(4):
        prod = prod + lax.dot_general(
            cols[q * 192 : q * 192 + 384, :],
            gps[q * 192 : q * 192 + 192, :],
            (((1,), (1,)), ((), ())),
            preferred_element_type=F32,
        )
    group = lane((8, T)) // C
    rows = []
    for row in range(0, 288, 8):
        a, b = prod[row : row + 8], prod[row + 96 : row + 104]
        a = jnp.concatenate([a[:, T:], jnp.zeros((8, 64), F32)], axis=1), a[:, :T]
        b = jnp.concatenate([b[:, T:], jnp.zeros((8, 64), F32)], axis=1), b[:, :T]
        near = a[1] + pltpu.roll(b[1], T - C, 1)
        far = a[0] + pltpu.roll(b[0], T - C, 1)
        rows.append((near, pltpu.roll(near, T - C, 1), pltpu.roll(far, 2 * C, 1), far))
    for i in range(27):
        near, moved, far, _ = rows[i]
        dz, at = divmod(i, 9)
        near2, moved2, far2, plain2 = rows[27 + at]
        last = pltpu.roll((near2, near2, plain2)[dz], (3 * C, C, 3 * C)[dz], 1)
        out = jnp.where(group == 0, near, jnp.where(group == 1, moved, jnp.where(group == 2, far, last)))
        wire[8 * i : 8 * i + 8] = out
    total = jnp.concatenate([total[:C] + total[C:], jnp.zeros((T - C, T), F32)], axis=0)
    total = jnp.sum(total.T, axis=0, keepdims=True)
    wire[216:] = jnp.broadcast_to(total, (8, T))


def front(vx, gx, xlow, xhigh, yeven, yodd, wf, bias):
    face = like(BF16, C, ROW)
    out = (like(BF16, 8, C, ROW), face, face, like(F32, 224, T))
    scratch = [pltpu.VMEM((10, C, T), F32), pltpu.VMEM((960, ROW), BF16), pltpu.VMEM((768, ROW), BF16)]
    return call(front_body, out, scratch, 2_500_000_000, vx, gx, xlow, xhigh, yeven, yodd, wf, bias)


def back_body(gp, xlow, xhigh, yeven, yodd, wd, data, near, cols, stage, block, sems):
    sort_edges(yeven, yodd, near)
    for x in range(-1, 9):
        stack(cols, x + 1, field_at(x, gp, xlow, xhigh), near[x + 1])
    copies = []
    for q in range(4):
        both = jnp.dot(wd[...], cols[q * 192 : q * 192 + 384, :], preferred_element_type=F32)
        for t in range(8):
            out = step_z(both[:, tile(t)])
            for x in range(2):
                stage[2 * q + x, pl.ds(t, C, stride=8), :] = out[x * C : x * C + C]
        for x in (2 * q, 2 * q + 1):
            for pair in range(C // 2):
                even, odd = stage[x, pl.ds(pair * 16, 8), :], stage[x, pl.ds(pair * 16 + 8, 8), :]
                block[x, :, tile(pair)] = jnp.concatenate(exchange_halves(even, odd), axis=0).astype(BF16)
        copies.append(pltpu.make_async_copy(block.at[pl.ds(2 * q, 2)], data.at[pl.ds(2 * q, 2)], sems.at[q]))
        copies[-1].start()
    for copy in copies:
        copy.wait()


def back(gp, xlow, xhigh, yeven, yodd, wd):
    scratch = [
        pltpu.VMEM((10, C, T), F32),
        pltpu.VMEM((960, ROW), BF16),
        pltpu.VMEM((8, 8 * C, T), F32),
        pltpu.VMEM((8, 16, C * Z), BF16),
        pltpu.SemaphoreType.DMA((4,)),
    ]
    out = like(BF16, 8, 16, C * Z)
    return call(back_body, out, scratch, 1_000_000_000, gp, xlow, xhigh, yeven, yodd, wd, out_specs=HBM)


def add_body(a, b, out):
    out[...] = (a[...].astype(F32) + b[...].astype(F32)).astype(out.dtype)


def add(a, b, dtype):
    return call(add_body, like(dtype, *a.shape), [], 100_000, a, b)


def finish_body(scale, own, other, filters, biases):
    for when, wire in ((is_even("gx"), other), (jnp.logical_not(is_even("gx")), own)):

        @pl.when(when)
        def _(wire=wire):
            for row in range(0, 288, 8):
                for dz in range(3):
                    at, group = (row, dz) if row < 216 else (row - 216 + 72 * dz, 3)
                    part = wire[at : at + 8]
                    moved = part if group == 0 else pltpu.roll(part, T - group * C, 1)
                    block, inside = divmod(row, C)
                    filters[block * 3 + dz, inside : inside + 8, :] = moved[:, :C] * scale
            biases[...] = wire[216:217, :C] * scale


def finish(own, other, scale):
    out = (like(F32, 27, C, C), like(F32, 1, C))
    return call(lambda *refs: finish_body(scale, *refs), out, [], 100_000, own, other)


def swap(array, axis, size, odd):
    pairs = []
    for low in range(odd, size - 1, 2):
        pairs += [(low, low + 1), (low + 1, low)]
    return lax.ppermute(array, axis, pairs)


def band(strip):
    pad = [jnp.pad(strip, ((0, 0), (0, 0), (96 * x, 96 - 96 * x))) for x in range(2)]
    return jnp.stack(pad, axis=1).reshape(192, 384)


def shards(volume, cotangent, weight, bias):
    nx, ny = lax.axis_size("gx"), lax.axis_size("gy")
    wf = band(jnp.transpose(weight, (2, 4, 0, 1, 3)).reshape(3, C, 288))
    wd = band(jnp.transpose(weight[::-1, ::-1, ::-1], (2, 3, 0, 1, 4)).reshape(3, C, 288))
    vx, gx, xeven, xodd = pack(volume, cotangent)
    xodd, bias = lax.optimization_barrier((xodd, bias))
    offset = jnp.broadcast_to(bias[:, None], (C, T))
    xodd = swap(xodd, "gx", nx, 1)
    xeven = swap(xeven, "gx", nx, 0)
    xodd, offset = lax.optimization_barrier((xodd, offset))
    yeven, yodd, xlow, xhigh = edges(vx, xeven, xodd)
    yodd = swap(yodd, "gy", ny, 1)
    yeven = swap(yeven, "gy", ny, 0)
    gp, xeven, xodd, wire = front(vx, gx, xlow, xhigh, yeven, yodd, wf, offset)

    state = dict(gp=gp, xeven=xeven, xodd=xodd)

    def along_x():
        state["xodd"] = swap(state["xodd"], "gx", nx, 1)
        state["xeven"] = swap(state["xeven"], "gx", nx, 0)

    def along_y():
        yeven, yodd, xlow, xhigh = edges(state["gp"], state.pop("xeven"), state.pop("xodd"))
        state.update(yeven=yeven, yodd=yodd, xlow=xlow, xhigh=xhigh)
        state["yeven"] = swap(yeven, "gy", ny, 0)

    def along_y_odd():
        state["yodd"] = swap(state["yodd"], "gy", ny, 1)

    def data():
        state["data"] = back(state["gp"], state["xlow"], state["xhigh"], state["yeven"], state["yodd"], wd)

    def beside(work, sent, move):
        sent, given = lax.optimization_barrier((sent, dict(state)))
        state.update(given)
        got = move(sent)
        work()
        return sent, got

    def between(axis, step):
        pairs = []
        for x in range(1, nx, 2):
            for y in range(ny):
                to = (x ^ step, y) if axis == "gx" else (x, y ^ step)
                pairs.append((x * ny + y, to[0] * ny + to[1]))
        return lambda sent: lax.ppermute(sent, ("gx", "gy"), pairs)

    wire = add(wire, swap(wire, "gx", nx, 0), BF16)
    steps = [("gx", 1 << b) for b in range(1, nx.bit_length() - 1)] + [("gy", 1 << b) for b in range(ny.bit_length() - 1)]
    works = [along_x, along_y, along_y_odd, data]
    for n, (axis, step) in enumerate(steps):
        work = works.pop(0) if works else lambda: None
        sent, got = beside(work, wire, between(axis, step))
        last = n == len(steps) - 1
        if "data" in state:
            got, state["data"] = lax.optimization_barrier((got, state["data"]))
        wire = add(sent, got, F32 if last else BF16)
    for work in works:
        work()
    scale = 1.0 / math.sqrt(8 * nx * 16 * ny * Z)
    filters, biases = finish(wire, swap(wire, "gx", nx, 0), scale)
    return state["data"], filters.reshape(3, 3, 3, C, C), biases.reshape(C)


def solution(mesh):
    in_specs = (P("gx", "gy", None), P("gx", "gy", None), P(), P())
    out_specs = (P("gx", "gy", None), P(), P())
    return jax.shard_map(shards, mesh=mesh, in_specs=in_specs, out_specs=out_specs, check_vma=False)
```

time: 48 us -> 57.5 us (1.20)
  starting transfers between devices: 23.6 us -> 37.5 us
  Pallas kernels: 13.9 us -> 9.45 us
    ppermute x4 -> x10, starting transfers between devices: 4.6 us -> 34.8 us  [swap(): return lax.ppermute(array, axis, pairs)]
    ppermute x5 -> x4, starting transfers between devices: 19 us -> 2.63 us  [between(): return lambda sent: lax.ppermute(sent, ('gx', 'gy'), pairs)]
    pallas_call x9 -> x11, Pallas kernels: 13.9 us -> 9.45 us  [call(): pl.pallas_call(body, out_shape=out_shape, in_specs=in_specs or [VMEM] * l...]
    ppermute x4 -> x10, waiting for transfers between devices: 1.87 us -> 5.57 us  [swap(): return lax.ppermute(array, axis, pairs)]
    ppermute x5 -> x4, waiting for transfers between devices: 3.65 us -> 0.01 us  [between(): return lambda sent: lax.ppermute(sent, ('gx', 'gy'), pairs)]
  transfers between devices with their start and end apart: 9 -> 14, of which waited for: 5 -> 4; matrix products, arithmetic and copies ran while one was open for 2% -> 2% of each run, Pallas kernels for 13% -> 4%
where the time goes in v1:
time: 57.5 us; the launch traced here: 57.1 us
  starting transfers between devices  37.5 us (65%)
  Pallas kernels  9.45 us (16%)
  waiting for transfers between devices  5.58 us (10%)
  local copies, waits for them, and re-layouts  3.65 us (6%)
  between operations  0.93 us (2%)
    ppermute x10, starting transfers between devices, swap(): return lax.ppermute(array, axis, pairs)  34.8 us
    pallas_call x11, Pallas kernels, call(): pl.pallas_call(body, out_shape=out_shape, in_specs=in_specs or [VMEM] * l...  9.45 us
    ppermute x10, waiting for transfers between devices, swap(): return lax.ppermute(array, axis, pairs)  5.57 us
    ppermute x4, starting transfers between devices, between(): return lambda sent: lax.ppermute(sent, ('gx', 'gy'), pairs)  2.63 us
    unnamed x8, local copies, waits for them, and re-layouts  2.62 us
  transfers between devices with their start and end apart: 14, of which 4 were waited for; matrix products, arithmetic and copies ran while one was open for 2% of the time, Pallas kernels for 4%

profile of v1, /device:TPU:0, one launch (start us, length us, event | category | flops | bytes accessed | tf_op | source)
XLA Modules:
  0.0 57.1 jit_solution(6729613152929620836)
XLA Ops:
  0.6 0.0 copy-start
  0.6 1.0 %copy-done = bf16[8,16,2048]{2,1,0:T(8,128)(2,1)S(1)} copy-done((bf16[8,16,2048]{2,1,0:T(8,128)(2,1)S(1)}, bf16[8,16,2048]{2,1,0:T(8,128)(2,1)}, u32[]{:S(2)}) %copy-start) | copy-done | bytes 524312
  1.7 0.0 copy-start.1
  1.7 1.0 %copy-done.1 = bf16[8,16,2048]{2,1,0:T(8,128)(2,1)S(1)} copy-done((bf16[8,16,2048]{2,1,0:T(8,128)(2,1)S(1)}, bf16[8,16,2048]{2,1,0:T(8,128)(2,1)}, u32[]{:S(2)}) %copy-start.1) | copy-done | bytes 524312
  2.7 0.0 copy-start.2
  2.7 3.2 %shard_map.67 = (bf16[8,32,1024]{2,1,0:T(8,128)(2,1)S(1)}, bf16[8,32,1024]{2,1,0:T(8,128)(2,1)S(1)}, bf16[32,1024]{1,0:T(8,128)(2,1)S(1)}, bf16[32,1024]{1,0:T(8,128)(2,1)S(1)}) custom-call(bf16[8,16,2048]{2,1,0:T(8,128)(2,1)S(1)} %copy-done, bf16[8,16,2048]{2,1,0:T(8,128)(2,1)S(1)} %copy-done.1), custom_call_target="tpu_custom_call" | custom-call | flops 2000000 | bytes 2228224 | tf_op jit(solution)/shard_map/pallas_call | solution.py:23
  5.9 0.7 %collective-permute-start.1 = (bf16[32,1024]{1,0:T(8,128)(2,1)S(1)}, bf16[32,1024]{1,0:T(8,128)(2,1)S(1)}, u32[]{:S(2)}, u32[]{:S(2)}) collective-permute-start(bf16[32,1024]{1,0:T(8,128)(2,1)S(1)} %get-tuple-element.51), channel_id=1, source_target_pairs={{8,16},{16,8},{9,17},{17,9},{10,18},{18,10},{11,19},{19,11},{12,20... | collective-permute-start | bytes 196616 | tf_op jit(solution)/shard_map/ppermute | solution.py:297
  6.6 4.4 %collective-permute-start = (bf16[32,1024]{1,0:T(8,128)(2,1)S(1)}, bf16[32,1024]{1,0:T(8,128)(2,1)S(1)}, u32[]{:S(2)}, u32[]{:S(2)}) collective-permute-start(bf16[32,1024]{1,0:T(8,128)(2,1)S(1)} %get-tuple-element.49), channel_id=1, source_target_pairs={{0,8},{8,0},{16,24},{24,16},{1,9},{9,1},{17,25},{25,17},{2,10},{10... | collective-permute-start | bytes 196616 | tf_op jit(solution)/shard_map/ppermute | solution.py:297
  11.0 0.0 copy-done.2
  11.0 0.2 copy.9
  11.2 0.2 reshape.25
  11.4 0.0 copy-start.3
  11.4 0.1 pad_bitcast_fusion.3
  11.5 0.0 collective-permute-done.1.xodd
  11.5 0.5 copy-done.3
  12.0 0.1 broadcast_in_dim.2.bias
  12.1 0.0 collective-permute-done.xeven
  12.1 0.1 shard_map.68
  12.2 1.6 %collective-permute-start.2 = (bf16[5,32,128]{2,1,0:T(8,128)(2,1)S(1)}, bf16[5,32,128]{2,1,0:T(8,128)(2,1)S(1)}, u32[]{:S(2)}, u32[]{:S(2)}) collective-permute-start(bf16[5,32,128]{2,1,0:T(8,128)(2,1)S(1)} %get-tuple-element.56), channel_id=1, source_target_pairs={{0,1},{1,0},{2,3},{3,2},{4,5},{5,4},{6,7},{7,6},{8,9},{9,8},{10,11... | collective-permute-start | bytes 122888 | tf_op jit(solution)/shard_map/ppermute | solution.py:297
  13.8 0.7 %collective-permute-start.3 = (bf16[5,32,128]{2,1,0:T(8,128)(2,1)S(1)}, bf16[5,32,128]{2,1,0:T(8,128)(2,1)S(1)}, u32[]{:S(2)}, u32[]{:S(2)}) collective-permute-start(bf16[5,32,128]{2,1,0:T(8,128)(2,1)S(1)} %get-tuple-element.57), channel_id=1, source_target_pairs={{1,2},{2,1},{3,4},{4,3},{5,6},{6,5},{9,10},{10,9},{11,12},{12,11},... | collective-permute-start | bytes 122888 | tf_op jit(solution)/shard_map/ppermute | solution.py:297
  14.5 2.1 %collective-permute-done.2.yeven = bf16[5,32,128]{2,1,0:T(8,128)(2,1)S(1)} collective-permute-done((bf16[5,32,128]{2,1,0:T(8,128)(2,1)S(1)}, bf16[5,32,128]{2,1,0:T(8,128)(2,1)S(1)}, u32[]{:S(2)}, u32[]{:S(2)}) %collective-permute-start.2) | collective-permute-done | bytes 40992 | tf_op jit(solution)/shard_map/ppermute | solution.py:297
  16.6 0.0 collective-permute-done.3.yodd
  16.6 2.9 %shard_map.69 = (bf16[8,32,1024]{2,1,0:T(8,128)(2,1)S(1)}, bf16[32,1024]{1,0:T(8,128)(2,1)S(1)}, bf16[32,1024]{1,0:T(8,128)(2,1)S(1)}, f32[224,128]{1,0:T(8,128)S(1)}) custom-call(bf16[8,32,1024]{2,1,0:T(8,128)(2,1)S(1)} %get-tuple-element.47.field.vx, bf16[8,32,1024]{2,1,0:T(8,128)(2,1)S(1)} %get-tuple-element.48.gx, ...), custom_call_target="tpu_custom_call" | custom-call | flops 2500000000 | bytes 2195456 | tf_op jit(solution)/shard_map/pallas_call | solution.py:23
  19.5 0.1 collective-permute-start.4
  19.6 1.3 %collective-permute-done.4.b = f32[224,128]{1,0:T(8,128)S(1)} collective-permute-done((f32[224,128]{1,0:T(8,128)S(1)}, f32[224,128]{1,0:T(8,128)S(1)}, u32[]{:S(2)}, u32[]{:S(2)}) %collective-permute-start.4) | collective-permute-done | bytes 114720 | tf_op jit(solution)/shard_map/ppermute | solution.py:297
  20.9 0.7 %collective-permute-start.5 = (bf16[224,128]{1,0:T(8,128)(2,1)S(1)}, bf16[224,128]{1,0:T(8,128)(2,1)S(1)}, u32[]{:S(2)}, u32[]{:S(2)}) collective-permute-start(bf16[224,128]{1,0:T(8,128)(2,1)S(1)} %shard_map.70.a), channel_id=1, source_target_pairs={{8,24},{9,25},{10,26},{11,27},{12,28},{13,29},{14,30},{15,31},{24,... | collective-permute-start | bytes 172040 | tf_op jit(solution)/shard_map/ppermute | solution.py:350
  21.6 3.3 %collective-permute-start.6 = (bf16[32,1024]{1,0:T(8,128)(2,1)S(1)}, bf16[32,1024]{1,0:T(8,128)(2,1)S(1)}, u32[]{:S(2)}, u32[]{:S(2)}) collective-permute-start(bf16[32,1024]{1,0:T(8,128)(2,1)S(1)} %get-tuple-element.65), channel_id=1, source_target_pairs={{0,8},{8,0},{16,24},{24,16},{1,9},{9,1},{17,25},{25,17},{2,10},{10... | collective-permute-start | bytes 196616 | tf_op jit(solution)/shard_map/ppermute | solution.py:297
  24.9 0.7 %collective-permute-start.7 = (bf16[32,1024]{1,0:T(8,128)(2,1)S(1)}, bf16[32,1024]{1,0:T(8,128)(2,1)S(1)}, u32[]{:S(2)}, u32[]{:S(2)}) collective-permute-start(bf16[32,1024]{1,0:T(8,128)(2,1)S(1)} %get-tuple-element.66), channel_id=1, source_target_pairs={{8,16},{16,8},{9,17},{17,9},{10,18},{18,10},{11,19},{19,11},{12,20... | collective-permute-start | bytes 196616 | tf_op jit(solution)/shard_map/ppermute | solution.py:297
  25.6 0.2 copy.11
  25.7 0.2 reshape.27
  25.9 0.0 collective-permute-done.5.b
  26.0 0.0 collective-permute-done.6.xeven
  26.0 0.0 collective-permute-done.7.xodd
  26.0 0.1 shard_map.73
  26.1 4.9 %collective-permute-start.9 = (bf16[5,32,128]{2,1,0:T(8,128)(2,1)S(1)}, bf16[5,32,128]{2,1,0:T(8,128)(2,1)S(1)}, u32[]{:S(2)}, u32[]{:S(2)}) collective-permute-start(bf16[5,32,128]{2,1,0:T(8,128)(2,1)S(1)} %get-tuple-element.73), channel_id=1, source_target_pairs={{0,1},{1,0},{2,3},{3,2},{4,5},{5,4},{6,7},{7,6},{8,9},{9,8},{10,11... | collective-permute-start | bytes 122888 | tf_op jit(solution)/shard_map/ppermute | solution.py:297
  31.0 0.7 %collective-permute-start.8 = (bf16[224,128]{1,0:T(8,128)(2,1)S(1)}, bf16[224,128]{1,0:T(8,128)(2,1)S(1)}, u32[]{:S(2)}, u32[]{:S(2)}) collective-permute-start(bf16[224,128]{1,0:T(8,128)(2,1)S(1)} %shard_map.71.a), channel_id=1, source_target_pairs={{8,9},{9,8},{10,11},{11,10},{12,13},{13,12},{14,15},{15,14},{24,25... | collective-permute-start | bytes 172040 | tf_op jit(solution)/shard_map/ppermute | solution.py:350
  31.7 0.1 pad_bitcast_fusion.1
  31.8 0.0 collective-permute-done.8.b
  31.8 1.2 %collective-permute-done.9.yeven = bf16[5,32,128]{2,1,0:T(8,128)(2,1)S(1)} collective-permute-done((bf16[5,32,128]{2,1,0:T(8,128)(2,1)S(1)}, bf16[5,32,128]{2,1,0:T(8,128)(2,1)S(1)}, u32[]{:S(2)}, u32[]{:S(2)}) %collective-permute-start.9) | collective-permute-done | bytes 40992 | tf_op jit(solution)/shard_map/ppermute | solution.py:297
  33.0 0.7 %collective-permute-start.10 = (bf16[224,128]{1,0:T(8,128)(2,1)S(1)}, bf16[224,128]{1,0:T(8,128)(2,1)S(1)}, u32[]{:S(2)}, u32[]{:S(2)}) collective-permute-start(bf16[224,128]{1,0:T(8,128)(2,1)S(1)} %shard_map.72.a), channel_id=1, source_target_pairs={{8,10},{9,11},{10,8},{11,9},{12,14},{13,15},{14,12},{15,13},{24,26... | collective-permute-start | bytes 172040 | tf_op jit(solution)/shard_map/ppermute | solution.py:350
  33.6 0.7 %collective-permute-start.11 = (bf16[5,32,128]{2,1,0:T(8,128)(2,1)S(1)}, bf16[5,32,128]{2,1,0:T(8,128)(2,1)S(1)}, u32[]{:S(2)}, u32[]{:S(2)}) collective-permute-start(bf16[5,32,128]{2,1,0:T(8,128)(2,1)S(1)} %get-tuple-element.80), channel_id=1, source_target_pairs={{1,2},{2,1},{3,4},{4,3},{5,6},{6,5},{9,10},{10,9},{11,12},{12,11},... | collective-permute-start | bytes 122888 | tf_op jit(solution)/shard_map/ppermute | solution.py:297
  34.4 0.0 collective-permute-done.10.b
  34.4 0.0 collective-permute-done.11.yodd
  34.4 0.7 %collective-permute-start.12 = (bf16[224,128]{1,0:T(8,128)(2,1)S(1)}, bf16[224,128]{1,0:T(8,128)(2,1)S(1)}, u32[]{:S(2)}, u32[]{:S(2)}) collective-permute-start(bf16[224,128]{1,0:T(8,128)(2,1)S(1)} %shard_map.74.a), channel_id=1, source_target_pairs={{8,12},{9,13},{10,14},{11,15},{12,8},{13,9},{14,10},{15,11},{24,28... | collective-permute-start | bytes 172040 | tf_op jit(solution)/shard_map/ppermute | solution.py:350
  35.1 2.1 %shard_map.75 = bf16[8,16,2048]{2,1,0:T(8,128)(2,1)} custom-call(bf16[8,32,1024]{2,1,0:T(8,128)(2,1)S(1)} %get-tuple-element.82.field.gp, bf16[32,1024]{1,0:T(8,128)(2,1)S(1)} %get-tuple-element.83.xlow, bf16[32,1024]{1,0:T(8,128)(2,1)S(1)} %get-tuple-element.84.xhigh, bf16[5,32,128]{2,1,0:T(8,128)(2,1)S(1)} %collective-permute-done.9.yeven, ...), custom_call_target="tpu_custom_call" | custom-call | flops 1000000000 | bytes 1409024 | tf_op jit(solution)/shard_map/pallas_call | solution.py:23
  37.2 0.0 collective-permute-done.12.b
  37.2 18.0 %collective-permute-start.13 = (f32[224,128]{1,0:T(8,128)S(1)}, f32[224,128]{1,0:T(8,128)S(1)}, u32[]{:S(2)}, u32[]{:S(2)}) collective-permute-start(f32[224,128]{1,0:T(8,128)S(1)} %shard_map.76.refs_0_), channel_id=1, source_target_pairs={{0,8},{8,0},{16,24},{24,16},{1,9},{9,1},{17,25},{25,17},{2,10},{10... | collective-permute-start | bytes 344072 | tf_op jit(solution)/shard_map/ppermute | solution.py:297
  55.2 1.0 %collective-permute-done.13.refs_1_ = f32[224,128]{1,0:T(8,128)S(1)} collective-permute-done((f32[224,128]{1,0:T(8,128)S(1)}, f32[224,128]{1,0:T(8,128)S(1)}, u32[]{:S(2)}, u32[]{:S(2)}) %collective-permute-start.13) | collective-permute-done | bytes 114720 | tf_op jit(solution)/shard_map/ppermute | solution.py:297
  56.2 0.9 %shard_map.77 = (f32[27,32,32]{2,1,0:T(8,128)}, f32[1,32]{1,0:T(1,128)}) custom-call(f32[224,128]{1,0:T(8,128)S(1)} %shard_map.76.refs_0_, f32[224,128]{1,0:T(8,128)S(1)} %collective-permute-done.13.refs_1_), custom_call_target="tpu_custom_call" | custom-call | flops 100000 | bytes 340096 | tf_op jit(solution)/shard_map/pallas_call | solution.py:23
  (10 shorter events, 0.2 us)
Async XLA Ops:
  0.6 1.0 %copy-start = (bf16[8,16,2048]{2,1,0:T(8,128)(2,1)S(1)}, bf16[8,16,2048]{2,1,0:T(8,128)(2,1)}, u32[]{:S(2)}) copy-start(bf16[8,16,2048]{2,1,0:T(8,128)(2,1)} %v.1) | copy-start | bytes 1572868
  1.7 1.0 %copy-start.1 = (bf16[8,16,2048]{2,1,0:T(8,128)(2,1)S(1)}, bf16[8,16,2048]{2,1,0:T(8,128)(2,1)}, u32[]{:S(2)}) copy-start(bf16[8,16,2048]{2,1,0:T(8,128)(2,1)} %g.1) | copy-start | bytes 1572868
  2.7 8.3 %copy-start.2 = (bf16[3,3,3,32,32]{4,3,2,1,0:T(8,128)(2,1)S(1)}, bf16[3,3,3,32,32]{4,3,2,1,0:T(8,128)(2,1)}, u32[]{:S(2)}) copy-start(bf16[3,3,3,32,32]{4,3,2,1,0:T(8,128)(2,1)} %param.6) | copy-start | bytes 165892
  5.9 5.6 %collective-permute-start.1 = (bf16[32,1024]{1,0:T(8,128)(2,1)S(1)}, bf16[32,1024]{1,0:T(8,128)(2,1)S(1)}, u32[]{:S(2)}, u32[]{:S(2)}) collective-permute-start(bf16[32,1024]{1,0:T(8,128)(2,1)S(1)} %get-tuple-element.51), channel_id=1, source_target_pairs={{8,16},{16,8},{9,17},{17,9},{10,18},{18,10},{11,19},{19,11},{12,20... | collective-permute-start | bytes 196616 | tf_op jit(solution)/shard_map/ppermute | solution.py:297
  6.6 5.5 %collective-permute-start = (bf16[32,1024]{1,0:T(8,128)(2,1)S(1)}, bf16[32,1024]{1,0:T(8,128)(2,1)S(1)}, u32[]{:S(2)}, u32[]{:S(2)}) collective-permute-start(bf16[32,1024]{1,0:T(8,128)(2,1)S(1)} %get-tuple-element.49), channel_id=1, source_target_pairs={{0,8},{8,0},{16,24},{24,16},{1,9},{9,1},{17,25},{25,17},{2,10},{10... | collective-permute-start | bytes 196616 | tf_op jit(solution)/shard_map/ppermute | solution.py:297
  11.4 0.7 %copy-start.3 = (f32[32]{0:T(128)S(1)}, f32[32]{0:T(128)}, u32[]{:S(2)}) copy-start(f32[32]{0:T(128)} %param.7) | copy-start | bytes 388
  12.2 4.4 %collective-permute-start.2 = (bf16[5,32,128]{2,1,0:T(8,128)(2,1)S(1)}, bf16[5,32,128]{2,1,0:T(8,128)(2,1)S(1)}, u32[]{:S(2)}, u32[]{:S(2)}) collective-permute-start(bf16[5,32,128]{2,1,0:T(8,128)(2,1)S(1)} %get-tuple-element.56), channel_id=1, source_target_pairs={{0,1},{1,0},{2,3},{3,2},{4,5},{5,4},{6,7},{7,6},{8,9},{9,8},{10,11... | collective-permute-start | bytes 122888 | tf_op jit(solution)/shard_map/ppermute | solution.py:297
  13.8 2.8 %collective-permute-start.3 = (bf16[5,32,128]{2,1,0:T(8,128)(2,1)S(1)}, bf16[5,32,128]{2,1,0:T(8,128)(2,1)S(1)}, u32[]{:S(2)}, u32[]{:S(2)}) collective-permute-start(bf16[5,32,128]{2,1,0:T(8,128)(2,1)S(1)} %get-tuple-element.57), channel_id=1, source_target_pairs={{1,2},{2,1},{3,4},{4,3},{5,6},{6,5},{9,10},{10,9},{11,12},{12,11},... | collective-permute-start | bytes 122888 | tf_op jit(solution)/shard_map/ppermute | solution.py:297
  19.5 1.4 %collective-permute-start.4 = (f32[224,128]{1,0:T(8,128)S(1)}, f32[224,128]{1,0:T(8,128)S(1)}, u32[]{:S(2)}, u32[]{:S(2)}) collective-permute-start(f32[224,128]{1,0:T(8,128)S(1)} %get-tuple-element.59.a), channel_id=1, source_target_pairs={{0,8},{8,0},{16,24},{24,16},{1,9},{9,1},{17,25},{25,17},{2,10},{10... | collective-permute-start | bytes 344072 | tf_op jit(solution)/shard_map/ppermute | solution.py:297
  20.9 5.0 %collective-permute-start.5 = (bf16[224,128]{1,0:T(8,128)(2,1)S(1)}, bf16[224,128]{1,0:T(8,128)(2,1)S(1)}, u32[]{:S(2)}, u32[]{:S(2)}) collective-permute-start(bf16[224,128]{1,0:T(8,128)(2,1)S(1)} %shard_map.70.a), channel_id=1, source_target_pairs={{8,24},{9,25},{10,26},{11,27},{12,28},{13,29},{14,30},{15,31},{24,... | collective-permute-start | bytes 172040 | tf_op jit(solution)/shard_map/ppermute | solution.py:350
  21.6 4.4 %collective-permute-start.6 = (bf16[32,1024]{1,0:T(8,128)(2,1)S(1)}, bf16[32,1024]{1,0:T(8,128)(2,1)S(1)}, u32[]{:S(2)}, u32[]{:S(2)}) collective-permute-start(bf16[32,1024]{1,0:T(8,128)(2,1)S(1)} %get-tuple-element.65), channel_id=1, source_target_pairs={{0,8},{8,0},{16,24},{24,16},{1,9},{9,1},{17,25},{25,17},{2,10},{10... | collective-permute-start | bytes 196616 | tf_op jit(solution)/shard_map/ppermute | solution.py:297
  24.9 1.1 %collective-permute-start.7 = (bf16[32,1024]{1,0:T(8,128)(2,1)S(1)}, bf16[32,1024]{1,0:T(8,128)(2,1)S(1)}, u32[]{:S(2)}, u32[]{:S(2)}) collective-permute-start(bf16[32,1024]{1,0:T(8,128)(2,1)S(1)} %get-tuple-element.66), channel_id=1, source_target_pairs={{8,16},{16,8},{9,17},{17,9},{10,18},{18,10},{11,19},{19,11},{12,20... | collective-permute-start | bytes 196616 | tf_op jit(solution)/shard_map/ppermute | solution.py:297
  26.1 6.8 %collective-permute-start.9 = (bf16[5,32,128]{2,1,0:T(8,128)(2,1)S(1)}, bf16[5,32,128]{2,1,0:T(8,128)(2,1)S(1)}, u32[]{:S(2)}, u32[]{:S(2)}) collective-permute-start(bf16[5,32,128]{2,1,0:T(8,128)(2,1)S(1)} %get-tuple-element.73), channel_id=1, source_target_pairs={{0,1},{1,0},{2,3},{3,2},{4,5},{5,4},{6,7},{7,6},{8,9},{9,8},{10,11... | collective-permute-start | bytes 122888 | tf_op jit(solution)/shard_map/ppermute | solution.py:297
  31.0 0.8 %collective-permute-start.8 = (bf16[224,128]{1,0:T(8,128)(2,1)S(1)}, bf16[224,128]{1,0:T(8,128)(2,1)S(1)}, u32[]{:S(2)}, u32[]{:S(2)}) collective-permute-start(bf16[224,128]{1,0:T(8,128)(2,1)S(1)} %shard_map.71.a), channel_id=1, source_target_pairs={{8,9},{9,8},{10,11},{11,10},{12,13},{13,12},{14,15},{15,14},{24,25... | collective-permute-start | bytes 172040 | tf_op jit(solution)/shard_map/ppermute | solution.py:350
  33.0 1.4 %collective-permute-start.10 = (bf16[224,128]{1,0:T(8,128)(2,1)S(1)}, bf16[224,128]{1,0:T(8,128)(2,1)S(1)}, u32[]{:S(2)}, u32[]{:S(2)}) collective-permute-start(bf16[224,128]{1,0:T(8,128)(2,1)S(1)} %shard_map.72.a), channel_id=1, source_target_pairs={{8,10},{9,11},{10,8},{11,9},{12,14},{13,15},{14,12},{15,13},{24,26... | collective-permute-start | bytes 172040 | tf_op jit(solution)/shard_map/ppermute | solution.py:350
  33.6 0.8 %collective-permute-start.11 = (bf16[5,32,128]{2,1,0:T(8,128)(2,1)S(1)}, bf16[5,32,128]{2,1,0:T(8,128)(2,1)S(1)}, u32[]{:S(2)}, u32[]{:S(2)}) collective-permute-start(bf16[5,32,128]{2,1,0:T(8,128)(2,1)S(1)} %get-tuple-element.80), channel_id=1, source_target_pairs={{1,2},{2,1},{3,4},{4,3},{5,6},{6,5},{9,10},{10,9},{11,12},{12,11},... | collective-permute-start | bytes 122888 | tf_op jit(solution)/shard_map/ppermute | solution.py:297
  34.4 2.8 %collective-permute-start.12 = (bf16[224,128]{1,0:T(8,128)(2,1)S(1)}, bf16[224,128]{1,0:T(8,128)(2,1)S(1)}, u32[]{:S(2)}, u32[]{:S(2)}) collective-permute-start(bf16[224,128]{1,0:T(8,128)(2,1)S(1)} %shard_map.74.a), channel_id=1, source_target_pairs={{8,12},{9,13},{10,14},{11,15},{12,8},{13,9},{14,10},{15,11},{24,28... | collective-permute-start | bytes 172040 | tf_op jit(solution)/shard_map/ppermute | solution.py:350
  37.2 18.9 %collective-permute-start.13 = (f32[224,128]{1,0:T(8,128)S(1)}, f32[224,128]{1,0:T(8,128)S(1)}, u32[]{:S(2)}, u32[]{:S(2)}) collective-permute-start(f32[224,128]{1,0:T(8,128)S(1)} %shard_map.76.refs_0_), channel_id=1, source_target_pairs={{0,8},{8,0},{16,24},{24,16},{1,9},{9,1},{17,25},{25,17},{2,10},{10... | collective-permute-start | bytes 344072 | tf_op jit(solution)/shard_map/ppermute | solution.py:297

commit v2 on v1

v2 whole, which is shorter than its diff:
```python
import math

import jax
import jax.numpy as jnp
from jax import lax
from jax.experimental import pallas as pl
from jax.experimental.pallas import tpu as pltpu
from jax.sharding import PartitionSpec as P

C = 32
Z = 64
T = 128
ROW = 8 * T
HALF = 112
F32 = jnp.float32
BF16 = jnp.bfloat16
VMEM_LIMIT = 48 * 1024 * 1024
VMEM = pl.BlockSpec(memory_space=pltpu.VMEM)
HBM = pl.BlockSpec(memory_space=pltpu.HBM)


def call(body, out_shape, scratch_shapes, flops, *args, in_specs=None, out_specs=None, aliases=None):
    traffic = sum(math.prod(a.shape) * a.dtype.itemsize for a in (*args, *jax.tree.leaves(out_shape)))
    return pl.pallas_call(
        body,
        out_shape=out_shape,
        in_specs=in_specs or [VMEM] * len(args),
        out_specs=out_specs or jax.tree.map(lambda _: VMEM, out_shape),
        scratch_shapes=scratch_shapes,
        input_output_aliases=aliases or {},
        compiler_params=pltpu.CompilerParams(vmem_limit_bytes=VMEM_LIMIT),
        cost_estimate=pl.CostEstimate(flops=flops, bytes_accessed=traffic, transcendentals=0),
    )(*args)


def like(dtype, *shape):
    return jax.ShapeDtypeStruct(shape, dtype)


def lane(shape):
    return lax.broadcasted_iota(jnp.int32, shape, len(shape) - 1)


def swap_halves(a):
    return pltpu.roll(a, T // 2, a.ndim - 1)


def halves(low, high):
    return jnp.where(lane(low.shape) < T // 2, low, high)


def exchange_halves(a, b):
    mixed = swap_halves(halves(b, a))
    return halves(a, mixed), halves(mixed, b)


def from_below(a):
    return jnp.where(lane(a.shape) % Z == 0, 0.0, pltpu.roll(a, 1, a.ndim - 1))


def from_above(a):
    return jnp.where(lane(a.shape) % Z == Z - 1, 0.0, pltpu.roll(a, T - 1, a.ndim - 1))


def tile(t):
    return slice(t * T, t * T + T)


def to_channels(rows, stage):
    rows = rows.astype(F32)
    for pair in range(C // 2):
        even, odd = exchange_halves(rows[:8, tile(pair)], rows[8:, tile(pair)])
        stage[pl.ds(pair * 16, 8), :] = even
        stage[pl.ds(pair * 16 + 8, 8), :] = odd
    return [stage[pl.ds(t, C, stride=8), :] for t in range(8)]


def is_even(axis):
    return lax.axis_index(axis) % 2 == 0


def clear_ends(axis, low, high):
    @pl.when(lax.axis_index(axis) == 0)
    def _():
        low[...] = jnp.zeros_like(low)

    @pl.when(lax.axis_index(axis) == lax.axis_size(axis) - 1)
    def _():
        high[...] = jnp.zeros_like(high)


def my_half():
    total = 0
    for axis in ("gx", "gy"):
        for b in range(lax.axis_size(axis).bit_length() - 1):
            total = total + lax.axis_index(axis) // (1 << b)
    return total % 2


def faces(field, even, odd):
    for when, low, high in ((is_even("gx"), odd, even), (jnp.logical_not(is_even("gx")), even, odd)):

        @pl.when(when)
        def _(low=low, high=high):
            for t in range(8):
                low[:, tile(t)] = field(0, t)
                high[:, tile(t)] = field(7, t)


def pack_body(v, vx, *refs):
    stage = refs[-1]
    for x in range(8):
        for t, part in enumerate(to_channels(v[x], stage.at[x])):
            vx[x, :, tile(t)] = part.astype(BF16)
    if len(refs) > 1:
        faces(whole(vx), *refs[:2])


def pack(array, with_faces):
    face = like(BF16, C, ROW)
    out = (like(BF16, 8, C, ROW),) + (face, face) * with_faces
    return call(pack_body, out, [pltpu.VMEM((8, 8 * C, T), F32)], 1_000_000, array)


def whole(ref):
    return lambda x, t: ref[x, :, tile(t)]


def split(mid, edge):
    return lambda x, t: edge[x, :, tile(t // 7)] if t in (0, 7) else mid[x, :, tile(t - 1)]


def with_faces(field, xlow, xhigh):
    return lambda x, t: xlow[:, tile(t)] if x < 0 else xhigh[:, tile(t)] if x > 7 else field(x, t)


def faces_body(mid, edge, even, odd):
    faces(split(mid, edge), even, odd)


def gradient_faces(mid, edge):
    face = like(BF16, C, ROW)
    return call(faces_body, (face, face), [], 100_000, mid, edge)


def sort(axis, even, odd, low, high):
    @pl.when(is_even(axis))
    def _():
        low[...] = odd[...]
        high[...] = even[...]

    @pl.when(jnp.logical_not(is_even(axis)))
    def _():
        low[...] = even[...]
        high[...] = odd[...]

    clear_ends(axis, low, high)


def edge_message(field, low_when, out):
    @pl.when(low_when)
    def _():
        for row in range(5):
            out[row] = halves(field(row + 4, 0).astype(F32), swap_halves(field(row - 1, 0).astype(F32))).astype(BF16)

    @pl.when(jnp.logical_not(low_when))
    def _():
        for row in range(5):
            out[row] = halves(swap_halves(field(row - 1, 7).astype(F32)), field(row + 4, 7).astype(F32)).astype(BF16)


def ends(ref):
    last = ref.shape[-1] // T - 1
    return lambda x, t: ref[x, :, tile(last if t else 0)]


def odd_edge_body(field, xeven, xodd, out, xlow, xhigh):
    sort("gx", xeven, xodd, xlow, xhigh)
    edge_message(with_faces(ends(field), xlow, xhigh), is_even("gy"), out)


def odd_edge(field, xeven, xodd):
    face = like(BF16, C, ROW)
    return call(odd_edge_body, (like(BF16, 5, C, T), face, face), [], 100_000, field, xeven, xodd)


def even_edge_body(field, xlow, xhigh, out):
    edge_message(with_faces(ends(field), xlow, xhigh), jnp.logical_not(is_even("gy")), out)


def even_edge(field, xlow, xhigh):
    return call(even_edge_body, like(BF16, 5, C, T), [], 100_000, field, xlow, xhigh)


def sort_edges(even, odd, near):
    for when, low, high in ((is_even("gy"), odd, even), (jnp.logical_not(is_even("gy")), even, odd)):

        @pl.when(when)
        def _(low=low, high=high):
            for row in range(5):
                a, b = low[row].astype(F32), high[row].astype(F32)
                near[row] = halves(a, b)
                near[row + 5] = halves(swap_halves(a), swap_halves(b))

    place = lax.axis_index("gy")
    for when, empty in ((place == 0, 0), (place == lax.axis_size("gy") - 1, 1)):

        @pl.when(when)
        def _(empty=empty):
            for row in range(10):
                near[row] = halves(near[row], jnp.zeros((C, T), F32)) if empty else halves(jnp.zeros((C, T), F32), near[row])


def activation(pre, grad_out):
    sig = 1.0 / (1.0 + jnp.exp(-pre))
    return grad_out.astype(F32) * sig * (1.0 + pre * (1.0 - sig))


def stack(out, i, tiles, field, near=None):
    for n, t in enumerate(tiles):
        for dy in range(3):
            if t + dy == 0:
                part = halves(near, swap_halves(field(7).astype(F32))).astype(BF16)
            elif t + dy == 9:
                part = halves(swap_halves(field(0).astype(F32)), near).astype(BF16)
            else:
                part = field(t + dy - 1)
            out[(3 * i + dy) * C : (3 * i + dy + 1) * C, tile(n)] = part


def step_z(part):
    return from_below(part[:64]) + part[64:128] + from_above(part[128:])


def gradient(tiles, gx, wf, bias, cols, gps, out):
    offset = jnp.concatenate([bias[...]] * 2, axis=0)
    total = jnp.zeros((64, T), F32)
    for q in range(4):
        both = jnp.dot(wf[...], cols[q * 192 : q * 192 + 384, :], preferred_element_type=F32)
        for n, t in enumerate(tiles):
            grad_out = gx[2 * q : 2 * q + 2, :, tile(t)].reshape(64, T)
            grad = activation(step_z(both[:, tile(n)]) + offset, grad_out).astype(BF16)
            out[2 * q : 2 * q + 2, :, tile(n)] = grad.reshape(2, C, T)
            grad = grad.astype(F32)
            total = total + grad
            gps[q * 192 : q * 192 + 64, tile(n)] = from_above(grad).astype(BF16)
            gps[q * 192 + 64 : q * 192 + 128, tile(n)] = grad.astype(BF16)
            gps[q * 192 + 128 : q * 192 + 192, tile(n)] = from_below(grad).astype(BF16)
    prod = jnp.zeros((384, 192), F32)
    for q in range(4):
        prod = prod + lax.dot_general(
            cols[q * 192 : q * 192 + 384, :],
            gps[q * 192 : q * 192 + 192, :],
            (((1,), (1,)), ((), ())),
            preferred_element_type=F32,
        )
    return total, prod


MID = range(1, 7)
EDGE = (0, 7)


def middle_body(vx, gx, xlow, xhigh, wf, bias, gmid, total, prod, cols, gps):
    field = with_faces(whole(vx), xlow, xhigh)
    for x in range(-1, 9):
        stack(cols, x + 1, MID, lambda t, x=x: field(x, t))
    total[...], prod[...] = gradient(MID, gx, wf, bias, cols, gps, gmid)


def middle(vx, gx, xlow, xhigh, wf, bias):
    out = (like(BF16, 8, C, 6 * T), like(F32, 64, T), like(F32, 384, 192))
    scratch = [pltpu.VMEM((960, 6 * T), BF16), pltpu.VMEM((768, 6 * T), BF16)]
    return call(middle_body, out, scratch, 1_800_000_000, vx, gx, xlow, xhigh, wf, bias)


def outer_body(vx, gx, xlow, xhigh, yeven, yodd, wf, bias, total, prod, gedge, keep, give, near, cols, gps, wire):
    sort_edges(yeven, yodd, near)
    field = with_faces(whole(vx), xlow, xhigh)
    for x in range(-1, 9):
        stack(cols, x + 1, EDGE, lambda t, x=x: field(x, t), near[x + 1])
    more_total, more = gradient(EDGE, gx, wf, bias, cols, gps, gedge)
    total, prod = total[...] + more_total, prod[...] + more
    group = lane((8, T)) // C
    rows = []
    for row in range(0, 288, 8):
        a, b = prod[row : row + 8], prod[row + 96 : row + 104]
        a = jnp.concatenate([a[:, T:], jnp.zeros((8, 64), F32)], axis=1), a[:, :T]
        b = jnp.concatenate([b[:, T:], jnp.zeros((8, 64), F32)], axis=1), b[:, :T]
        near = a[1] + pltpu.roll(b[1], T - C, 1)
        far = a[0] + pltpu.roll(b[0], T - C, 1)
        rows.append((near, pltpu.roll(near, T - C, 1), pltpu.roll(far, 2 * C, 1), far))
    for i in range(27):
        near, moved, far, _ = rows[i]
        dz, at = divmod(i, 9)
        near2, moved2, far2, plain2 = rows[27 + at]
        last = pltpu.roll((near2, near2, plain2)[dz], (3 * C, C, 3 * C)[dz], 1)
        out = jnp.where(group == 0, near, jnp.where(group == 1, moved, jnp.where(group == 2, far, last)))
        wire[8 * i : 8 * i + 8] = out
    total = jnp.concatenate([total[:C] + total[C:], jnp.zeros((T - C, T), F32)], axis=0)
    total = jnp.sum(total.T, axis=0, keepdims=True)
    wire[216:] = jnp.broadcast_to(total, (8, T))
    for half in range(2):

        @pl.when(my_half() == half)
        def _(half=half):
            keep[...] = wire[half * HALF : half * HALF + HALF]
            give[...] = wire[HALF - half * HALF : 2 * HALF - half * HALF]


def outer(vx, gx, xlow, xhigh, yeven, yodd, wf, bias, total, prod):
    out = (like(BF16, 8, C, 2 * T), like(F32, HALF, T), like(F32, HALF, T))
    scratch = [
        pltpu.VMEM((10, C, T), F32),
        pltpu.VMEM((960, 2 * T), BF16),
        pltpu.VMEM((768, 2 * T), BF16),
        pltpu.VMEM((2 * HALF, T), F32),
    ]
    args = (vx, gx, xlow, xhigh, yeven, yodd, wf, bias, total, prod)
    return call(outer_body, out, scratch, 700_000_000, *args)


def back_body(gmid, gedge, xlow, xhigh, yeven, yodd, wd, data, near, cols, stage, block, sems):
    sort_edges(yeven, yodd, near)
    field = with_faces(split(gmid, gedge), xlow, xhigh)
    for x in range(-1, 9):
        stack(cols, x + 1, range(8), lambda t, x=x: field(x, t), near[x + 1])
    copies = []
    for q in range(4):
        both = jnp.dot(wd[...], cols[q * 192 : q * 192 + 384, :], preferred_element_type=F32)
        for t in range(8):
            out = step_z(both[:, tile(t)])
            for x in range(2):
                stage[2 * q + x, pl.ds(t, C, stride=8), :] = out[x * C : x * C + C]
        for x in (2 * q, 2 * q + 1):
            for pair in range(C // 2):
                even, odd = stage[x, pl.ds(pair * 16, 8), :], stage[x, pl.ds(pair * 16 + 8, 8), :]
                block[x, :, tile(pair)] = jnp.concatenate(exchange_halves(even, odd), axis=0).astype(BF16)
        copies.append(pltpu.make_async_copy(block.at[pl.ds(2 * q, 2)], data.at[pl.ds(2 * q, 2)], sems.at[q]))
        copies[-1].start()
    for copy in copies:
        copy.wait()


def back(gmid, gedge, xlow, xhigh, yeven, yodd, wd):
    scratch = [
        pltpu.VMEM((10, C, T), F32),
        pltpu.VMEM((960, ROW), BF16),
        pltpu.VMEM((8, 8 * C, T), F32),
        pltpu.VMEM((8, 16, C * Z), BF16),
        pltpu.SemaphoreType.DMA((4,)),
    ]
    out = like(BF16, 8, 16, C * Z)
    return call(back_body, out, scratch, 1_000_000_000, gmid, gedge, xlow, xhigh, yeven, yodd, wd, out_specs=HBM)


def add_body(a, b, out):
    out[...] = (a[...].astype(F32) + b[...].astype(F32)).astype(out.dtype)


def add(a, b, dtype):
    return call(add_body, like(dtype, *a.shape), [], 100_000, a, b)


def finish_body(scale, own, other, filters, biases):
    for half, halves_of in enumerate(((own, other), (other, own))):

        @pl.when(my_half() == half)
        def _(halves_of=halves_of):
            for row in range(0, 288, 8):
                for dz in range(3):
                    at, group = (row, dz) if row < 216 else (row - 216 + 72 * dz, 3)
                    part = halves_of[at // HALF][at % HALF : at % HALF + 8]
                    moved = part if group == 0 else pltpu.roll(part, T - group * C, 1)
                    block, inside = divmod(row, C)
                    filters[block * 3 + dz, inside : inside + 8, :] = moved[:, :C] * scale
            biases[...] = halves_of[1][216 - HALF : 217 - HALF, :C] * scale


def finish(own, other, scale):
    out = (like(F32, 27, C, C), like(F32, 1, C))
    return call(lambda *refs: finish_body(scale, *refs), out, [], 100_000, own, other)


def permute(array, target):
    nx, ny = lax.axis_size("gx"), lax.axis_size("gy")
    pairs = []
    for x in range(nx):
        for y in range(ny):
            to = target(x, y)
            pairs.append((x * ny + y, to[0] * ny + to[1]))
    return lax.ppermute(array, ("gx", "gy"), pairs)


def swap_x(array, odd):
    nx = lax.axis_size("gx")
    return permute(array, lambda x, y: ((((x + odd) ^ 1) - odd) % nx, y))


def swap_y(array, odd):
    ny = lax.axis_size("gy")

    def target(x, y):
        to = ((y + odd) ^ 1) - odd
        return (x, to) if 0 <= to < ny else (x ^ 1, y)

    return permute(array, target)


def band(strip):
    pad = [jnp.pad(strip, ((0, 0), (0, 0), (96 * x, 96 - 96 * x))) for x in range(2)]
    return jnp.stack(pad, axis=1).reshape(192, 384)


def shards(volume, cotangent, weight, bias):
    nx, ny = lax.axis_size("gx"), lax.axis_size("gy")
    wf = band(jnp.transpose(weight, (2, 4, 0, 1, 3)).reshape(3, C, 288))
    wd = band(jnp.transpose(weight[::-1, ::-1, ::-1], (2, 3, 0, 1, 4)).reshape(3, C, 288))
    barrier = lax.optimization_barrier
    vx, xeven, xodd = pack(volume, True)
    xodd, bias, cotangent = barrier((xodd, bias, cotangent))
    offset = jnp.broadcast_to(bias[:, None], (C, T))
    xodd = swap_x(xodd, 1)
    xeven = swap_x(xeven, 0)
    (gx,) = pack(cotangent, False)
    xodd, offset, gx = barrier((xodd, offset, gx))
    yodd, xlow, xhigh = odd_edge(vx, xeven, xodd)
    yodd, xlow, xhigh = barrier((yodd, xlow, xhigh))
    yeven = even_edge(vx, xlow, xhigh)
    yodd = swap_y(yodd, 1)
    yeven, xlow, xhigh = barrier((yeven, xlow, xhigh))
    yeven = swap_y(yeven, 0)
    gmid, total, prod = middle(vx, gx, xlow, xhigh, wf, offset)
    gedge, keep, give = outer(vx, gx, xlow, xhigh, yeven, yodd, wf, offset, total, prod)

    state = dict(gmid=gmid, gedge=gedge)

    def along_x():
        xeven, xodd = gradient_faces(state["gmid"], state["gedge"])
        state["xodd"] = swap_x(xodd, 1)
        state["xeven"] = swap_x(xeven, 0)

    def along_y_odd():
        yodd, state["xlow"], state["xhigh"] = odd_edge(state["gedge"], state.pop("xeven"), state.pop("xodd"))
        state["yodd"] = swap_y(yodd, 1)

    def along_y_even():
        state["yeven"] = swap_y(even_edge(state["gedge"], state["xlow"], state["xhigh"]), 0)

    def data():
        names = ("gmid", "gedge", "xlow", "xhigh", "yeven", "yodd")
        state["data"] = back(*(state[name] for name in names), wd)

    def step(sent, move, work, then):
        if work:
            sent, given = barrier((sent, dict(state)))
            state.update(given)
        got = move(sent)
        if work:
            work()
        if then:
            got, state[then] = barrier((got, state[then]))
        return got

    got = step(give, lambda sent: swap_x(sent, 0), along_x, None)
    wire = add(keep, got, BF16)
    steps = [(1 << b, 0) for b in range(1, nx.bit_length() - 1)] + [(0, 1 << b) for b in range(ny.bit_length() - 1)]
    works = [(None, None), (along_y_odd, None), (along_y_even, None), (data, "data")]
    for n, (dx, dy) in enumerate(steps):
        work, then = works.pop(0) if works else (None, None)
        got = step(wire, lambda sent: permute(sent, lambda x, y: (x ^ dx ^ 1, y ^ dy)), work, then)
        wire = add(wire, got, F32 if n == len(steps) - 1 else BF16)
    for work, _ in works:
        if work:
            work()
    scale = 1.0 / math.sqrt(8 * nx * 16 * ny * Z)
    filters, biases = finish(wire, swap_x(wire, 0), scale)
    return state["data"], filters.reshape(3, 3, 3, C, C), biases.reshape(C)


def solution(mesh):
    in_specs = (P("gx", "gy", None), P("gx", "gy", None), P(), P())
    out_specs = (P("gx", "gy", None), P(), P())
    return jax.shard_map(shards, mesh=mesh, in_specs=in_specs, out_specs=out_specs, check_vma=False)
```

time: 57.5 us -> 38.9 us (0.68)
  starting transfers between devices: 37.5 us -> 19.8 us
  waiting for transfers between devices: 5.58 us -> 7.31 us
  Pallas kernels: 9.45 us -> 7.78 us
  local copies, waits for them, and re-layouts: 3.65 us -> 2.85 us
    ppermute x14, starting transfers between devices: 37.5 us -> 19.8 us  [permute(): return lax.ppermute(array, ('gx', 'gy'), pairs)]
    ppermute x14, waiting for transfers between devices: 5.58 us -> 7.31 us  [permute(): return lax.ppermute(array, ('gx', 'gy'), pairs)]
    pallas_call x11 -> x16, Pallas kernels: 9.45 us -> 7.78 us  [call(): pl.pallas_call(body, out_shape=out_shape, in_specs=in_specs or [VMEM] * l...]
    unnamed x8, local copies, waits for them, and re-layouts: 2.62 us -> 1.82 us
  transfers between devices with their start and end apart: 14 -> 14, of which waited for: 4 -> 5; matrix products, arithmetic and copies ran while one was open for 2% -> 3% of each run, Pallas kernels for 4% -> 12%
where the time goes in v2:
time: 38.9 us; the launch traced here: 38.6 us
  starting transfers between devices  19.8 us (51%)
  Pallas kernels  7.78 us (20%)
  waiting for transfers between devices  7.31 us (19%)
  local copies, waits for them, and re-layouts  2.85 us (7%)
  between operations  0.86 us (2%)
    ppermute x14, starting transfers between devices, permute(): return lax.ppermute(array, ('gx', 'gy'), pairs)  19.8 us
    pallas_call x16, Pallas kernels, call(): pl.pallas_call(body, out_shape=out_shape, in_specs=in_specs or [VMEM] * l...  7.78 us
    ppermute x14, waiting for transfers between devices, permute(): return lax.ppermute(array, ('gx', 'gy'), pairs)  7.31 us
    unnamed x8, local copies, waits for them, and re-layouts  1.82 us
  transfers between devices with their start and end apart: 14, of which 5 were waited for; matrix products, arithmetic and copies ran while one was open for 3% of the time, Pallas kernels for 12%

profile of v2, /device:TPU:0, one launch (start us, length us, event | category | flops | bytes accessed | tf_op | source)
XLA Modules:
  0.0 38.6 jit_solution(8464491791194585092)
XLA Ops:
  0.6 0.0 copy-start
  0.6 1.0 %copy-done = bf16[8,16,2048]{2,1,0:T(8,128)(2,1)S(1)} copy-done((bf16[8,16,2048]{2,1,0:T(8,128)(2,1)S(1)}, bf16[8,16,2048]{2,1,0:T(8,128)(2,1)}, u32[]{:S(2)}) %copy-start) | copy-done | bytes 524312
  1.7 0.0 copy-start.2
  1.7 0.3 shard_map.67
  2.0 2.5 %collective-permute-start = (bf16[32,1024]{1,0:T(8,128)(2,1)S(1)}, bf16[32,1024]{1,0:T(8,128)(2,1)S(1)}, u32[]{:S(2)}, u32[]{:S(2)}) collective-permute-start(bf16[32,1024]{1,0:T(8,128)(2,1)S(1)} %get-tuple-element.56), channel_id=1, source_target_pairs={{0,24},{1,25},{2,26},{3,27},{4,28},{5,29},{6,30},{7,31},{8,16},{9,... | collective-permute-start | bytes 196616 | tf_op jit(solution)/shard_map/ppermute | solution.py:392
  4.5 0.7 %collective-permute-start.1 = (bf16[32,1024]{1,0:T(8,128)(2,1)S(1)}, bf16[32,1024]{1,0:T(8,128)(2,1)S(1)}, u32[]{:S(2)}, u32[]{:S(2)}) collective-permute-start(bf16[32,1024]{1,0:T(8,128)(2,1)S(1)} %get-tuple-element.60), channel_id=1, source_target_pairs={{0,8},{1,9},{2,10},{3,11},{4,12},{5,13},{6,14},{7,15},{8,0},{9,1},... | collective-permute-start | bytes 196616 | tf_op jit(solution)/shard_map/ppermute | solution.py:392
  5.2 0.0 copy-done.2
  5.2 0.2 copy.9
  5.3 0.0 copy-start.1
  5.4 0.2 reshape.25
  5.6 0.1 pad_bitcast_fusion.3
  5.7 0.7 %copy-done.1 = bf16[8,16,2048]{2,1,0:T(8,128)(2,1)S(1)} copy-done((bf16[8,16,2048]{2,1,0:T(8,128)(2,1)S(1)}, bf16[8,16,2048]{2,1,0:T(8,128)(2,1)}, u32[]{:S(2)}) %copy-start.1) | copy-done | bytes 524312
  6.4 0.0 copy-start.3
  6.4 0.3 shard_map.68.gx
  6.7 0.2 collective-permute-done.xodd
  7.0 0.1 copy-done.3
  7.1 0.1 broadcast_in_dim.2.bias
  7.1 0.0 collective-permute-done.1.xeven
  7.1 0.1 shard_map.69
  7.2 0.1 shard_map.70
  7.3 2.3 %collective-permute-start.2 = (bf16[5,32,128]{2,1,0:T(8,128)(2,1)S(1)}, bf16[5,32,128]{2,1,0:T(8,128)(2,1)S(1)}, u32[]{:S(2)}, u32[]{:S(2)}) collective-permute-start(bf16[5,32,128]{2,1,0:T(8,128)(2,1)S(1)} %shard_map.70), channel_id=1, source_target_pairs={{0,1},{1,0},{2,3},{3,2},{4,5},{5,4},{6,7},{7,6},{8,9},{9,8},{10,11... | collective-permute-start | bytes 122888 | tf_op jit(solution)/shard_map/ppermute | solution.py:392
  9.7 0.0 collective-permute-start.3
  9.7 2.2 %shard_map.71 = (bf16[8,32,768]{2,1,0:T(8,128)(2,1)S(1)}, f32[64,128]{1,0:T(8,128)S(1)}, f32[384,192]{1,0:T(8,128)S(1)}) custom-call(bf16[8,32,1024]{2,1,0:T(8,128)(2,1)S(1)} %get-tuple-element.54.field.vx, bf16[8,32,1024]{2,1,0:T(8,128)(2,1)S(1)} %shard_map.68.gx, bf16[32,1024]{1,0:T(8,128)(2,1)S(1)} %get-tuple-element.64.xlow, ...), custom_call_target="tpu_custom_call" | custom-call | flops 1800000000 | bytes 2064384 | tf_op jit(solution)/shard_map/pallas_call | solution.py:24
  11.9 0.0 collective-permute-done.2.yeven
  11.9 0.0 collective-permute-done.3.yodd
  11.9 1.4 %shard_map.72 = (bf16[8,32,256]{2,1,0:T(8,128)(2,1)S(1)}, f32[112,128]{1,0:T(8,128)S(1)}, f32[112,128]{1,0:T(8,128)S(1)}) custom-call(bf16[8,32,1024]{2,1,0:T(8,128)(2,1)S(1)} %get-tuple-element.54.field.vx, bf16[8,32,1024]{2,1,0:T(8,128)(2,1)S(1)} %shard_map.68.gx, bf16[32,1024]{1,0:T(8,128)(2,1)S(1)} %get-tuple-element.64.xlow, ...), custom_call_target="tpu_custom_call" | custom-call | flops 700000000 | bytes 1998848 | tf_op jit(solution)/shard_map/pallas_call | solution.py:24
  13.3 0.6 %collective-permute-start.4 = (f32[112,128]{1,0:T(8,128)S(1)}, f32[112,128]{1,0:T(8,128)S(1)}, u32[]{:S(2)}, u32[]{:S(2)}) collective-permute-start(f32[112,128]{1,0:T(8,128)S(1)} %get-tuple-element.75), channel_id=1, source_target_pairs={{0,8},{1,9},{2,10},{3,11},{4,12},{5,13},{6,14},{7,15},{8,0},{9,1},... | collective-permute-start | bytes 172040 | tf_op jit(solution)/shard_map/ppermute | solution.py:392
  13.9 0.1 collective-permute-start.6
  14.0 1.7 %collective-permute-start.7 = (bf16[32,1024]{1,0:T(8,128)(2,1)S(1)}, bf16[32,1024]{1,0:T(8,128)(2,1)S(1)}, u32[]{:S(2)}, u32[]{:S(2)}) collective-permute-start(bf16[32,1024]{1,0:T(8,128)(2,1)S(1)} %get-tuple-element.79), channel_id=1, source_target_pairs={{0,24},{1,25},{2,26},{3,27},{4,28},{5,29},{6,30},{7,31},{8,16},{9,... | collective-permute-start | bytes 196616 | tf_op jit(solution)/shard_map/ppermute | solution.py:392
  15.7 0.0 collective-permute-done.4.b
  15.7 0.7 %collective-permute-start.5 = (bf16[112,128]{1,0:T(8,128)(2,1)S(1)}, bf16[112,128]{1,0:T(8,128)(2,1)S(1)}, u32[]{:S(2)}, u32[]{:S(2)}) collective-permute-start(bf16[112,128]{1,0:T(8,128)(2,1)S(1)} %shard_map.73.a), channel_id=1, source_target_pairs={{0,24},{1,25},{2,26},{3,27},{4,28},{5,29},{6,30},{7,31},{8,16},{9,... | collective-permute-start | bytes 86024 | tf_op jit(solution)/shard_map/ppermute | solution.py:392
  16.4 0.2 copy.11
  16.6 0.2 reshape.27
  16.8 2.3 %collective-permute-done.5.b = bf16[112,128]{1,0:T(8,128)(2,1)S(1)} collective-permute-done((bf16[112,128]{1,0:T(8,128)(2,1)S(1)}, bf16[112,128]{1,0:T(8,128)(2,1)S(1)}, u32[]{:S(2)}, u32[]{:S(2)}) %collective-permute-start.5) | collective-permute-done | bytes 28704 | tf_op jit(solution)/shard_map/ppermute | solution.py:392
  19.0 0.0 collective-permute-done.6.xeven
  19.1 0.0 collective-permute-done.7.xodd
  19.1 0.1 shard_map.77
  19.2 0.4 collective-permute-start.9
  19.6 4.8 %collective-permute-start.8 = (bf16[112,128]{1,0:T(8,128)(2,1)S(1)}, bf16[112,128]{1,0:T(8,128)(2,1)S(1)}, u32[]{:S(2)}, u32[]{:S(2)}) collective-permute-start(bf16[112,128]{1,0:T(8,128)(2,1)S(1)} %shard_map.74.a), channel_id=1, source_target_pairs={{0,9},{1,8},{2,11},{3,10},{4,13},{5,12},{6,15},{7,14},{8,1},{9,0},... | collective-permute-start | bytes 86024 | tf_op jit(solution)/shard_map/ppermute | solution.py:392
  24.3 0.1 pad_bitcast_fusion.1
  24.4 1.5 %collective-permute-done.8.b = bf16[112,128]{1,0:T(8,128)(2,1)S(1)} collective-permute-done((bf16[112,128]{1,0:T(8,128)(2,1)S(1)}, bf16[112,128]{1,0:T(8,128)(2,1)S(1)}, u32[]{:S(2)}, u32[]{:S(2)}) %collective-permute-start.8) | collective-permute-done | bytes 28704 | tf_op jit(solution)/shard_map/ppermute | solution.py:392
  25.9 0.0 collective-permute-done.9.yodd
  25.9 0.1 shard_map.79
  26.0 2.2 %collective-permute-start.11 = (bf16[5,32,128]{2,1,0:T(8,128)(2,1)S(1)}, bf16[5,32,128]{2,1,0:T(8,128)(2,1)S(1)}, u32[]{:S(2)}, u32[]{:S(2)}) collective-permute-start(bf16[5,32,128]{2,1,0:T(8,128)(2,1)S(1)} %shard_map.79), channel_id=1, source_target_pairs={{0,1},{1,0},{2,3},{3,2},{4,5},{5,4},{6,7},{7,6},{8,9},{9,8},{10,11... | collective-permute-start | bytes 122888 | tf_op jit(solution)/shard_map/ppermute | solution.py:392
  28.2 1.0 %collective-permute-start.10 = (bf16[112,128]{1,0:T(8,128)(2,1)S(1)}, bf16[112,128]{1,0:T(8,128)(2,1)S(1)}, u32[]{:S(2)}, u32[]{:S(2)}) collective-permute-start(bf16[112,128]{1,0:T(8,128)(2,1)S(1)} %shard_map.76.a), channel_id=1, source_target_pairs={{0,10},{1,11},{2,8},{3,9},{4,14},{5,15},{6,12},{7,13},{8,2},{9,3},... | collective-permute-start | bytes 86024 | tf_op jit(solution)/shard_map/ppermute | solution.py:392
  29.3 2.4 %collective-permute-done.10.b = bf16[112,128]{1,0:T(8,128)(2,1)S(1)} collective-permute-done((bf16[112,128]{1,0:T(8,128)(2,1)S(1)}, bf16[112,128]{1,0:T(8,128)(2,1)S(1)}, u32[]{:S(2)}, u32[]{:S(2)}) %collective-permute-start.10) | collective-permute-done | bytes 28704 | tf_op jit(solution)/shard_map/ppermute | solution.py:392
  31.7 0.0 collective-permute-done.11.yeven
  31.7 2.5 %collective-permute-start.12 = (bf16[112,128]{1,0:T(8,128)(2,1)S(1)}, bf16[112,128]{1,0:T(8,128)(2,1)S(1)}, u32[]{:S(2)}, u32[]{:S(2)}) collective-permute-start(bf16[112,128]{1,0:T(8,128)(2,1)S(1)} %shard_map.78.a), channel_id=1, source_target_pairs={{0,12},{1,13},{2,14},{3,15},{4,8},{5,9},{6,10},{7,11},{8,4},{9,5},... | collective-permute-start | bytes 86024 | tf_op jit(solution)/shard_map/ppermute | solution.py:392
  34.2 2.2 %shard_map.80 = bf16[8,16,2048]{2,1,0:T(8,128)(2,1)} custom-call(bf16[8,32,768]{2,1,0:T(8,128)(2,1)S(1)} %get-tuple-element.95.mid.gmid, bf16[8,32,256]{2,1,0:T(8,128)(2,1)S(1)} %get-tuple-element.96.edge.field.gedge, bf16[32,1024]{1,0:T(8,128)(2,1)S(1)} %get-tuple-element.97.xlow, bf16[32,1024]{1,0:T(8,128)(2,1)S(1)} %get-tuple-element.98.xhigh, ...), custom_call_target="tpu_custom_call" | custom-call | flops 1000000000 | bytes 1409024 | tf_op jit(solution)/shard_map/pallas_call | solution.py:24
  36.3 0.0 collective-permute-done.12.b
  36.4 0.5 %collective-permute-start.13 = (f32[112,128]{1,0:T(8,128)S(1)}, f32[112,128]{1,0:T(8,128)S(1)}, u32[]{:S(2)}, u32[]{:S(2)}) collective-permute-start(f32[112,128]{1,0:T(8,128)S(1)} %shard_map.81.refs_0_), channel_id=1, source_target_pairs={{0,8},{1,9},{2,10},{3,11},{4,12},{5,13},{6,14},{7,15},{8,0},{9,1},... | collective-permute-start | bytes 172040 | tf_op jit(solution)/shard_map/ppermute | solution.py:392
  36.8 0.9 %collective-permute-done.13.refs_1_ = f32[112,128]{1,0:T(8,128)S(1)} collective-permute-done((f32[112,128]{1,0:T(8,128)S(1)}, f32[112,128]{1,0:T(8,128)S(1)}, u32[]{:S(2)}, u32[]{:S(2)}) %collective-permute-start.13) | collective-permute-done | bytes 57376 | tf_op jit(solution)/shard_map/ppermute | solution.py:392
  37.7 0.9 %shard_map.82 = (f32[27,32,32]{2,1,0:T(8,128)}, f32[1,32]{1,0:T(1,128)}) custom-call(f32[112,128]{1,0:T(8,128)S(1)} %shard_map.81.refs_0_, f32[112,128]{1,0:T(8,128)S(1)} %collective-permute-done.13.refs_1_), custom_call_target="tpu_custom_call" | custom-call | flops 100000 | bytes 225408 | tf_op jit(solution)/shard_map/pallas_call | solution.py:24
  (11 shorter events, 0.2 us)
Async XLA Ops:
  0.6 1.0 %copy-start = (bf16[8,16,2048]{2,1,0:T(8,128)(2,1)S(1)}, bf16[8,16,2048]{2,1,0:T(8,128)(2,1)}, u32[]{:S(2)}) copy-start(bf16[8,16,2048]{2,1,0:T(8,128)(2,1)} %v.1) | copy-start | bytes 1572868
  1.7 3.5 %copy-start.2 = (bf16[3,3,3,32,32]{4,3,2,1,0:T(8,128)(2,1)S(1)}, bf16[3,3,3,32,32]{4,3,2,1,0:T(8,128)(2,1)}, u32[]{:S(2)}) copy-start(bf16[3,3,3,32,32]{4,3,2,1,0:T(8,128)(2,1)} %param.6) | copy-start | bytes 165892
  2.0 5.0 %collective-permute-start = (bf16[32,1024]{1,0:T(8,128)(2,1)S(1)}, bf16[32,1024]{1,0:T(8,128)(2,1)S(1)}, u32[]{:S(2)}, u32[]{:S(2)}) collective-permute-start(bf16[32,1024]{1,0:T(8,128)(2,1)S(1)} %get-tuple-element.56), channel_id=1, source_target_pairs={{0,24},{1,25},{2,26},{3,27},{4,28},{5,29},{6,30},{7,31},{8,16},{9,... | collective-permute-start | bytes 196616 | tf_op jit(solution)/shard_map/ppermute | solution.py:392
  4.5 2.7 %collective-permute-start.1 = (bf16[32,1024]{1,0:T(8,128)(2,1)S(1)}, bf16[32,1024]{1,0:T(8,128)(2,1)S(1)}, u32[]{:S(2)}, u32[]{:S(2)}) collective-permute-start(bf16[32,1024]{1,0:T(8,128)(2,1)S(1)} %get-tuple-element.60), channel_id=1, source_target_pairs={{0,8},{1,9},{2,10},{3,11},{4,12},{5,13},{6,14},{7,15},{8,0},{9,1},... | collective-permute-start | bytes 196616 | tf_op jit(solution)/shard_map/ppermute | solution.py:392
  5.3 1.0 %copy-start.1 = (bf16[8,16,2048]{2,1,0:T(8,128)(2,1)S(1)}, bf16[8,16,2048]{2,1,0:T(8,128)(2,1)}, u32[]{:S(2)}) copy-start(bf16[8,16,2048]{2,1,0:T(8,128)(2,1)} %v.2) | copy-start | bytes 1572868
  6.4 0.7 %copy-start.3 = (f32[32]{0:T(128)S(1)}, f32[32]{0:T(128)}, u32[]{:S(2)}) copy-start(f32[32]{0:T(128)} %param.7) | copy-start | bytes 388
  7.3 4.5 %collective-permute-start.2 = (bf16[5,32,128]{2,1,0:T(8,128)(2,1)S(1)}, bf16[5,32,128]{2,1,0:T(8,128)(2,1)S(1)}, u32[]{:S(2)}, u32[]{:S(2)}) collective-permute-start(bf16[5,32,128]{2,1,0:T(8,128)(2,1)S(1)} %shard_map.70), channel_id=1, source_target_pairs={{0,1},{1,0},{2,3},{3,2},{4,5},{5,4},{6,7},{7,6},{8,9},{9,8},{10,11... | collective-permute-start | bytes 122888 | tf_op jit(solution)/shard_map/ppermute | solution.py:392
  9.7 2.2 %collective-permute-start.3 = (bf16[5,32,128]{2,1,0:T(8,128)(2,1)S(1)}, bf16[5,32,128]{2,1,0:T(8,128)(2,1)S(1)}, u32[]{:S(2)}, u32[]{:S(2)}) collective-permute-start(bf16[5,32,128]{2,1,0:T(8,128)(2,1)S(1)} %get-tuple-element.67), channel_id=1, source_target_pairs={{0,8},{1,2},{2,1},{3,4},{4,3},{5,6},{6,5},{7,15},{8,0},{9,10},{10,... | collective-permute-start | bytes 122888 | tf_op jit(solution)/shard_map/ppermute | solution.py:392
  13.3 2.4 %collective-permute-start.4 = (f32[112,128]{1,0:T(8,128)S(1)}, f32[112,128]{1,0:T(8,128)S(1)}, u32[]{:S(2)}, u32[]{:S(2)}) collective-permute-start(f32[112,128]{1,0:T(8,128)S(1)} %get-tuple-element.75), channel_id=1, source_target_pairs={{0,8},{1,9},{2,10},{3,11},{4,12},{5,13},{6,14},{7,15},{8,0},{9,1},... | collective-permute-start | bytes 172040 | tf_op jit(solution)/shard_map/ppermute | solution.py:392
  13.9 5.2 %collective-permute-start.6 = (bf16[32,1024]{1,0:T(8,128)(2,1)S(1)}, bf16[32,1024]{1,0:T(8,128)(2,1)S(1)}, u32[]{:S(2)}, u32[]{:S(2)}) collective-permute-start(bf16[32,1024]{1,0:T(8,128)(2,1)S(1)} %get-tuple-element.78), channel_id=1, source_target_pairs={{0,8},{1,9},{2,10},{3,11},{4,12},{5,13},{6,14},{7,15},{8,0},{9,1},... | collective-permute-start | bytes 196616 | tf_op jit(solution)/shard_map/ppermute | solution.py:392
  14.0 5.1 %collective-permute-start.7 = (bf16[32,1024]{1,0:T(8,128)(2,1)S(1)}, bf16[32,1024]{1,0:T(8,128)(2,1)S(1)}, u32[]{:S(2)}, u32[]{:S(2)}) collective-permute-start(bf16[32,1024]{1,0:T(8,128)(2,1)S(1)} %get-tuple-element.79), channel_id=1, source_target_pairs={{0,24},{1,25},{2,26},{3,27},{4,28},{5,29},{6,30},{7,31},{8,16},{9,... | collective-permute-start | bytes 196616 | tf_op jit(solution)/shard_map/ppermute | solution.py:392
  15.7 3.4 %collective-permute-start.5 = (bf16[112,128]{1,0:T(8,128)(2,1)S(1)}, bf16[112,128]{1,0:T(8,128)(2,1)S(1)}, u32[]{:S(2)}, u32[]{:S(2)}) collective-permute-start(bf16[112,128]{1,0:T(8,128)(2,1)S(1)} %shard_map.73.a), channel_id=1, source_target_pairs={{0,24},{1,25},{2,26},{3,27},{4,28},{5,29},{6,30},{7,31},{8,16},{9,... | collective-permute-start | bytes 86024 | tf_op jit(solution)/shard_map/ppermute | solution.py:392
  19.2 6.7 %collective-permute-start.9 = (bf16[5,32,128]{2,1,0:T(8,128)(2,1)S(1)}, bf16[5,32,128]{2,1,0:T(8,128)(2,1)S(1)}, u32[]{:S(2)}, u32[]{:S(2)}) collective-permute-start(bf16[5,32,128]{2,1,0:T(8,128)(2,1)S(1)} %get-tuple-element.87), channel_id=1, source_target_pairs={{0,8},{1,2},{2,1},{3,4},{4,3},{5,6},{6,5},{7,15},{8,0},{9,10},{10,... | collective-permute-start | bytes 122888 | tf_op jit(solution)/shard_map/ppermute | solution.py:392
  19.6 6.3 %collective-permute-start.8 = (bf16[112,128]{1,0:T(8,128)(2,1)S(1)}, bf16[112,128]{1,0:T(8,128)(2,1)S(1)}, u32[]{:S(2)}, u32[]{:S(2)}) collective-permute-start(bf16[112,128]{1,0:T(8,128)(2,1)S(1)} %shard_map.74.a), channel_id=1, source_target_pairs={{0,9},{1,8},{2,11},{3,10},{4,13},{5,12},{6,15},{7,14},{8,1},{9,0},... | collective-permute-start | bytes 86024 | tf_op jit(solution)/shard_map/ppermute | solution.py:392
  26.0 5.6 %collective-permute-start.11 = (bf16[5,32,128]{2,1,0:T(8,128)(2,1)S(1)}, bf16[5,32,128]{2,1,0:T(8,128)(2,1)S(1)}, u32[]{:S(2)}, u32[]{:S(2)}) collective-permute-start(bf16[5,32,128]{2,1,0:T(8,128)(2,1)S(1)} %shard_map.79), channel_id=1, source_target_pairs={{0,1},{1,0},{2,3},{3,2},{4,5},{5,4},{6,7},{7,6},{8,9},{9,8},{10,11... | collective-permute-start | bytes 122888 | tf_op jit(solution)/shard_map/ppermute | solution.py:392
  28.2 3.5 %collective-permute-start.10 = (bf16[112,128]{1,0:T(8,128)(2,1)S(1)}, bf16[112,128]{1,0:T(8,128)(2,1)S(1)}, u32[]{:S(2)}, u32[]{:S(2)}) collective-permute-start(bf16[112,128]{1,0:T(8,128)(2,1)S(1)} %shard_map.76.a), channel_id=1, source_target_pairs={{0,10},{1,11},{2,8},{3,9},{4,14},{5,15},{6,12},{7,13},{8,2},{9,3},... | collective-permute-start | bytes 86024 | tf_op jit(solution)/shard_map/ppermute | solution.py:392
  31.7 4.6 %collective-permute-start.12 = (bf16[112,128]{1,0:T(8,128)(2,1)S(1)}, bf16[112,128]{1,0:T(8,128)(2,1)S(1)}, u32[]{:S(2)}, u32[]{:S(2)}) collective-permute-start(bf16[112,128]{1,0:T(8,128)(2,1)S(1)} %shard_map.78.a), channel_id=1, source_target_pairs={{0,12},{1,13},{2,14},{3,15},{4,8},{5,9},{6,10},{7,11},{8,4},{9,5},... | collective-permute-start | bytes 86024 | tf_op jit(solution)/shard_map/ppermute | solution.py:392
  36.4 1.4 %collective-permute-start.13 = (f32[112,128]{1,0:T(8,128)S(1)}, f32[112,128]{1,0:T(8,128)S(1)}, u32[]{:S(2)}, u32[]{:S(2)}) collective-permute-start(f32[112,128]{1,0:T(8,128)S(1)} %shard_map.81.refs_0_), channel_id=1, source_target_pairs={{0,8},{1,9},{2,10},{3,11},{4,12},{5,13},{6,14},{7,15},{8,0},{9,1},... | collective-permute-start | bytes 172040 | tf_op jit(solution)/shard_map/ppermute | solution.py:392

commit v3 on v2

--- a/solution.py
+++ b/solution.py
@@ -107,19 +107,14 @@
                 high[:, tile(t)] = field(7, t)
 
 
-def pack_body(v, vx, *refs):
-    stage = refs[-1]
-    for x in range(8):
-        for t, part in enumerate(to_channels(v[x], stage.at[x])):
-            vx[x, :, tile(t)] = part.astype(BF16)
-    if len(refs) > 1:
-        faces(whole(vx), *refs[:2])
-
-
-def pack(array, with_faces):
-    face = like(BF16, C, ROW)
-    out = (like(BF16, 8, C, ROW),) + (face, face) * with_faces
-    return call(pack_body, out, [pltpu.VMEM((8, 8 * C, T), F32)], 1_000_000, array)
+def pack_body(array, out, stage):
+    for x in range(array.shape[0]):
+        for t, part in enumerate(to_channels(array[x], stage.at[x])):
+            out[x, :, tile(t)] = part.astype(BF16)
+
+
+def pack(array):
+    return call(pack_body, like(BF16, 8, C, ROW), [pltpu.VMEM((8, 8 * C, T), F32)], 1_000_000, array)
 
 
 def whole(ref):
@@ -174,14 +169,20 @@
     return lambda x, t: ref[x, :, tile(last if t else 0)]
 
 
-def odd_edge_body(field, xeven, xodd, out, xlow, xhigh):
+def odd_edge_body(field, xeven, xodd, out, xlow, xhigh, *scratch):
+    if scratch:
+        stage, packed = scratch
+        pack_body(xeven, packed.at[pl.ds(0, 1)], stage.at[pl.ds(0, 1)])
+        pack_body(xodd, packed.at[pl.ds(1, 1)], stage.at[pl.ds(1, 1)])
+        xeven, xodd = packed.at[0], packed.at[1]
     sort("gx", xeven, xodd, xlow, xhigh)
     edge_message(with_faces(ends(field), xlow, xhigh), is_even("gy"), out)
 
 
 def odd_edge(field, xeven, xodd):
     face = like(BF16, C, ROW)
-    return call(odd_edge_body, (like(BF16, 5, C, T), face, face), [], 100_000, field, xeven, xodd)
+    scratch = [pltpu.VMEM((2, 8 * C, T), F32), pltpu.VMEM((2, C, ROW), BF16)] if xeven.ndim == 3 else []
+    return call(odd_edge_body, (like(BF16, 5, C, T), face, face), scratch, 100_000, field, xeven, xodd)
 
 
 def even_edge_body(field, xlow, xhigh, out):
@@ -274,7 +275,7 @@
     return call(middle_body, out, scratch, 1_800_000_000, vx, gx, xlow, xhigh, wf, bias)
 
 
-def outer_body(vx, gx, xlow, xhigh, yeven, yodd, wf, bias, total, prod, gedge, keep, give, near, cols, gps, wire):
+def outer_body(vx, gx, xlow, xhigh, yodd, yeven, wf, bias, total, prod, gedge, keep, give, near, cols, gps, wire):
     sort_edges(yeven, yodd, near)
     field = with_faces(whole(vx), xlow, xhigh)
     for x in range(-1, 9):
@@ -308,7 +309,7 @@
             give[...] = wire[HALF - half * HALF : 2 * HALF - half * HALF]
 
 
-def outer(vx, gx, xlow, xhigh, yeven, yodd, wf, bias, total, prod):
+def outer(vx, gx, xlow, xhigh, yodd, yeven, wf, bias, total, prod):
     out = (like(BF16, 8, C, 2 * T), like(F32, HALF, T), like(F32, HALF, T))
     scratch = [
         pltpu.VMEM((10, C, T), F32),
@@ -316,42 +317,65 @@
         pltpu.VMEM((768, 2 * T), BF16),
         pltpu.VMEM((2 * HALF, T), F32),
     ]
-    args = (vx, gx, xlow, xhigh, yeven, yodd, wf, bias, total, prod)
+    args = (vx, gx, xlow, xhigh, yodd, yeven, wf, bias, total, prod)
     return call(outer_body, out, scratch, 700_000_000, *args)
 
 
-def back_body(gmid, gedge, xlow, xhigh, yeven, yodd, wd, data, near, cols, stage, block, sems):
+def products(tiles, wd, cols, stage):
+    for q in range(4):
+        both = jnp.dot(wd[...], cols[q * 192 : q * 192 + 384, :], preferred_element_type=F32)
+        for n, t in enumerate(tiles):
+            out = step_z(both[:, tile(n)])
+            for x in range(2):
+                stage[2 * q + x, pl.ds(t, C, stride=8), :] = out[x * C : x * C + C]
+
+
+def back_middle_body(*refs):
+    gmid, gedge, xlow, xhigh, wd, stage, cols = refs
+    field = with_faces(split(gmid, gedge), xlow, xhigh)
+    for x in range(-1, 9):
+        stack(cols, x + 1, MID, lambda t, x=x: field(x, t))
+    products(MID, wd, cols, stage)
+
+
+def back_middle(gmid, gedge, xlow, xhigh, wd):
+    out = like(F32, 8, 8 * C, T)
+    return call(back_middle_body, out, [pltpu.VMEM((960, 6 * T), BF16)], 800_000_000, gmid, gedge, xlow, xhigh, wd)
+
+
+def back_outer_body(*refs):
+    gmid, gedge, xlow, xhigh, yodd, yeven, wd, mid, data, near, cols, stage, block, sems = refs
     sort_edges(yeven, yodd, near)
     field = with_faces(split(gmid, gedge), xlow, xhigh)
     for x in range(-1, 9):
-        stack(cols, x + 1, range(8), lambda t, x=x: field(x, t), near[x + 1])
+        stack(cols, x + 1, EDGE, lambda t, x=x: field(x, t), near[x + 1])
+    products(EDGE, wd, cols, stage)
+    row = lax.broadcasted_iota(jnp.int32, (8, T), 0)
+    inside = jnp.logical_and(row > 0, row < 7)
     copies = []
-    for q in range(4):
-        both = jnp.dot(wd[...], cols[q * 192 : q * 192 + 384, :], preferred_element_type=F32)
-        for t in range(8):
-            out = step_z(both[:, tile(t)])
-            for x in range(2):
-                stage[2 * q + x, pl.ds(t, C, stride=8), :] = out[x * C : x * C + C]
-        for x in (2 * q, 2 * q + 1):
-            for pair in range(C // 2):
-                even, odd = stage[x, pl.ds(pair * 16, 8), :], stage[x, pl.ds(pair * 16 + 8, 8), :]
-                block[x, :, tile(pair)] = jnp.concatenate(exchange_halves(even, odd), axis=0).astype(BF16)
-        copies.append(pltpu.make_async_copy(block.at[pl.ds(2 * q, 2)], data.at[pl.ds(2 * q, 2)], sems.at[q]))
-        copies[-1].start()
+    for x in range(8):
+        for pair in range(C // 2):
+            at = [pl.ds(pair * 16 + 8 * k, 8) for k in range(2)]
+            even, odd = (jnp.where(inside, mid[x, rows, :], stage[x, rows, :]) for rows in at)
+            block[x, :, tile(pair)] = jnp.concatenate(exchange_halves(even, odd), axis=0).astype(BF16)
+        if x % 2:
+            copies.append(pltpu.make_async_copy(block.at[pl.ds(x - 1, 2)], data.at[pl.ds(x - 1, 2)], sems.at[x // 2]))
+            copies[-1].start()
     for copy in copies:
         copy.wait()
 
 
-def back(gmid, gedge, xlow, xhigh, yeven, yodd, wd):
+def back_outer(gmid, gedge, xlow, xhigh, yodd, yeven, wd, mid):
     scratch = [
         pltpu.VMEM((10, C, T), F32),
-        pltpu.VMEM((960, ROW), BF16),
+        pltpu.VMEM((960, 2 * T), BF16),
         pltpu.VMEM((8, 8 * C, T), F32),
         pltpu.VMEM((8, 16, C * Z), BF16),
         pltpu.SemaphoreType.DMA((4,)),
     ]
     out = like(BF16, 8, 16, C * Z)
-    return call(back_body, out, scratch, 1_000_000_000, gmid, gedge, xlow, xhigh, yeven, yodd, wd, out_specs=HBM)
+    args = (gmid, gedge, xlow, xhigh, yodd, yeven, wd, mid)
+    return call(back_outer_body, out, scratch, 300_000_000, *args, out_specs=HBM)
 
 
 def add_body(a, b, out):
@@ -417,21 +441,25 @@
     wf = band(jnp.transpose(weight, (2, 4, 0, 1, 3)).reshape(3, C, 288))
     wd = band(jnp.transpose(weight[::-1, ::-1, ::-1], (2, 3, 0, 1, 4)).reshape(3, C, 288))
     barrier = lax.optimization_barrier
-    vx, xeven, xodd = pack(volume, True)
-    xodd, bias, cotangent = barrier((xodd, bias, cotangent))
+    up = 7 * (1 - lax.axis_index("gx") % 2)
+    xeven = lax.dynamic_slice_in_dim(volume, up, 1, 0)
+    xodd = lax.dynamic_slice_in_dim(volume, 7 - up, 1, 0)
+    xodd, xeven, bias, cotangent = barrier((xodd, xeven, bias, cotangent))
+    vx = pack(volume)
     offset = jnp.broadcast_to(bias[:, None], (C, T))
     xodd = swap_x(xodd, 1)
     xeven = swap_x(xeven, 0)
-    (gx,) = pack(cotangent, False)
+    gx = pack(cotangent)
     xodd, offset, gx = barrier((xodd, offset, gx))
     yodd, xlow, xhigh = odd_edge(vx, xeven, xodd)
     yodd, xlow, xhigh = barrier((yodd, xlow, xhigh))
     yeven = even_edge(vx, xlow, xhigh)
-    yodd = swap_y(yodd, 1)
     yeven, xlow, xhigh = barrier((yeven, xlow, xhigh))
     yeven = swap_y(yeven, 0)
+    yodd = swap_y(yodd, 1)
     gmid, total, prod = middle(vx, gx, xlow, xhigh, wf, offset)
-    gedge, keep, give = outer(vx, gx, xlow, xhigh, yeven, yodd, wf, offset, total, prod)
+    yodd, total = barrier((yodd, total))
+    gedge, keep, give = outer(vx, gx, xlow, xhigh, yodd, yeven, wf, offset, total, prod)
 
     state = dict(gmid=gmid, gedge=gedge)
 
@@ -440,37 +468,43 @@
         state["xodd"] = swap_x(xodd, 1)
         state["xeven"] = swap_x(xeven, 0)
 
-    def along_y_odd():
-        yodd, state["xlow"], state["xhigh"] = odd_edge(state["gedge"], state.pop("xeven"), state.pop("xodd"))
+    def along_y():
+        yodd, state["xlow"], state["xhigh"] = odd_edge(state["gedge"], state["xeven"], state["xodd"])
+        state["yeven"] = swap_y(even_edge(state["gedge"], state["xlow"], state["xhigh"]), 0)
         state["yodd"] = swap_y(yodd, 1)
 
-    def along_y_even():
-        state["yeven"] = swap_y(even_edge(state["gedge"], state["xlow"], state["xhigh"]), 0)
-
     def data():
-        names = ("gmid", "gedge", "xlow", "xhigh", "yeven", "yodd")
-        state["data"] = back(*(state[name] for name in names), wd)
-
-    def step(sent, move, work, then):
+        args = state["gmid"], state["gedge"], state["xlow"], state["xhigh"]
+        mid, yodd = barrier((back_middle(*args, wd), state["yodd"]))
+        state["data"] = back_outer(*args, yodd, state["yeven"], wd, mid)
+
+    works = [
+        (None, (), None),
+        (along_x, ("gmid",), None),
+        (None, (), None),
+        (along_y, ("gedge", "xeven", "xodd"), None),
+        (data, ("gmid",), "data"),
+    ]
+
+    def step(sent, target):
+        work, tied, then = works.pop(0) if works else (None, None, None)
         if work:
-            sent, given = barrier((sent, dict(state)))
+            sent, given = barrier((sent, {name: state[name] for name in tied}))
             state.update(given)
-        got = move(sent)
+        got = permute(sent, target)
         if work:
             work()
         if then:
             got, state[then] = barrier((got, state[then]))
-        return got
-
-    got = step(give, lambda sent: swap_x(sent, 0), along_x, None)
+        return sent, got
+
+    _, got = step(give, lambda x, y: (x ^ 1, y))
     wire = add(keep, got, BF16)
     steps = [(1 << b, 0) for b in range(1, nx.bit_length() - 1)] + [(0, 1 << b) for b in range(ny.bit_length() - 1)]
-    works = [(None, None), (along_y_odd, None), (along_y_even, None), (data, "data")]
     for n, (dx, dy) in enumerate(steps):
-        work, then = works.pop(0) if works else (None, None)
-        got = step(wire, lambda sent: permute(sent, lambda x, y: (x ^ dx ^ 1, y ^ dy)), work, then)
-        wire = add(wire, got, F32 if n == len(steps) - 1 else BF16)
-    for work, _ in works:
+        sent, got = step(wire, lambda x, y: (x ^ dx ^ 1, y ^ dy))
+        wire = add(sent, got, F32 if n == len(steps) - 1 else BF16)
+    for work, tied, _ in works:
         if work:
             work()
     scale = 1.0 / math.sqrt(8 * nx * 16 * ny * Z)

time: 38.9 us -> 33.9 us (0.87)
  starting transfers between devices: 19.8 us -> 16 us
  waiting for transfers between devices: 7.31 us -> 4.71 us
  local copies, waits for them, and re-layouts: 2.85 us -> 3.72 us
  Pallas kernels: 7.78 us -> 8.24 us
    ppermute x14, starting transfers between devices: 19.8 us -> 16 us  [permute(): return lax.ppermute(array, ('gx', 'gy'), pairs)]
    ppermute x14, waiting for transfers between devices: 7.31 us -> 4.71 us  [permute(): return lax.ppermute(array, ('gx', 'gy'), pairs)]
    dynamic_slice x0 -> x1, local copies, waits for them, and re-layouts: none -> 0.94 us  [shards(): xeven = lax.dynamic_slice_in_dim(volume, up, 1, 0)]
    pallas_call x16 -> x17, Pallas kernels: 7.78 us -> 8.24 us  [call(): pl.pallas_call(body, out_shape=out_shape, in_specs=in_specs or [VMEM] * l...]
  transfers between devices with their start and end apart: 14 -> 14, of which waited for: 5 -> 4; matrix products, arithmetic and copies ran while one was open for 3% -> 3% of each run, Pallas kernels for 12% -> 16%
where the time goes in v3:
time: 33.9 us; the launch traced here: 33.6 us
  starting transfers between devices  16 us (47%)
  Pallas kernels  8.24 us (24%)
  waiting for transfers between devices  4.71 us (14%)
  local copies, waits for them, and re-layouts  3.72 us (11%)
  between operations  0.91 us (3%)
    ppermute x14, starting transfers between devices, permute(): return lax.ppermute(array, ('gx', 'gy'), pairs)  16 us
    pallas_call x17, Pallas kernels, call(): pl.pallas_call(body, out_shape=out_shape, in_specs=in_specs or [VMEM] * l...  8.24 us
    ppermute x14, waiting for transfers between devices, permute(): return lax.ppermute(array, ('gx', 'gy'), pairs)  4.71 us
    unnamed x8, local copies, waits for them, and re-layouts  1.75 us
    dynamic_slice x1, local copies, waits for them, and re-layouts, shards(): xeven = lax.dynamic_slice_in_dim(volume, up, 1, 0)  0.94 us
  transfers between devices with their start and end apart: 14, of which 4 were waited for; matrix products, arithmetic and copies ran while one was open for 3% of the time, Pallas kernels for 16%

profile of v3, /device:TPU:0, one launch (start us, length us, event | category | flops | bytes accessed | tf_op | source)
XLA Modules:
  0.0 33.6 jit_solution(12439449183668999584)
XLA Ops:
  0.6 0.0 copy-start.2
  0.7 0.9 %constant_dynamic-slice_fusion = (bf16[1,16,2048]{2,1,0:T(8,128)(2,1)S(1)}, bf16[1,16,2048]{2,1,0:T(8,128)(2,1)S(1)}) fusion(bf16[8,16,2048]{2,1,0:T(8,128)(2,1)} %array.1, s32[]{:T(128)S(6)} %select_n.15, s32[]{:T(128)S(6)} %select_n.14), kind=kLoop, calls=%fused_computation.7 | loop fusion | bytes 262152 | tf_op jit(solution)/shard_map/dynamic_slice | solution.py:445
  1.6 2.5 %collective-permute-start = (bf16[1,16,2048]{2,1,0:T(8,128)(2,1)S(1)}, bf16[1,16,2048]{2,1,0:T(8,128)(2,1)S(1)}, u32[]{:S(2)}, u32[]{:S(2)}) collective-permute-start(bf16[1,16,2048]{2,1,0:T(8,128)(2,1)S(1)} %get-tuple-element.43), channel_id=1, source_target_pairs={{0,24},{1,25},{2,26},{3,27},{4,28},{5,29},{6,30},{7,31},{8,16},{9,... | collective-permute-start | bytes 196616 | tf_op jit(solution)/shard_map/ppermute | solution.py:416
  4.1 0.7 %collective-permute-start.1 = (bf16[1,16,2048]{2,1,0:T(8,128)(2,1)S(1)}, bf16[1,16,2048]{2,1,0:T(8,128)(2,1)S(1)}, u32[]{:S(2)}, u32[]{:S(2)}) collective-permute-start(bf16[1,16,2048]{2,1,0:T(8,128)(2,1)S(1)} %get-tuple-element.47), channel_id=1, source_target_pairs={{0,8},{1,9},{2,10},{3,11},{4,12},{5,13},{6,14},{7,15},{8,0},{9,1},... | collective-permute-start | bytes 196616 | tf_op jit(solution)/shard_map/ppermute | solution.py:416
  4.8 0.0 copy-done.2
  4.8 0.2 copy.9
  5.0 0.0 copy-start
  5.0 0.2 reshape.25
  5.2 0.1 pad_bitcast_fusion.3
  5.3 0.7 %copy-done = bf16[8,16,2048]{2,1,0:T(8,128)(2,1)S(1)} copy-done((bf16[8,16,2048]{2,1,0:T(8,128)(2,1)S(1)}, bf16[8,16,2048]{2,1,0:T(8,128)(2,1)}, u32[]{:S(2)}) %copy-start) | copy-done | bytes 524312
  6.0 0.0 copy-start.1
  6.0 0.3 shard_map.67.field.vx
  6.3 0.7 %copy-done.1 = bf16[8,16,2048]{2,1,0:T(8,128)(2,1)S(1)} copy-done((bf16[8,16,2048]{2,1,0:T(8,128)(2,1)S(1)}, bf16[8,16,2048]{2,1,0:T(8,128)(2,1)}, u32[]{:S(2)}) %copy-start.1) | copy-done | bytes 524312
  7.0 0.0 copy-start.3
  7.0 0.3 shard_map.68.gx
  7.4 0.0 collective-permute-done.xodd
  7.4 0.3 copy-done.3
  7.7 0.1 broadcast_in_dim.2.bias
  7.8 0.0 collective-permute-done.1.xeven
  7.8 0.2 shard_map.69
  8.0 0.1 shard_map.70
  8.1 0.1 collective-permute-start.2
  8.2 3.0 %collective-permute-start.3 = (bf16[5,32,128]{2,1,0:T(8,128)(2,1)S(1)}, bf16[5,32,128]{2,1,0:T(8,128)(2,1)S(1)}, u32[]{:S(2)}, u32[]{:S(2)}) collective-permute-start(bf16[5,32,128]{2,1,0:T(8,128)(2,1)S(1)} %shard_map.70), channel_id=1, source_target_pairs={{0,1},{1,0},{2,3},{3,2},{4,5},{5,4},{6,7},{7,6},{8,9},{9,8},{10,11... | collective-permute-start | bytes 122888 | tf_op jit(solution)/shard_map/ppermute | solution.py:416
  11.2 2.1 %shard_map.71 = (bf16[8,32,768]{2,1,0:T(8,128)(2,1)S(1)}, f32[64,128]{1,0:T(8,128)S(1)}, f32[384,192]{1,0:T(8,128)S(1)}) custom-call(bf16[8,32,1024]{2,1,0:T(8,128)(2,1)S(1)} %shard_map.67.field.vx, bf16[8,32,1024]{2,1,0:T(8,128)(2,1)S(1)} %shard_map.68.gx, bf16[32,1024]{1,0:T(8,128)(2,1)S(1)} %get-tuple-element.51.xlow, ...), custom_call_target="tpu_custom_call" | custom-call | flops 1800000000 | bytes 2064384 | tf_op jit(solution)/shard_map/pallas_call | solution.py:24
  13.4 0.0 collective-permute-done.2.yodd
  13.4 0.0 collective-permute-done.3.yeven
  13.4 1.4 %shard_map.72 = (bf16[8,32,256]{2,1,0:T(8,128)(2,1)S(1)}, f32[112,128]{1,0:T(8,128)S(1)}, f32[112,128]{1,0:T(8,128)S(1)}) custom-call(bf16[8,32,1024]{2,1,0:T(8,128)(2,1)S(1)} %shard_map.67.field.vx, bf16[8,32,1024]{2,1,0:T(8,128)(2,1)S(1)} %shard_map.68.gx, bf16[32,1024]{1,0:T(8,128)(2,1)S(1)} %get-tuple-element.51.xlow, ...), custom_call_target="tpu_custom_call" | custom-call | flops 700000000 | bytes 1998848 | tf_op jit(solution)/shard_map/pallas_call | solution.py:24
  14.8 0.1 collective-permute-start.4
  14.9 1.2 %collective-permute-done.4.b = f32[112,128]{1,0:T(8,128)S(1)} collective-permute-done((f32[112,128]{1,0:T(8,128)S(1)}, f32[112,128]{1,0:T(8,128)S(1)}, u32[]{:S(2)}, u32[]{:S(2)}) %collective-permute-start.4) | collective-permute-done | bytes 57376 | tf_op jit(solution)/shard_map/ppermute | solution.py:416
  16.2 1.1 %collective-permute-start.5 = (bf16[112,128]{1,0:T(8,128)(2,1)S(1)}, bf16[112,128]{1,0:T(8,128)(2,1)S(1)}, u32[]{:S(2)}, u32[]{:S(2)}) collective-permute-start(bf16[112,128]{1,0:T(8,128)(2,1)S(1)} %shard_map.73.a), channel_id=1, source_target_pairs={{0,24},{1,25},{2,26},{3,27},{4,28},{5,29},{6,30},{7,31},{8,16},{9,... | collective-permute-start | bytes 86024 | tf_op jit(solution)/shard_map/ppermute | solution.py:416
  17.3 0.2 copy.11
  17.5 0.2 reshape.27
  17.7 0.4 %collective-permute-start.7 = (bf16[32,1024]{1,0:T(8,128)(2,1)S(1)}, bf16[32,1024]{1,0:T(8,128)(2,1)S(1)}, u32[]{:S(2)}, u32[]{:S(2)}) collective-permute-start(bf16[32,1024]{1,0:T(8,128)(2,1)S(1)} %get-tuple-element.66), channel_id=1, source_target_pairs={{0,8},{1,9},{2,10},{3,11},{4,12},{5,13},{6,14},{7,15},{8,0},{9,1},... | collective-permute-start | bytes 196616 | tf_op jit(solution)/shard_map/ppermute | solution.py:416
  18.1 0.5 %collective-permute-start.8 = (bf16[32,1024]{1,0:T(8,128)(2,1)S(1)}, bf16[32,1024]{1,0:T(8,128)(2,1)S(1)}, u32[]{:S(2)}, u32[]{:S(2)}) collective-permute-start(bf16[32,1024]{1,0:T(8,128)(2,1)S(1)} %get-tuple-element.67), channel_id=1, source_target_pairs={{0,24},{1,25},{2,26},{3,27},{4,28},{5,29},{6,30},{7,31},{8,16},{9,... | collective-permute-start | bytes 196616 | tf_op jit(solution)/shard_map/ppermute | solution.py:416
  18.6 0.9 %collective-permute-done.5.b = bf16[112,128]{1,0:T(8,128)(2,1)S(1)} collective-permute-done((bf16[112,128]{1,0:T(8,128)(2,1)S(1)}, bf16[112,128]{1,0:T(8,128)(2,1)S(1)}, u32[]{:S(2)}, u32[]{:S(2)}) %collective-permute-start.5) | collective-permute-done | bytes 28704 | tf_op jit(solution)/shard_map/ppermute | solution.py:416
  19.5 1.6 %collective-permute-start.6 = (bf16[112,128]{1,0:T(8,128)(2,1)S(1)}, bf16[112,128]{1,0:T(8,128)(2,1)S(1)}, u32[]{:S(2)}, u32[]{:S(2)}) collective-permute-start(bf16[112,128]{1,0:T(8,128)(2,1)S(1)} %shard_map.74.a), channel_id=1, source_target_pairs={{0,9},{1,8},{2,11},{3,10},{4,13},{5,12},{6,15},{7,14},{8,1},{9,0},... | collective-permute-start | bytes 86024 | tf_op jit(solution)/shard_map/ppermute | solution.py:416
  21.2 0.1 pad_bitcast_fusion.1
  21.3 1.6 %collective-permute-done.6.b = bf16[112,128]{1,0:T(8,128)(2,1)S(1)} collective-permute-done((bf16[112,128]{1,0:T(8,128)(2,1)S(1)}, bf16[112,128]{1,0:T(8,128)(2,1)S(1)}, u32[]{:S(2)}, u32[]{:S(2)}) %collective-permute-start.6) | collective-permute-done | bytes 28704 | tf_op jit(solution)/shard_map/ppermute | solution.py:416
  22.9 0.0 collective-permute-done.7.xeven
  22.9 0.0 collective-permute-done.8.xodd
  22.9 1.5 %collective-permute-start.9 = (bf16[112,128]{1,0:T(8,128)(2,1)S(1)}, bf16[112,128]{1,0:T(8,128)(2,1)S(1)}, u32[]{:S(2)}, u32[]{:S(2)}) collective-permute-start(bf16[112,128]{1,0:T(8,128)(2,1)S(1)} %shard_map.75.a), channel_id=1, source_target_pairs={{0,10},{1,11},{2,8},{3,9},{4,14},{5,15},{6,12},{7,13},{8,2},{9,3},... | collective-permute-start | bytes 86024 | tf_op jit(solution)/shard_map/ppermute | solution.py:416
  24.5 0.1 shard_map.78
  24.7 0.1 shard_map.80
  24.8 1.7 %collective-permute-start.12 = (bf16[5,32,128]{2,1,0:T(8,128)(2,1)S(1)}, bf16[5,32,128]{2,1,0:T(8,128)(2,1)S(1)}, u32[]{:S(2)}, u32[]{:S(2)}) collective-permute-start(bf16[5,32,128]{2,1,0:T(8,128)(2,1)S(1)} %shard_map.80), channel_id=1, source_target_pairs={{0,1},{1,0},{2,3},{3,2},{4,5},{5,4},{6,7},{7,6},{8,9},{9,8},{10,11... | collective-permute-start | bytes 122888 | tf_op jit(solution)/shard_map/ppermute | solution.py:416
  26.5 0.1 collective-permute-start.11
  26.6 0.0 collective-permute-done.9.b
  26.6 2.3 %collective-permute-start.10 = (bf16[112,128]{1,0:T(8,128)(2,1)S(1)}, bf16[112,128]{1,0:T(8,128)(2,1)S(1)}, u32[]{:S(2)}, u32[]{:S(2)}) collective-permute-start(bf16[112,128]{1,0:T(8,128)(2,1)S(1)} %shard_map.77.a), channel_id=1, source_target_pairs={{0,12},{1,13},{2,14},{3,15},{4,8},{5,9},{6,10},{7,11},{8,4},{9,5},... | collective-permute-start | bytes 86024 | tf_op jit(solution)/shard_map/ppermute | solution.py:416
  28.9 0.9 %shard_map.79.refs_7_ = f32[8,256,128]{2,1,0:T(8,128)S(1)} custom-call(bf16[8,32,768]{2,1,0:T(8,128)(2,1)S(1)} %get-tuple-element.70.mid.refs_0_, bf16[8,32,256]{2,1,0:T(8,128)(2,1)S(1)} %get-tuple-element.71.edge.field.refs_1_, bf16[32,1024]{1,0:T(8,128)(2,1)S(1)} %get-tuple-element.74.refs_2_.xlow, bf16[32,1024]{1,0:T(8,128)(2,1)S(1)} %get-tuple-element.75.refs_3_.xhigh, ...), custom_call_target="tpu_custom_call" | custom-call | flops 800000000 | bytes 1851392 | tf_op jit(solution)/shard_map/pallas_call | solution.py:24
  29.8 0.0 collective-permute-done.11.refs_4_
  29.8 0.0 collective-permute-done.12.refs_5_
  29.8 1.6 %shard_map.81 = bf16[8,16,2048]{2,1,0:T(8,128)(2,1)} custom-call(bf16[8,32,768]{2,1,0:T(8,128)(2,1)S(1)} %get-tuple-element.70.mid.refs_0_, bf16[8,32,256]{2,1,0:T(8,128)(2,1)S(1)} %get-tuple-element.71.edge.field.refs_1_, bf16[32,1024]{1,0:T(8,128)(2,1)S(1)} %get-tuple-element.74.refs_2_.xlow, bf16[32,1024]{1,0:T(8,128)(2,1)S(1)} %get-tuple-element.75.refs_3_.xhigh, ...), custom_call_target="tpu_custom_call" | custom-call | flops 300000000 | bytes 2457600 | tf_op jit(solution)/shard_map/pallas_call | solution.py:24
  31.4 0.0 collective-permute-done.10.b
  31.4 0.4 %collective-permute-start.13 = (f32[112,128]{1,0:T(8,128)S(1)}, f32[112,128]{1,0:T(8,128)S(1)}, u32[]{:S(2)}, u32[]{:S(2)}) collective-permute-start(f32[112,128]{1,0:T(8,128)S(1)} %shard_map.82.refs_0_), channel_id=1, source_target_pairs={{0,8},{1,9},{2,10},{3,11},{4,12},{5,13},{6,14},{7,15},{8,0},{9,1},... | collective-permute-start | bytes 172040 | tf_op jit(solution)/shard_map/ppermute | solution.py:416
  31.8 0.9 %collective-permute-done.13.refs_1_ = f32[112,128]{1,0:T(8,128)S(1)} collective-permute-done((f32[112,128]{1,0:T(8,128)S(1)}, f32[112,128]{1,0:T(8,128)S(1)}, u32[]{:S(2)}, u32[]{:S(2)}) %collective-permute-start.13) | collective-permute-done | bytes 57376 | tf_op jit(solution)/shard_map/ppermute | solution.py:416
  32.7 0.9 %shard_map.83 = (f32[27,32,32]{2,1,0:T(8,128)}, f32[1,32]{1,0:T(1,128)}) custom-call(f32[112,128]{1,0:T(8,128)S(1)} %shard_map.82.refs_0_, f32[112,128]{1,0:T(8,128)S(1)} %collective-permute-done.13.refs_1_), custom_call_target="tpu_custom_call" | custom-call | flops 100000 | bytes 225408 | tf_op jit(solution)/shard_map/pallas_call | solution.py:24
  (11 shorter events, 0.2 us)
Async XLA Ops:
  0.6 4.1 %copy-start.2 = (bf16[3,3,3,32,32]{4,3,2,1,0:T(8,128)(2,1)S(1)}, bf16[3,3,3,32,32]{4,3,2,1,0:T(8,128)(2,1)}, u32[]{:S(2)}) copy-start(bf16[3,3,3,32,32]{4,3,2,1,0:T(8,128)(2,1)} %param.6) | copy-start | bytes 165892
  1.6 5.8 %collective-permute-start = (bf16[1,16,2048]{2,1,0:T(8,128)(2,1)S(1)}, bf16[1,16,2048]{2,1,0:T(8,128)(2,1)S(1)}, u32[]{:S(2)}, u32[]{:S(2)}) collective-permute-start(bf16[1,16,2048]{2,1,0:T(8,128)(2,1)S(1)} %get-tuple-element.43), channel_id=1, source_target_pairs={{0,24},{1,25},{2,26},{3,27},{4,28},{5,29},{6,30},{7,31},{8,16},{9,... | collective-permute-start | bytes 196616 | tf_op jit(solution)/shard_map/ppermute | solution.py:416
  4.1 3.7 %collective-permute-start.1 = (bf16[1,16,2048]{2,1,0:T(8,128)(2,1)S(1)}, bf16[1,16,2048]{2,1,0:T(8,128)(2,1)S(1)}, u32[]{:S(2)}, u32[]{:S(2)}) collective-permute-start(bf16[1,16,2048]{2,1,0:T(8,128)(2,1)S(1)} %get-tuple-element.47), channel_id=1, source_target_pairs={{0,8},{1,9},{2,10},{3,11},{4,12},{5,13},{6,14},{7,15},{8,0},{9,1},... | collective-permute-start | bytes 196616 | tf_op jit(solution)/shard_map/ppermute | solution.py:416
  5.0 1.0 %copy-start = (bf16[8,16,2048]{2,1,0:T(8,128)(2,1)S(1)}, bf16[8,16,2048]{2,1,0:T(8,128)(2,1)}, u32[]{:S(2)}) copy-start(bf16[8,16,2048]{2,1,0:T(8,128)(2,1)} %array.1) | copy-start | bytes 1572868
  6.0 1.0 %copy-start.1 = (bf16[8,16,2048]{2,1,0:T(8,128)(2,1)S(1)}, bf16[8,16,2048]{2,1,0:T(8,128)(2,1)}, u32[]{:S(2)}) copy-start(bf16[8,16,2048]{2,1,0:T(8,128)(2,1)} %array.2) | copy-start | bytes 1572868
  7.0 0.7 %copy-start.3 = (f32[32]{0:T(128)S(1)}, f32[32]{0:T(128)}, u32[]{:S(2)}) copy-start(f32[32]{0:T(128)} %param.7) | copy-start | bytes 388
  8.1 5.3 %collective-permute-start.2 = (bf16[5,32,128]{2,1,0:T(8,128)(2,1)S(1)}, bf16[5,32,128]{2,1,0:T(8,128)(2,1)S(1)}, u32[]{:S(2)}, u32[]{:S(2)}) collective-permute-start(bf16[5,32,128]{2,1,0:T(8,128)(2,1)S(1)} %get-tuple-element.53), channel_id=1, source_target_pairs={{0,8},{1,2},{2,1},{3,4},{4,3},{5,6},{6,5},{7,15},{8,0},{9,10},{10,... | collective-permute-start | bytes 122888 | tf_op jit(solution)/shard_map/ppermute | solution.py:416
  8.2 5.2 %collective-permute-start.3 = (bf16[5,32,128]{2,1,0:T(8,128)(2,1)S(1)}, bf16[5,32,128]{2,1,0:T(8,128)(2,1)S(1)}, u32[]{:S(2)}, u32[]{:S(2)}) collective-permute-start(bf16[5,32,128]{2,1,0:T(8,128)(2,1)S(1)} %shard_map.70), channel_id=1, source_target_pairs={{0,1},{1,0},{2,3},{3,2},{4,5},{5,4},{6,7},{7,6},{8,9},{9,8},{10,11... | collective-permute-start | bytes 122888 | tf_op jit(solution)/shard_map/ppermute | solution.py:416
  14.8 1.3 %collective-permute-start.4 = (f32[112,128]{1,0:T(8,128)S(1)}, f32[112,128]{1,0:T(8,128)S(1)}, u32[]{:S(2)}, u32[]{:S(2)}) collective-permute-start(f32[112,128]{1,0:T(8,128)S(1)} %get-tuple-element.61), channel_id=1, source_target_pairs={{0,8},{1,9},{2,10},{3,11},{4,12},{5,13},{6,14},{7,15},{8,0},{9,1},... | collective-permute-start | bytes 172040 | tf_op jit(solution)/shard_map/ppermute | solution.py:416
  16.2 3.4 %collective-permute-start.5 = (bf16[112,128]{1,0:T(8,128)(2,1)S(1)}, bf16[112,128]{1,0:T(8,128)(2,1)S(1)}, u32[]{:S(2)}, u32[]{:S(2)}) collective-permute-start(bf16[112,128]{1,0:T(8,128)(2,1)S(1)} %shard_map.73.a), channel_id=1, source_target_pairs={{0,24},{1,25},{2,26},{3,27},{4,28},{5,29},{6,30},{7,31},{8,16},{9,... | collective-permute-start | bytes 86024 | tf_op jit(solution)/shard_map/ppermute | solution.py:416
  17.7 5.2 %collective-permute-start.7 = (bf16[32,1024]{1,0:T(8,128)(2,1)S(1)}, bf16[32,1024]{1,0:T(8,128)(2,1)S(1)}, u32[]{:S(2)}, u32[]{:S(2)}) collective-permute-start(bf16[32,1024]{1,0:T(8,128)(2,1)S(1)} %get-tuple-element.66), channel_id=1, source_target_pairs={{0,8},{1,9},{2,10},{3,11},{4,12},{5,13},{6,14},{7,15},{8,0},{9,1},... | collective-permute-start | bytes 196616 | tf_op jit(solution)/shard_map/ppermute | solution.py:416
  18.1 4.8 %collective-permute-start.8 = (bf16[32,1024]{1,0:T(8,128)(2,1)S(1)}, bf16[32,1024]{1,0:T(8,128)(2,1)S(1)}, u32[]{:S(2)}, u32[]{:S(2)}) collective-permute-start(bf16[32,1024]{1,0:T(8,128)(2,1)S(1)} %get-tuple-element.67), channel_id=1, source_target_pairs={{0,24},{1,25},{2,26},{3,27},{4,28},{5,29},{6,30},{7,31},{8,16},{9,... | collective-permute-start | bytes 196616 | tf_op jit(solution)/shard_map/ppermute | solution.py:416
  19.5 3.4 %collective-permute-start.6 = (bf16[112,128]{1,0:T(8,128)(2,1)S(1)}, bf16[112,128]{1,0:T(8,128)(2,1)S(1)}, u32[]{:S(2)}, u32[]{:S(2)}) collective-permute-start(bf16[112,128]{1,0:T(8,128)(2,1)S(1)} %shard_map.74.a), channel_id=1, source_target_pairs={{0,9},{1,8},{2,11},{3,10},{4,13},{5,12},{6,15},{7,14},{8,1},{9,0},... | collective-permute-start | bytes 86024 | tf_op jit(solution)/shard_map/ppermute | solution.py:416
  22.9 3.6 %collective-permute-start.9 = (bf16[112,128]{1,0:T(8,128)(2,1)S(1)}, bf16[112,128]{1,0:T(8,128)(2,1)S(1)}, u32[]{:S(2)}, u32[]{:S(2)}) collective-permute-start(bf16[112,128]{1,0:T(8,128)(2,1)S(1)} %shard_map.75.a), channel_id=1, source_target_pairs={{0,10},{1,11},{2,8},{3,9},{4,14},{5,15},{6,12},{7,13},{8,2},{9,3},... | collective-permute-start | bytes 86024 | tf_op jit(solution)/shard_map/ppermute | solution.py:416
  24.8 5.0 %collective-permute-start.12 = (bf16[5,32,128]{2,1,0:T(8,128)(2,1)S(1)}, bf16[5,32,128]{2,1,0:T(8,128)(2,1)S(1)}, u32[]{:S(2)}, u32[]{:S(2)}) collective-permute-start(bf16[5,32,128]{2,1,0:T(8,128)(2,1)S(1)} %shard_map.80), channel_id=1, source_target_pairs={{0,1},{1,0},{2,3},{3,2},{4,5},{5,4},{6,7},{7,6},{8,9},{9,8},{10,11... | collective-permute-start | bytes 122888 | tf_op jit(solution)/shard_map/ppermute | solution.py:416
  26.5 3.3 %collective-permute-start.11 = (bf16[5,32,128]{2,1,0:T(8,128)(2,1)S(1)}, bf16[5,32,128]{2,1,0:T(8,128)(2,1)S(1)}, u32[]{:S(2)}, u32[]{:S(2)}) collective-permute-start(bf16[5,32,128]{2,1,0:T(8,128)(2,1)S(1)} %get-tuple-element.76), channel_id=1, source_target_pairs={{0,8},{1,2},{2,1},{3,4},{4,3},{5,6},{6,5},{7,15},{8,0},{9,10},{10,... | collective-permute-start | bytes 122888 | tf_op jit(solution)/shard_map/ppermute | solution.py:416
  26.6 4.8 %collective-permute-start.10 = (bf16[112,128]{1,0:T(8,128)(2,1)S(1)}, bf16[112,128]{1,0:T(8,128)(2,1)S(1)}, u32[]{:S(2)}, u32[]{:S(2)}) collective-permute-start(bf16[112,128]{1,0:T(8,128)(2,1)S(1)} %shard_map.77.a), channel_id=1, source_target_pairs={{0,12},{1,13},{2,14},{3,15},{4,8},{5,9},{6,10},{7,11},{8,4},{9,5},... | collective-permute-start | bytes 86024 | tf_op jit(solution)/shard_map/ppermute | solution.py:416
  31.4 1.3 %collective-permute-start.13 = (f32[112,128]{1,0:T(8,128)S(1)}, f32[112,128]{1,0:T(8,128)S(1)}, u32[]{:S(2)}, u32[]{:S(2)}) collective-permute-start(f32[112,128]{1,0:T(8,128)S(1)} %shard_map.82.refs_0_), channel_id=1, source_target_pairs={{0,8},{1,9},{2,10},{3,11},{4,12},{5,13},{6,14},{7,15},{8,0},{9,1},... | collective-permute-start | bytes 172040 | tf_op jit(solution)/shard_map/ppermute | solution.py:416

commit v4 on v3

--- a/solution.py
+++ b/solution.py
@@ -23,7 +23,7 @@
     traffic = sum(math.prod(a.shape) * a.dtype.itemsize for a in (*args, *jax.tree.leaves(out_shape)))
     return pl.pallas_call(
         body,
-        out_shape=out_shape,
+        out_shape=jax.tree.map(lambda a: like(a.dtype, *a.shape), out_shape),
         in_specs=in_specs or [VMEM] * len(args),
         out_specs=out_specs or jax.tree.map(lambda _: VMEM, out_shape),
         scratch_shapes=scratch_shapes,
@@ -272,7 +272,7 @@
 def middle(vx, gx, xlow, xhigh, wf, bias):
     out = (like(BF16, 8, C, 6 * T), like(F32, 64, T), like(F32, 384, 192))
     scratch = [pltpu.VMEM((960, 6 * T), BF16), pltpu.VMEM((768, 6 * T), BF16)]
-    return call(middle_body, out, scratch, 1_800_000_000, vx, gx, xlow, xhigh, wf, bias)
+    return call(middle_body, out, scratch, 1_000_000, vx, gx, xlow, xhigh, wf, bias)
 
 
 def outer_body(vx, gx, xlow, xhigh, yodd, yeven, wf, bias, total, prod, gedge, keep, give, near, cols, gps, wire):
@@ -321,69 +321,49 @@
     return call(outer_body, out, scratch, 700_000_000, *args)
 
 
-def products(tiles, wd, cols, stage):
-    for q in range(4):
-        both = jnp.dot(wd[...], cols[q * 192 : q * 192 + 384, :], preferred_element_type=F32)
-        for n, t in enumerate(tiles):
-            out = step_z(both[:, tile(n)])
-            for x in range(2):
-                stage[2 * q + x, pl.ds(t, C, stride=8), :] = out[x * C : x * C + C]
-
-
-def back_middle_body(*refs):
-    gmid, gedge, xlow, xhigh, wd, stage, cols = refs
-    field = with_faces(split(gmid, gedge), xlow, xhigh)
-    for x in range(-1, 9):
-        stack(cols, x + 1, MID, lambda t, x=x: field(x, t))
-    products(MID, wd, cols, stage)
-
-
-def back_middle(gmid, gedge, xlow, xhigh, wd):
-    out = like(F32, 8, 8 * C, T)
-    return call(back_middle_body, out, [pltpu.VMEM((960, 6 * T), BF16)], 800_000_000, gmid, gedge, xlow, xhigh, wd)
-
-
-def back_outer_body(*refs):
-    gmid, gedge, xlow, xhigh, yodd, yeven, wd, mid, data, near, cols, stage, block, sems = refs
+def back_body(gmid, gedge, xlow, xhigh, yodd, yeven, wd, block, near, cols, stage):
     sort_edges(yeven, yodd, near)
     field = with_faces(split(gmid, gedge), xlow, xhigh)
     for x in range(-1, 9):
-        stack(cols, x + 1, EDGE, lambda t, x=x: field(x, t), near[x + 1])
-    products(EDGE, wd, cols, stage)
-    row = lax.broadcasted_iota(jnp.int32, (8, T), 0)
-    inside = jnp.logical_and(row > 0, row < 7)
-    copies = []
-    for x in range(8):
-        for pair in range(C // 2):
-            at = [pl.ds(pair * 16 + 8 * k, 8) for k in range(2)]
-            even, odd = (jnp.where(inside, mid[x, rows, :], stage[x, rows, :]) for rows in at)
-            block[x, :, tile(pair)] = jnp.concatenate(exchange_halves(even, odd), axis=0).astype(BF16)
-        if x % 2:
-            copies.append(pltpu.make_async_copy(block.at[pl.ds(x - 1, 2)], data.at[pl.ds(x - 1, 2)], sems.at[x // 2]))
-            copies[-1].start()
-    for copy in copies:
-        copy.wait()
-
-
-def back_outer(gmid, gedge, xlow, xhigh, yodd, yeven, wd, mid):
+        stack(cols, x + 1, range(8), lambda t, x=x: field(x, t), near[x + 1])
+    for q in range(4):
+        both = jnp.dot(wd[...], cols[q * 192 : q * 192 + 384, :], preferred_element_type=F32)
+        for t in range(8):
+            out = step_z(both[:, tile(t)])
+            for x in range(2):
+                stage[2 * q + x, pl.ds(t, C, stride=8), :] = out[x * C : x * C + C]
+        for x in (2 * q, 2 * q + 1):
+            for pair in range(C // 2):
+                even, odd = stage[x, pl.ds(pair * 16, 8), :], stage[x, pl.ds(pair * 16 + 8, 8), :]
+                block[x, :, tile(pair)] = jnp.concatenate(exchange_halves(even, odd), axis=0).astype(BF16)
+
+
+def back(gmid, gedge, xlow, xhigh, yodd, yeven, wd):
     scratch = [
         pltpu.VMEM((10, C, T), F32),
-        pltpu.VMEM((960, 2 * T), BF16),
+        pltpu.VMEM((960, ROW), BF16),
         pltpu.VMEM((8, 8 * C, T), F32),
-        pltpu.VMEM((8, 16, C * Z), BF16),
-        pltpu.SemaphoreType.DMA((4,)),
     ]
     out = like(BF16, 8, 16, C * Z)
-    args = (gmid, gedge, xlow, xhigh, yodd, yeven, wd, mid)
-    return call(back_outer_body, out, scratch, 300_000_000, *args, out_specs=HBM)
+    return call(back_body, out, scratch, 1_000_000_000, gmid, gedge, xlow, xhigh, yodd, yeven, wd)
+
+
+def flush_body(block, data, sem):
+    copy = pltpu.make_async_copy(block, data, sem)
+    copy.start()
+    copy.wait()
+
+
+def flush(block):
+    return call(flush_body, block, [pltpu.SemaphoreType.DMA], 100_000, block, out_specs=HBM)
 
 
 def add_body(a, b, out):
     out[...] = (a[...].astype(F32) + b[...].astype(F32)).astype(out.dtype)
 
 
-def add(a, b, dtype):
-    return call(add_body, like(dtype, *a.shape), [], 100_000, a, b)
+def add(a, b, dtype, cost=100_000):
+    return call(add_body, like(dtype, *a.shape), [], cost, a, b)
 
 
 def finish_body(scale, own, other, filters, biases):
@@ -444,19 +424,18 @@
     up = 7 * (1 - lax.axis_index("gx") % 2)
     xeven = lax.dynamic_slice_in_dim(volume, up, 1, 0)
     xodd = lax.dynamic_slice_in_dim(volume, 7 - up, 1, 0)
-    xodd, xeven, bias, cotangent = barrier((xodd, xeven, bias, cotangent))
+    xodd, xeven, bias = barrier((xodd, xeven, bias))
     vx = pack(volume)
-    offset = jnp.broadcast_to(bias[:, None], (C, T))
     xodd = swap_x(xodd, 1)
     xeven = swap_x(xeven, 0)
-    gx = pack(cotangent)
-    xodd, offset, gx = barrier((xodd, offset, gx))
     yodd, xlow, xhigh = odd_edge(vx, xeven, xodd)
     yodd, xlow, xhigh = barrier((yodd, xlow, xhigh))
     yeven = even_edge(vx, xlow, xhigh)
-    yeven, xlow, xhigh = barrier((yeven, xlow, xhigh))
+    yeven, xlow, xhigh, cotangent, bias = barrier((yeven, xlow, xhigh, cotangent, bias))
+    offset = jnp.broadcast_to(bias[:, None], (C, T))
     yeven = swap_y(yeven, 0)
     yodd = swap_y(yodd, 1)
+    gx = pack(cotangent)
     gmid, total, prod = middle(vx, gx, xlow, xhigh, wf, offset)
     yodd, total = barrier((yodd, total))
     gedge, keep, give = outer(vx, gx, xlow, xhigh, yodd, yeven, wf, offset, total, prod)
@@ -474,16 +453,19 @@
         state["yodd"] = swap_y(yodd, 1)
 
     def data():
-        args = state["gmid"], state["gedge"], state["xlow"], state["xhigh"]
-        mid, yodd = barrier((back_middle(*args, wd), state["yodd"]))
-        state["data"] = back_outer(*args, yodd, state["yeven"], wd, mid)
+        names = ("gmid", "gedge", "xlow", "xhigh", "yodd", "yeven")
+        state["block"] = back(*(state[name] for name in names), wd)
+
+    def data_out():
+        state["data"] = flush(state["block"])
 
     works = [
         (None, (), None),
         (along_x, ("gmid",), None),
         (None, (), None),
         (along_y, ("gedge", "xeven", "xodd"), None),
-        (data, ("gmid",), "data"),
+        (data, ("gmid",), "block"),
+        (data_out, ("block",), "data"),
     ]
 
     def step(sent, target):
@@ -503,12 +485,13 @@
     steps = [(1 << b, 0) for b in range(1, nx.bit_length() - 1)] + [(0, 1 << b) for b in range(ny.bit_length() - 1)]
     for n, (dx, dy) in enumerate(steps):
         sent, got = step(wire, lambda x, y: (x ^ dx ^ 1, y ^ dy))
-        wire = add(sent, got, F32 if n == len(steps) - 1 else BF16)
+        wire = add(sent, got, F32 if n == len(steps) - 1 else BF16, 10**9 if n == len(steps) - 2 else 100_000)
+    scale = 1.0 / math.sqrt(8 * nx * 16 * ny * Z)
+    sent, got = step(wire, lambda x, y: (x ^ 1, y))
     for work, tied, _ in works:
         if work:
             work()
-    scale = 1.0 / math.sqrt(8 * nx * 16 * ny * Z)
-    filters, biases = finish(wire, swap_x(wire, 0), scale)
+    filters, biases = finish(sent, got, scale)
     return state["data"], filters.reshape(3, 3, 3, C, C), biases.reshape(C)
 
 

time: 33.9 us -> 33.2 us (0.979)
  starting transfers between devices: 16 us -> 14.4 us
  waiting for transfers between devices: 4.71 us -> 5.79 us
    ppermute x14, starting transfers between devices: 16 us -> 14.4 us  [permute(): return lax.ppermute(array, ('gx', 'gy'), pairs)]
    ppermute x14, waiting for transfers between devices: 4.71 us -> 5.79 us  [permute(): return lax.ppermute(array, ('gx', 'gy'), pairs)]
  transfers between devices with their start and end apart: 14 -> 14, of which waited for: 4 -> 6; matrix products, arithmetic and copies ran while one was open for 3% -> 3% of each run, Pallas kernels for 16% -> 16%
where the time goes in v4:
time: 33.2 us; the launch traced here: 33 us
  starting transfers between devices  14.4 us (43%)
  Pallas kernels  7.95 us (24%)
  waiting for transfers between devices  5.79 us (17%)
  local copies, waits for them, and re-layouts  3.91 us (12%)
  between operations  0.89 us (3%)
    ppermute x14, starting transfers between devices, permute(): return lax.ppermute(array, ('gx', 'gy'), pairs)  14.4 us
    pallas_call x17, Pallas kernels, call(): pl.pallas_call(body, out_shape=jax.tree.map(lambda a: like(a.dtype, *a.sh...  7.95 us
    ppermute x14, waiting for transfers between devices, permute(): return lax.ppermute(array, ('gx', 'gy'), pairs)  5.79 us
    unnamed x8, local copies, waits for them, and re-layouts  2 us
    dynamic_slice x1, local copies, waits for them, and re-layouts, shards(): xeven = lax.dynamic_slice_in_dim(volume, up, 1, 0)  0.89 us
  transfers between devices with their start and end apart: 14, of which 6 were waited for; matrix products, arithmetic and copies ran while one was open for 3% of the time, Pallas kernels for 16%

profile of v4, /device:TPU:0, one launch (start us, length us, event | category | flops | bytes accessed | tf_op | source)
XLA Modules:
  0.0 33.0 jit_solution(14032498350509005272)
XLA Ops:
  0.7 0.9 %constant_dynamic-slice_fusion = (bf16[1,16,2048]{2,1,0:T(8,128)(2,1)S(1)}, bf16[1,16,2048]{2,1,0:T(8,128)(2,1)S(1)}) fusion(bf16[8,16,2048]{2,1,0:T(8,128)(2,1)} %array.1, s32[]{:T(128)S(6)} %select_n.15, s32[]{:T(128)S(6)} %select_n.14), kind=kLoop, calls=%fused_computation.7 | loop fusion | bytes 262152 | tf_op jit(solution)/shard_map/dynamic_slice | solution.py:425
  1.5 0.5 %collective-permute-start = (bf16[1,16,2048]{2,1,0:T(8,128)(2,1)S(1)}, bf16[1,16,2048]{2,1,0:T(8,128)(2,1)S(1)}, u32[]{:S(2)}, u32[]{:S(2)}) collective-permute-start(bf16[1,16,2048]{2,1,0:T(8,128)(2,1)S(1)} %get-tuple-element.43), channel_id=1, source_target_pairs={{0,8},{1,9},{2,10},{3,11},{4,12},{5,13},{6,14},{7,15},{8,0},{9,1},... | collective-permute-start | bytes 196616 | tf_op jit(solution)/shard_map/ppermute | solution.py:396
  2.1 2.6 %collective-permute-start.1 = (bf16[1,16,2048]{2,1,0:T(8,128)(2,1)S(1)}, bf16[1,16,2048]{2,1,0:T(8,128)(2,1)S(1)}, u32[]{:S(2)}, u32[]{:S(2)}) collective-permute-start(bf16[1,16,2048]{2,1,0:T(8,128)(2,1)S(1)} %get-tuple-element.44), channel_id=1, source_target_pairs={{0,24},{1,25},{2,26},{3,27},{4,28},{5,29},{6,30},{7,31},{8,16},{9,... | collective-permute-start | bytes 196616 | tf_op jit(solution)/shard_map/ppermute | solution.py:396
  4.7 0.0 copy-start
  4.7 1.0 %copy-done = bf16[8,16,2048]{2,1,0:T(8,128)(2,1)S(1)} copy-done((bf16[8,16,2048]{2,1,0:T(8,128)(2,1)S(1)}, bf16[8,16,2048]{2,1,0:T(8,128)(2,1)}, u32[]{:S(2)}) %copy-start) | copy-done | bytes 524312
  5.7 0.0 copy-start.2
  5.7 0.3 shard_map.67.field.vx
  6.1 0.6 %copy-done.2 = bf16[3,3,3,32,32]{4,3,2,1,0:T(8,128)(2,1)S(1)} copy-done((bf16[3,3,3,32,32]{4,3,2,1,0:T(8,128)(2,1)S(1)}, bf16[3,3,3,32,32]{4,3,2,1,0:T(8,128)(2,1)}, u32[]{:S(2)}) %copy-start.2) | copy-done | bytes 55320
  6.7 0.2 copy.9
  6.9 0.2 reshape.25
  7.1 0.1 pad_bitcast_fusion.3
  7.2 0.0 collective-permute-done.xeven
  7.2 0.0 collective-permute-done.1.xodd
  7.2 0.2 shard_map.68
  7.4 0.0 copy-start.1
  7.5 0.1 shard_map.69
  7.6 0.1 collective-permute-start.2
  7.7 3.0 %collective-permute-start.3 = (bf16[5,32,128]{2,1,0:T(8,128)(2,1)S(1)}, bf16[5,32,128]{2,1,0:T(8,128)(2,1)S(1)}, u32[]{:S(2)}, u32[]{:S(2)}) collective-permute-start(bf16[5,32,128]{2,1,0:T(8,128)(2,1)S(1)} %shard_map.69), channel_id=1, source_target_pairs={{0,1},{1,0},{2,3},{3,2},{4,5},{5,4},{6,7},{7,6},{8,9},{9,8},{10,11... | collective-permute-start | bytes 122888 | tf_op jit(solution)/shard_map/ppermute | solution.py:396
  10.7 0.0 copy-done.1
  10.7 0.0 copy-start.3
  10.7 0.3 shard_map.70.gx
  11.0 0.3 %copy-done.3 = f32[32]{0:T(128)S(1)} copy-done((f32[32]{0:T(128)S(1)}, f32[32]{0:T(128)}, u32[]{:S(2)}) %copy-start.3) | copy-done | bytes 152
  11.4 0.1 broadcast_in_dim.2.bias
  11.5 2.1 %shard_map.71 = (bf16[8,32,768]{2,1,0:T(8,128)(2,1)S(1)}, f32[64,128]{1,0:T(8,128)S(1)}, f32[384,192]{1,0:T(8,128)S(1)}) custom-call(bf16[8,32,1024]{2,1,0:T(8,128)(2,1)S(1)} %shard_map.67.field.vx, bf16[8,32,1024]{2,1,0:T(8,128)(2,1)S(1)} %shard_map.70.gx, bf16[32,1024]{1,0:T(8,128)(2,1)S(1)} %get-tuple-element.49.xlow, ...), custom_call_target="tpu_custom_call" | custom-call | flops 1000000 | bytes 2064384 | tf_op jit(solution)/shard_map/pallas_call | solution.py:24
  13.6 0.0 collective-permute-done.2.yodd
  13.6 0.0 collective-permute-done.3.yeven
  13.6 1.4 %shard_map.72 = (bf16[8,32,256]{2,1,0:T(8,128)(2,1)S(1)}, f32[112,128]{1,0:T(8,128)S(1)}, f32[112,128]{1,0:T(8,128)S(1)}) custom-call(bf16[8,32,1024]{2,1,0:T(8,128)(2,1)S(1)} %shard_map.67.field.vx, bf16[8,32,1024]{2,1,0:T(8,128)(2,1)S(1)} %shard_map.70.gx, bf16[32,1024]{1,0:T(8,128)(2,1)S(1)} %get-tuple-element.49.xlow, ...), custom_call_target="tpu_custom_call" | custom-call | flops 700000000 | bytes 1998848 | tf_op jit(solution)/shard_map/pallas_call | solution.py:24
  15.0 0.1 collective-permute-start.4
  15.1 1.2 %collective-permute-done.4.b = f32[112,128]{1,0:T(8,128)S(1)} collective-permute-done((f32[112,128]{1,0:T(8,128)S(1)}, f32[112,128]{1,0:T(8,128)S(1)}, u32[]{:S(2)}, u32[]{:S(2)}) %collective-permute-start.4) | collective-permute-done | bytes 57376 | tf_op jit(solution)/shard_map/ppermute | solution.py:396
  16.4 1.1 %collective-permute-start.5 = (bf16[112,128]{1,0:T(8,128)(2,1)S(1)}, bf16[112,128]{1,0:T(8,128)(2,1)S(1)}, u32[]{:S(2)}, u32[]{:S(2)}) collective-permute-start(bf16[112,128]{1,0:T(8,128)(2,1)S(1)} %shard_map.73.a), channel_id=1, source_target_pairs={{0,24},{1,25},{2,26},{3,27},{4,28},{5,29},{6,30},{7,31},{8,16},{9,... | collective-permute-start | bytes 86024 | tf_op jit(solution)/shard_map/ppermute | solution.py:396
  17.5 0.2 copy.11
  17.7 0.2 reshape.27
  17.9 0.4 %collective-permute-start.7 = (bf16[32,1024]{1,0:T(8,128)(2,1)S(1)}, bf16[32,1024]{1,0:T(8,128)(2,1)S(1)}, u32[]{:S(2)}, u32[]{:S(2)}) collective-permute-start(bf16[32,1024]{1,0:T(8,128)(2,1)S(1)} %get-tuple-element.64), channel_id=1, source_target_pairs={{0,8},{1,9},{2,10},{3,11},{4,12},{5,13},{6,14},{7,15},{8,0},{9,1},... | collective-permute-start | bytes 196616 | tf_op jit(solution)/shard_map/ppermute | solution.py:396
  18.3 0.5 %collective-permute-start.8 = (bf16[32,1024]{1,0:T(8,128)(2,1)S(1)}, bf16[32,1024]{1,0:T(8,128)(2,1)S(1)}, u32[]{:S(2)}, u32[]{:S(2)}) collective-permute-start(bf16[32,1024]{1,0:T(8,128)(2,1)S(1)} %get-tuple-element.65), channel_id=1, source_target_pairs={{0,24},{1,25},{2,26},{3,27},{4,28},{5,29},{6,30},{7,31},{8,16},{9,... | collective-permute-start | bytes 196616 | tf_op jit(solution)/shard_map/ppermute | solution.py:396
  18.8 0.9 %collective-permute-done.5.b = bf16[112,128]{1,0:T(8,128)(2,1)S(1)} collective-permute-done((bf16[112,128]{1,0:T(8,128)(2,1)S(1)}, bf16[112,128]{1,0:T(8,128)(2,1)S(1)}, u32[]{:S(2)}, u32[]{:S(2)}) %collective-permute-start.5) | collective-permute-done | bytes 28704 | tf_op jit(solution)/shard_map/ppermute | solution.py:396
  19.7 0.9 %collective-permute-start.6 = (bf16[112,128]{1,0:T(8,128)(2,1)S(1)}, bf16[112,128]{1,0:T(8,128)(2,1)S(1)}, u32[]{:S(2)}, u32[]{:S(2)}) collective-permute-start(bf16[112,128]{1,0:T(8,128)(2,1)S(1)} %shard_map.74.a), channel_id=1, source_target_pairs={{0,9},{1,8},{2,11},{3,10},{4,13},{5,12},{6,15},{7,14},{8,1},{9,0},... | collective-permute-start | bytes 86024 | tf_op jit(solution)/shard_map/ppermute | solution.py:396
  20.6 0.1 pad_bitcast_fusion.1
  20.7 2.4 %collective-permute-done.6.b = bf16[112,128]{1,0:T(8,128)(2,1)S(1)} collective-permute-done((bf16[112,128]{1,0:T(8,128)(2,1)S(1)}, bf16[112,128]{1,0:T(8,128)(2,1)S(1)}, u32[]{:S(2)}, u32[]{:S(2)}) %collective-permute-start.6) | collective-permute-done | bytes 28704 | tf_op jit(solution)/shard_map/ppermute | solution.py:396
  23.1 0.0 collective-permute-done.7.xeven
  23.1 0.0 collective-permute-done.8.xodd
  23.1 1.4 %collective-permute-start.9 = (bf16[112,128]{1,0:T(8,128)(2,1)S(1)}, bf16[112,128]{1,0:T(8,128)(2,1)S(1)}, u32[]{:S(2)}, u32[]{:S(2)}) collective-permute-start(bf16[112,128]{1,0:T(8,128)(2,1)S(1)} %shard_map.75.a), channel_id=1, source_target_pairs={{0,10},{1,11},{2,8},{3,9},{4,14},{5,15},{6,12},{7,13},{8,2},{9,3},... | collective-permute-start | bytes 86024 | tf_op jit(solution)/shard_map/ppermute | solution.py:396
  24.6 0.1 shard_map.78
  24.7 0.1 shard_map.79
  24.8 1.1 %collective-permute-start.12 = (bf16[5,32,128]{2,1,0:T(8,128)(2,1)S(1)}, bf16[5,32,128]{2,1,0:T(8,128)(2,1)S(1)}, u32[]{:S(2)}, u32[]{:S(2)}) collective-permute-start(bf16[5,32,128]{2,1,0:T(8,128)(2,1)S(1)} %shard_map.79), channel_id=1, source_target_pairs={{0,1},{1,0},{2,3},{3,2},{4,5},{5,4},{6,7},{7,6},{8,9},{9,8},{10,11... | collective-permute-start | bytes 122888 | tf_op jit(solution)/shard_map/ppermute | solution.py:396
  25.9 0.1 collective-permute-start.11
  26.0 0.5 %collective-permute-done.9.b = bf16[112,128]{1,0:T(8,128)(2,1)S(1)} collective-permute-done((bf16[112,128]{1,0:T(8,128)(2,1)S(1)}, bf16[112,128]{1,0:T(8,128)(2,1)S(1)}, u32[]{:S(2)}, u32[]{:S(2)}) %collective-permute-start.9) | collective-permute-done | bytes 28704 | tf_op jit(solution)/shard_map/ppermute | solution.py:396
  26.5 2.4 %collective-permute-start.10 = (bf16[112,128]{1,0:T(8,128)(2,1)S(1)}, bf16[112,128]{1,0:T(8,128)(2,1)S(1)}, u32[]{:S(2)}, u32[]{:S(2)}) collective-permute-start(bf16[112,128]{1,0:T(8,128)(2,1)S(1)} %shard_map.77.a), channel_id=1, source_target_pairs={{0,12},{1,13},{2,14},{3,15},{4,8},{5,9},{6,10},{7,11},{8,4},{9,5},... | collective-permute-start | bytes 86024 | tf_op jit(solution)/shard_map/ppermute | solution.py:396
  28.9 0.0 collective-permute-done.12.yeven
  28.9 0.0 collective-permute-done.11.yodd
  28.9 1.4 %shard_map.80.block = bf16[8,16,2048]{2,1,0:T(8,128)(2,1)S(1)} custom-call(bf16[8,32,768]{2,1,0:T(8,128)(2,1)S(1)} %get-tuple-element.68.mid.gmid, bf16[8,32,256]{2,1,0:T(8,128)(2,1)S(1)} %get-tuple-element.69.edge.field.gedge, bf16[32,1024]{1,0:T(8,128)(2,1)S(1)} %get-tuple-element.72.xlow, bf16[32,1024]{1,0:T(8,128)(2,1)S(1)} %get-tuple-element.73.xhigh, ...), custom_call_target="tpu_custom_call" | custom-call | flops 1000000000 | bytes 1409024 | tf_op jit(solution)/shard_map/pallas_call | solution.py:24
  30.3 0.4 %collective-permute-done.10.b = bf16[112,128]{1,0:T(8,128)(2,1)S(1)} collective-permute-done((bf16[112,128]{1,0:T(8,128)(2,1)S(1)}, bf16[112,128]{1,0:T(8,128)(2,1)S(1)}, u32[]{:S(2)}, u32[]{:S(2)}) %collective-permute-start.10) | collective-permute-done | bytes 28704 | tf_op jit(solution)/shard_map/ppermute | solution.py:396
  30.8 0.2 collective-permute-start.13
  31.0 0.8 %shard_map.82 = bf16[8,16,2048]{2,1,0:T(8,128)(2,1)} custom-call(bf16[8,16,2048]{2,1,0:T(8,128)(2,1)S(1)} %shard_map.80.block), custom_call_target="tpu_custom_call" | custom-call | flops 100000 | bytes 1048576 | tf_op jit(solution)/shard_map/pallas_call | solution.py:24
  31.8 0.3 collective-permute-done.13.refs_1_
  32.1 0.9 %shard_map.83 = (f32[27,32,32]{2,1,0:T(8,128)}, f32[1,32]{1,0:T(1,128)}) custom-call(f32[112,128]{1,0:T(8,128)S(1)} %shard_map.81.refs_0_, f32[112,128]{1,0:T(8,128)S(1)} %collective-permute-done.13.refs_1_), custom_call_target="tpu_custom_call" | custom-call | flops 100000 | bytes 225408 | tf_op jit(solution)/shard_map/pallas_call | solution.py:24
  (11 shorter events, 0.2 us)
Async XLA Ops:
  1.5 5.6 %collective-permute-start = (bf16[1,16,2048]{2,1,0:T(8,128)(2,1)S(1)}, bf16[1,16,2048]{2,1,0:T(8,128)(2,1)S(1)}, u32[]{:S(2)}, u32[]{:S(2)}) collective-permute-start(bf16[1,16,2048]{2,1,0:T(8,128)(2,1)S(1)} %get-tuple-element.43), channel_id=1, source_target_pairs={{0,8},{1,9},{2,10},{3,11},{4,12},{5,13},{6,14},{7,15},{8,0},{9,1},... | collective-permute-start | bytes 196616 | tf_op jit(solution)/shard_map/ppermute | solution.py:396
  2.1 5.1 %collective-permute-start.1 = (bf16[1,16,2048]{2,1,0:T(8,128)(2,1)S(1)}, bf16[1,16,2048]{2,1,0:T(8,128)(2,1)S(1)}, u32[]{:S(2)}, u32[]{:S(2)}) collective-permute-start(bf16[1,16,2048]{2,1,0:T(8,128)(2,1)S(1)} %get-tuple-element.44), channel_id=1, source_target_pairs={{0,24},{1,25},{2,26},{3,27},{4,28},{5,29},{6,30},{7,31},{8,16},{9,... | collective-permute-start | bytes 196616 | tf_op jit(solution)/shard_map/ppermute | solution.py:396
  4.7 1.0 %copy-start = (bf16[8,16,2048]{2,1,0:T(8,128)(2,1)S(1)}, bf16[8,16,2048]{2,1,0:T(8,128)(2,1)}, u32[]{:S(2)}) copy-start(bf16[8,16,2048]{2,1,0:T(8,128)(2,1)} %array.1) | copy-start | bytes 1572868
  5.7 0.9 %copy-start.2 = (bf16[3,3,3,32,32]{4,3,2,1,0:T(8,128)(2,1)S(1)}, bf16[3,3,3,32,32]{4,3,2,1,0:T(8,128)(2,1)}, u32[]{:S(2)}) copy-start(bf16[3,3,3,32,32]{4,3,2,1,0:T(8,128)(2,1)} %param.6) | copy-start | bytes 165892
  7.4 3.3 %copy-start.1 = (bf16[8,16,2048]{2,1,0:T(8,128)(2,1)S(1)}, bf16[8,16,2048]{2,1,0:T(8,128)(2,1)}, u32[]{:S(2)}) copy-start(bf16[8,16,2048]{2,1,0:T(8,128)(2,1)} %array.2) | copy-start | bytes 1572868
  7.6 6.0 %collective-permute-start.2 = (bf16[5,32,128]{2,1,0:T(8,128)(2,1)S(1)}, bf16[5,32,128]{2,1,0:T(8,128)(2,1)S(1)}, u32[]{:S(2)}, u32[]{:S(2)}) collective-permute-start(bf16[5,32,128]{2,1,0:T(8,128)(2,1)S(1)} %get-tuple-element.51), channel_id=1, source_target_pairs={{0,8},{1,2},{2,1},{3,4},{4,3},{5,6},{6,5},{7,15},{8,0},{9,10},{10,... | collective-permute-start | bytes 122888 | tf_op jit(solution)/shard_map/ppermute | solution.py:396
  7.7 5.9 %collective-permute-start.3 = (bf16[5,32,128]{2,1,0:T(8,128)(2,1)S(1)}, bf16[5,32,128]{2,1,0:T(8,128)(2,1)S(1)}, u32[]{:S(2)}, u32[]{:S(2)}) collective-permute-start(bf16[5,32,128]{2,1,0:T(8,128)(2,1)S(1)} %shard_map.69), channel_id=1, source_target_pairs={{0,1},{1,0},{2,3},{3,2},{4,5},{5,4},{6,7},{7,6},{8,9},{9,8},{10,11... | collective-permute-start | bytes 122888 | tf_op jit(solution)/shard_map/ppermute | solution.py:396
  10.7 0.7 %copy-start.3 = (f32[32]{0:T(128)S(1)}, f32[32]{0:T(128)}, u32[]{:S(2)}) copy-start(f32[32]{0:T(128)} %param.7) | copy-start | bytes 388
  15.0 1.3 %collective-permute-start.4 = (f32[112,128]{1,0:T(8,128)S(1)}, f32[112,128]{1,0:T(8,128)S(1)}, u32[]{:S(2)}, u32[]{:S(2)}) collective-permute-start(f32[112,128]{1,0:T(8,128)S(1)} %get-tuple-element.59), channel_id=1, source_target_pairs={{0,8},{1,9},{2,10},{3,11},{4,12},{5,13},{6,14},{7,15},{8,0},{9,1},... | collective-permute-start | bytes 172040 | tf_op jit(solution)/shard_map/ppermute | solution.py:396
  16.4 3.4 %collective-permute-start.5 = (bf16[112,128]{1,0:T(8,128)(2,1)S(1)}, bf16[112,128]{1,0:T(8,128)(2,1)S(1)}, u32[]{:S(2)}, u32[]{:S(2)}) collective-permute-start(bf16[112,128]{1,0:T(8,128)(2,1)S(1)} %shard_map.73.a), channel_id=1, source_target_pairs={{0,24},{1,25},{2,26},{3,27},{4,28},{5,29},{6,30},{7,31},{8,16},{9,... | collective-permute-start | bytes 86024 | tf_op jit(solution)/shard_map/ppermute | solution.py:396
  17.9 5.2 %collective-permute-start.7 = (bf16[32,1024]{1,0:T(8,128)(2,1)S(1)}, bf16[32,1024]{1,0:T(8,128)(2,1)S(1)}, u32[]{:S(2)}, u32[]{:S(2)}) collective-permute-start(bf16[32,1024]{1,0:T(8,128)(2,1)S(1)} %get-tuple-element.64), channel_id=1, source_target_pairs={{0,8},{1,9},{2,10},{3,11},{4,12},{5,13},{6,14},{7,15},{8,0},{9,1},... | collective-permute-start | bytes 196616 | tf_op jit(solution)/shard_map/ppermute | solution.py:396
  18.3 4.8 %collective-permute-start.8 = (bf16[32,1024]{1,0:T(8,128)(2,1)S(1)}, bf16[32,1024]{1,0:T(8,128)(2,1)S(1)}, u32[]{:S(2)}, u32[]{:S(2)}) collective-permute-start(bf16[32,1024]{1,0:T(8,128)(2,1)S(1)} %get-tuple-element.65), channel_id=1, source_target_pairs={{0,24},{1,25},{2,26},{3,27},{4,28},{5,29},{6,30},{7,31},{8,16},{9,... | collective-permute-start | bytes 196616 | tf_op jit(solution)/shard_map/ppermute | solution.py:396
  19.7 3.4 %collective-permute-start.6 = (bf16[112,128]{1,0:T(8,128)(2,1)S(1)}, bf16[112,128]{1,0:T(8,128)(2,1)S(1)}, u32[]{:S(2)}, u32[]{:S(2)}) collective-permute-start(bf16[112,128]{1,0:T(8,128)(2,1)S(1)} %shard_map.74.a), channel_id=1, source_target_pairs={{0,9},{1,8},{2,11},{3,10},{4,13},{5,12},{6,15},{7,14},{8,1},{9,0},... | collective-permute-start | bytes 86024 | tf_op jit(solution)/shard_map/ppermute | solution.py:396
  23.1 3.4 %collective-permute-start.9 = (bf16[112,128]{1,0:T(8,128)(2,1)S(1)}, bf16[112,128]{1,0:T(8,128)(2,1)S(1)}, u32[]{:S(2)}, u32[]{:S(2)}) collective-permute-start(bf16[112,128]{1,0:T(8,128)(2,1)S(1)} %shard_map.75.a), channel_id=1, source_target_pairs={{0,10},{1,11},{2,8},{3,9},{4,14},{5,15},{6,12},{7,13},{8,2},{9,3},... | collective-permute-start | bytes 86024 | tf_op jit(solution)/shard_map/ppermute | solution.py:396
  24.8 4.1 %collective-permute-start.12 = (bf16[5,32,128]{2,1,0:T(8,128)(2,1)S(1)}, bf16[5,32,128]{2,1,0:T(8,128)(2,1)S(1)}, u32[]{:S(2)}, u32[]{:S(2)}) collective-permute-start(bf16[5,32,128]{2,1,0:T(8,128)(2,1)S(1)} %shard_map.79), channel_id=1, source_target_pairs={{0,1},{1,0},{2,3},{3,2},{4,5},{5,4},{6,7},{7,6},{8,9},{9,8},{10,11... | collective-permute-start | bytes 122888 | tf_op jit(solution)/shard_map/ppermute | solution.py:396
  25.9 3.0 %collective-permute-start.11 = (bf16[5,32,128]{2,1,0:T(8,128)(2,1)S(1)}, bf16[5,32,128]{2,1,0:T(8,128)(2,1)S(1)}, u32[]{:S(2)}, u32[]{:S(2)}) collective-permute-start(bf16[5,32,128]{2,1,0:T(8,128)(2,1)S(1)} %get-tuple-element.74), channel_id=1, source_target_pairs={{0,8},{1,2},{2,1},{3,4},{4,3},{5,6},{6,5},{7,15},{8,0},{9,10},{10,... | collective-permute-start | bytes 122888 | tf_op jit(solution)/shard_map/ppermute | solution.py:396
  26.5 4.3 %collective-permute-start.10 = (bf16[112,128]{1,0:T(8,128)(2,1)S(1)}, bf16[112,128]{1,0:T(8,128)(2,1)S(1)}, u32[]{:S(2)}, u32[]{:S(2)}) collective-permute-start(bf16[112,128]{1,0:T(8,128)(2,1)S(1)} %shard_map.77.a), channel_id=1, source_target_pairs={{0,12},{1,13},{2,14},{3,15},{4,8},{5,9},{6,10},{7,11},{8,4},{9,5},... | collective-permute-start | bytes 86024 | tf_op jit(solution)/shard_map/ppermute | solution.py:396
  30.8 1.3 %collective-permute-start.13 = (f32[112,128]{1,0:T(8,128)S(1)}, f32[112,128]{1,0:T(8,128)S(1)}, u32[]{:S(2)}, u32[]{:S(2)}) collective-permute-start(f32[112,128]{1,0:T(8,128)S(1)} %shard_map.81.refs_0_), channel_id=1, source_target_pairs={{0,8},{1,9},{2,10},{3,11},{4,12},{5,13},{6,14},{7,15},{8,0},{9,1},... | collective-permute-start | bytes 172040 | tf_op jit(solution)/shard_map/ppermute | solution.py:396

commit v5 on v4

--- a/solution.py
+++ b/solution.py
@@ -113,8 +113,11 @@
             out[x, :, tile(t)] = part.astype(BF16)
 
 
-def pack(array):
-    return call(pack_body, like(BF16, 8, C, ROW), [pltpu.VMEM((8, 8 * C, T), F32)], 1_000_000, array)
+def pack(array, *after):
+    def body(array, *refs):
+        pack_body(array, *refs[-2:])
+
+    return call(body, like(BF16, 8, C, ROW), [pltpu.VMEM((8, 8 * C, T), F32)], 1_000_000, array, *after)
 
 
 def whole(ref):
@@ -425,14 +428,14 @@
     xeven = lax.dynamic_slice_in_dim(volume, up, 1, 0)
     xodd = lax.dynamic_slice_in_dim(volume, 7 - up, 1, 0)
     xodd, xeven, bias = barrier((xodd, xeven, bias))
-    vx = pack(volume)
+    offset = jnp.broadcast_to(bias[:, None], (C, T))
+    vx = pack(volume, wf, offset)
     xodd = swap_x(xodd, 1)
     xeven = swap_x(xeven, 0)
     yodd, xlow, xhigh = odd_edge(vx, xeven, xodd)
     yodd, xlow, xhigh = barrier((yodd, xlow, xhigh))
     yeven = even_edge(vx, xlow, xhigh)
-    yeven, xlow, xhigh, cotangent, bias = barrier((yeven, xlow, xhigh, cotangent, bias))
-    offset = jnp.broadcast_to(bias[:, None], (C, T))
+    yeven, xlow, xhigh, cotangent = barrier((yeven, xlow, xhigh, cotangent))
     yeven = swap_y(yeven, 0)
     yodd = swap_y(yodd, 1)
     gx = pack(cotangent)

time: 33.2 us -> 32.7 us (0.985)
  local copies, waits for them, and re-layouts: 3.91 us -> 2.61 us
  starting transfers between devices: 14.4 us -> 15.5 us
    unnamed x8, local copies, waits for them, and re-layouts: 2 us -> 0.64 us
    ppermute x14, starting transfers between devices: 14.4 us -> 15.5 us  [permute(): return lax.ppermute(array, ('gx', 'gy'), pairs)]
  transfers between devices with their start and end apart: 14 -> 14, of which waited for: 6 -> 7; matrix products, arithmetic and copies ran while one was open for 3% -> 3% of each run, Pallas kernels for 16% -> 16%
where the time goes in v5:
time: 32.7 us; the launch traced here: 32.5 us
  starting transfers between devices  15.5 us (47%)
  Pallas kernels  7.96 us (24%)
  waiting for transfers between devices  5.5 us (17%)
  local copies, waits for them, and re-layouts  2.61 us (8%)
  between operations  0.9 us (3%)
    ppermute x14, starting transfers between devices, permute(): return lax.ppermute(array, ('gx', 'gy'), pairs)  15.5 us
    pallas_call x17, Pallas kernels, call(): pl.pallas_call(body, out_shape=jax.tree.map(lambda a: like(a.dtype, *a.sh...  7.96 us
    ppermute x14, waiting for transfers between devices, permute(): return lax.ppermute(array, ('gx', 'gy'), pairs)  5.5 us
    dynamic_slice x1, local copies, waits for them, and re-layouts, shards(): xeven = lax.dynamic_slice_in_dim(volume, up, 1, 0)  0.94 us
  transfers between devices with their start and end apart: 14, of which 7 were waited for; matrix products, arithmetic and copies ran while one was open for 3% of the time, Pallas kernels for 16%

profile of v5, /device:TPU:0, one launch (start us, length us, event | category | flops | bytes accessed | tf_op | source)
XLA Modules:
  0.0 32.5 jit_solution(15414413541224422007)
XLA Ops:
  0.6 0.0 copy-start.2
  0.7 0.9 %constant_dynamic-slice_fusion = (bf16[1,16,2048]{2,1,0:T(8,128)(2,1)S(1)}, bf16[1,16,2048]{2,1,0:T(8,128)(2,1)S(1)}) fusion(bf16[8,16,2048]{2,1,0:T(8,128)(2,1)} %array.1, s32[]{:T(128)S(6)} %select_n.15, s32[]{:T(128)S(6)} %select_n.14), kind=kLoop, calls=%fused_computation.7 | loop fusion | bytes 262152 | tf_op jit(solution)/shard_map/dynamic_slice | solution.py:428
  1.6 0.5 %collective-permute-start = (bf16[1,16,2048]{2,1,0:T(8,128)(2,1)S(1)}, bf16[1,16,2048]{2,1,0:T(8,128)(2,1)S(1)}, u32[]{:S(2)}, u32[]{:S(2)}) collective-permute-start(bf16[1,16,2048]{2,1,0:T(8,128)(2,1)S(1)} %get-tuple-element.43), channel_id=1, source_target_pairs={{0,8},{1,9},{2,10},{3,11},{4,12},{5,13},{6,14},{7,15},{8,0},{9,1},... | collective-permute-start | bytes 196616 | tf_op jit(solution)/shard_map/ppermute | solution.py:399
  2.1 2.6 %collective-permute-start.1 = (bf16[1,16,2048]{2,1,0:T(8,128)(2,1)S(1)}, bf16[1,16,2048]{2,1,0:T(8,128)(2,1)S(1)}, u32[]{:S(2)}, u32[]{:S(2)}) collective-permute-start(bf16[1,16,2048]{2,1,0:T(8,128)(2,1)S(1)} %get-tuple-element.44), channel_id=1, source_target_pairs={{0,24},{1,25},{2,26},{3,27},{4,28},{5,29},{6,30},{7,31},{8,16},{9,... | collective-permute-start | bytes 196616 | tf_op jit(solution)/shard_map/ppermute | solution.py:399
  4.8 0.0 copy-done.2
  4.8 0.2 copy.9
  5.0 0.0 copy-start
  5.0 0.2 reshape.25
  5.2 0.1 pad_bitcast_fusion.3
  5.3 0.0 copy-start.3
  5.3 0.6 %copy-done.3 = f32[32]{0:T(128)S(1)} copy-done((f32[32]{0:T(128)S(1)}, f32[32]{0:T(128)}, u32[]{:S(2)}) %copy-start.3) | copy-done | bytes 152
  6.0 0.1 broadcast_in_dim.2.refs_1_.bias
  6.0 0.0 copy-done
  6.0 0.3 shard_map.67.field.vx
  6.3 0.0 copy-start.1
  6.4 0.0 collective-permute-done.xeven
  6.4 0.8 %collective-permute-done.1.xodd = bf16[1,16,2048]{2,1,0:T(8,128)(2,1)S(1)} collective-permute-done((bf16[1,16,2048]{2,1,0:T(8,128)(2,1)S(1)}, bf16[1,16,2048]{2,1,0:T(8,128)(2,1)S(1)}, u32[]{:S(2)}, u32[]{:S(2)}) %collective-permute-start.1) | collective-permute-done | bytes 65568 | tf_op jit(solution)/shard_map/ppermute | solution.py:399
  7.1 0.2 shard_map.68
  7.4 0.2 collective-permute-start.2
  7.6 0.1 shard_map.69
  7.7 2.9 %collective-permute-start.3 = (bf16[5,32,128]{2,1,0:T(8,128)(2,1)S(1)}, bf16[5,32,128]{2,1,0:T(8,128)(2,1)S(1)}, u32[]{:S(2)}, u32[]{:S(2)}) collective-permute-start(bf16[5,32,128]{2,1,0:T(8,128)(2,1)S(1)} %shard_map.69), channel_id=1, source_target_pairs={{0,1},{1,0},{2,3},{3,2},{4,5},{5,4},{6,7},{7,6},{8,9},{9,8},{10,11... | collective-permute-start | bytes 122888 | tf_op jit(solution)/shard_map/ppermute | solution.py:399
  10.6 0.0 copy-done.1
  10.6 0.3 shard_map.70.gx
  10.9 2.2 %shard_map.71 = (bf16[8,32,768]{2,1,0:T(8,128)(2,1)S(1)}, f32[64,128]{1,0:T(8,128)S(1)}, f32[384,192]{1,0:T(8,128)S(1)}) custom-call(bf16[8,32,1024]{2,1,0:T(8,128)(2,1)S(1)} %shard_map.67.field.vx, bf16[8,32,1024]{2,1,0:T(8,128)(2,1)S(1)} %shard_map.70.gx, bf16[32,1024]{1,0:T(8,128)(2,1)S(1)} %get-tuple-element.48.xlow, ...), custom_call_target="tpu_custom_call" | custom-call | flops 1000000 | bytes 2064384 | tf_op jit(solution)/shard_map/pallas_call | solution.py:24
  13.0 0.0 collective-permute-done.2.yodd
  13.1 0.0 collective-permute-done.3.yeven
  13.1 1.4 %shard_map.72 = (bf16[8,32,256]{2,1,0:T(8,128)(2,1)S(1)}, f32[112,128]{1,0:T(8,128)S(1)}, f32[112,128]{1,0:T(8,128)S(1)}) custom-call(bf16[8,32,1024]{2,1,0:T(8,128)(2,1)S(1)} %shard_map.67.field.vx, bf16[8,32,1024]{2,1,0:T(8,128)(2,1)S(1)} %shard_map.70.gx, bf16[32,1024]{1,0:T(8,128)(2,1)S(1)} %get-tuple-element.48.xlow, ...), custom_call_target="tpu_custom_call" | custom-call | flops 700000000 | bytes 1998848 | tf_op jit(solution)/shard_map/pallas_call | solution.py:24
  14.5 0.1 collective-permute-start.4
  14.6 1.2 %collective-permute-done.4.b = f32[112,128]{1,0:T(8,128)S(1)} collective-permute-done((f32[112,128]{1,0:T(8,128)S(1)}, f32[112,128]{1,0:T(8,128)S(1)}, u32[]{:S(2)}, u32[]{:S(2)}) %collective-permute-start.4) | collective-permute-done | bytes 57376 | tf_op jit(solution)/shard_map/ppermute | solution.py:399
  15.8 1.3 %collective-permute-start.5 = (bf16[112,128]{1,0:T(8,128)(2,1)S(1)}, bf16[112,128]{1,0:T(8,128)(2,1)S(1)}, u32[]{:S(2)}, u32[]{:S(2)}) collective-permute-start(bf16[112,128]{1,0:T(8,128)(2,1)S(1)} %shard_map.73.a), channel_id=1, source_target_pairs={{0,24},{1,25},{2,26},{3,27},{4,28},{5,29},{6,30},{7,31},{8,16},{9,... | collective-permute-start | bytes 86024 | tf_op jit(solution)/shard_map/ppermute | solution.py:399
  17.2 0.2 copy.11
  17.3 0.2 reshape.27
  17.6 0.4 %collective-permute-start.7 = (bf16[32,1024]{1,0:T(8,128)(2,1)S(1)}, bf16[32,1024]{1,0:T(8,128)(2,1)S(1)}, u32[]{:S(2)}, u32[]{:S(2)}) collective-permute-start(bf16[32,1024]{1,0:T(8,128)(2,1)S(1)} %get-tuple-element.62), channel_id=1, source_target_pairs={{0,8},{1,9},{2,10},{3,11},{4,12},{5,13},{6,14},{7,15},{8,0},{9,1},... | collective-permute-start | bytes 196616 | tf_op jit(solution)/shard_map/ppermute | solution.py:399
  18.0 0.3 collective-permute-start.8
  18.3 0.9 %collective-permute-done.5.b = bf16[112,128]{1,0:T(8,128)(2,1)S(1)} collective-permute-done((bf16[112,128]{1,0:T(8,128)(2,1)S(1)}, bf16[112,128]{1,0:T(8,128)(2,1)S(1)}, u32[]{:S(2)}, u32[]{:S(2)}) %collective-permute-start.5) | collective-permute-done | bytes 28704 | tf_op jit(solution)/shard_map/ppermute | solution.py:399
  19.2 1.3 %collective-permute-start.6 = (bf16[112,128]{1,0:T(8,128)(2,1)S(1)}, bf16[112,128]{1,0:T(8,128)(2,1)S(1)}, u32[]{:S(2)}, u32[]{:S(2)}) collective-permute-start(bf16[112,128]{1,0:T(8,128)(2,1)S(1)} %shard_map.74.a), channel_id=1, source_target_pairs={{0,9},{1,8},{2,11},{3,10},{4,13},{5,12},{6,15},{7,14},{8,1},{9,0},... | collective-permute-start | bytes 86024 | tf_op jit(solution)/shard_map/ppermute | solution.py:399
  20.5 0.1 pad_bitcast_fusion.1
  20.6 2.0 %collective-permute-done.6.b = bf16[112,128]{1,0:T(8,128)(2,1)S(1)} collective-permute-done((bf16[112,128]{1,0:T(8,128)(2,1)S(1)}, bf16[112,128]{1,0:T(8,128)(2,1)S(1)}, u32[]{:S(2)}, u32[]{:S(2)}) %collective-permute-start.6) | collective-permute-done | bytes 28704 | tf_op jit(solution)/shard_map/ppermute | solution.py:399
  22.6 0.0 collective-permute-done.7.xeven
  22.6 0.0 collective-permute-done.8.xodd
  22.6 1.4 %collective-permute-start.9 = (bf16[112,128]{1,0:T(8,128)(2,1)S(1)}, bf16[112,128]{1,0:T(8,128)(2,1)S(1)}, u32[]{:S(2)}, u32[]{:S(2)}) collective-permute-start(bf16[112,128]{1,0:T(8,128)(2,1)S(1)} %shard_map.75.a), channel_id=1, source_target_pairs={{0,10},{1,11},{2,8},{3,9},{4,14},{5,15},{6,12},{7,13},{8,2},{9,3},... | collective-permute-start | bytes 86024 | tf_op jit(solution)/shard_map/ppermute | solution.py:399
  24.0 0.1 shard_map.78
  24.2 0.1 shard_map.79
  24.3 1.6 %collective-permute-start.12 = (bf16[5,32,128]{2,1,0:T(8,128)(2,1)S(1)}, bf16[5,32,128]{2,1,0:T(8,128)(2,1)S(1)}, u32[]{:S(2)}, u32[]{:S(2)}) collective-permute-start(bf16[5,32,128]{2,1,0:T(8,128)(2,1)S(1)} %shard_map.79), channel_id=1, source_target_pairs={{0,1},{1,0},{2,3},{3,2},{4,5},{5,4},{6,7},{7,6},{8,9},{9,8},{10,11... | collective-permute-start | bytes 122888 | tf_op jit(solution)/shard_map/ppermute | solution.py:399
  25.8 0.1 collective-permute-start.11
  25.9 0.1 collective-permute-done.9.b
  26.0 2.4 %collective-permute-start.10 = (bf16[112,128]{1,0:T(8,128)(2,1)S(1)}, bf16[112,128]{1,0:T(8,128)(2,1)S(1)}, u32[]{:S(2)}, u32[]{:S(2)}) collective-permute-start(bf16[112,128]{1,0:T(8,128)(2,1)S(1)} %shard_map.77.a), channel_id=1, source_target_pairs={{0,12},{1,13},{2,14},{3,15},{4,8},{5,9},{6,10},{7,11},{8,4},{9,5},... | collective-permute-start | bytes 86024 | tf_op jit(solution)/shard_map/ppermute | solution.py:399
  28.4 0.0 collective-permute-done.12.yeven
  28.4 0.0 collective-permute-done.11.yodd
  28.4 1.4 %shard_map.80.block = bf16[8,16,2048]{2,1,0:T(8,128)(2,1)S(1)} custom-call(bf16[8,32,768]{2,1,0:T(8,128)(2,1)S(1)} %get-tuple-element.66.mid.gmid, bf16[8,32,256]{2,1,0:T(8,128)(2,1)S(1)} %get-tuple-element.67.edge.field.gedge, bf16[32,1024]{1,0:T(8,128)(2,1)S(1)} %get-tuple-element.70.xlow, bf16[32,1024]{1,0:T(8,128)(2,1)S(1)} %get-tuple-element.71.xhigh, ...), custom_call_target="tpu_custom_call" | custom-call | flops 1000000000 | bytes 1409024 | tf_op jit(solution)/shard_map/pallas_call | solution.py:24
  29.8 0.5 %collective-permute-done.10.b = bf16[112,128]{1,0:T(8,128)(2,1)S(1)} collective-permute-done((bf16[112,128]{1,0:T(8,128)(2,1)S(1)}, bf16[112,128]{1,0:T(8,128)(2,1)S(1)}, u32[]{:S(2)}, u32[]{:S(2)}) %collective-permute-start.10) | collective-permute-done | bytes 28704 | tf_op jit(solution)/shard_map/ppermute | solution.py:399
  30.3 0.4 %collective-permute-start.13 = (f32[112,128]{1,0:T(8,128)S(1)}, f32[112,128]{1,0:T(8,128)S(1)}, u32[]{:S(2)}, u32[]{:S(2)}) collective-permute-start(f32[112,128]{1,0:T(8,128)S(1)} %shard_map.81.refs_0_), channel_id=1, source_target_pairs={{0,8},{1,9},{2,10},{3,11},{4,12},{5,13},{6,14},{7,15},{8,0},{9,1},... | collective-permute-start | bytes 172040 | tf_op jit(solution)/shard_map/ppermute | solution.py:399
  30.7 0.8 %shard_map.82 = bf16[8,16,2048]{2,1,0:T(8,128)(2,1)} custom-call(bf16[8,16,2048]{2,1,0:T(8,128)(2,1)S(1)} %shard_map.80.block), custom_call_target="tpu_custom_call" | custom-call | flops 100000 | bytes 1048576 | tf_op jit(solution)/shard_map/pallas_call | solution.py:24
  31.5 0.1 collective-permute-done.13.refs_1_
  31.6 0.9 %shard_map.83 = (f32[27,32,32]{2,1,0:T(8,128)}, f32[1,32]{1,0:T(1,128)}) custom-call(f32[112,128]{1,0:T(8,128)S(1)} %shard_map.81.refs_0_, f32[112,128]{1,0:T(8,128)S(1)} %collective-permute-done.13.refs_1_), custom_call_target="tpu_custom_call" | custom-call | flops 100000 | bytes 225408 | tf_op jit(solution)/shard_map/pallas_call | solution.py:24
  (11 shorter events, 0.2 us)
Async XLA Ops:
  0.6 4.1 %copy-start.2 = (bf16[3,3,3,32,32]{4,3,2,1,0:T(8,128)(2,1)S(1)}, bf16[3,3,3,32,32]{4,3,2,1,0:T(8,128)(2,1)}, u32[]{:S(2)}) copy-start(bf16[3,3,3,32,32]{4,3,2,1,0:T(8,128)(2,1)} %param.6) | copy-start | bytes 165892
  1.6 4.8 %collective-permute-start = (bf16[1,16,2048]{2,1,0:T(8,128)(2,1)S(1)}, bf16[1,16,2048]{2,1,0:T(8,128)(2,1)S(1)}, u32[]{:S(2)}, u32[]{:S(2)}) collective-permute-start(bf16[1,16,2048]{2,1,0:T(8,128)(2,1)S(1)} %get-tuple-element.43), channel_id=1, source_target_pairs={{0,8},{1,9},{2,10},{3,11},{4,12},{5,13},{6,14},{7,15},{8,0},{9,1},... | collective-permute-start | bytes 196616 | tf_op jit(solution)/shard_map/ppermute | solution.py:399
  2.1 5.0 %collective-permute-start.1 = (bf16[1,16,2048]{2,1,0:T(8,128)(2,1)S(1)}, bf16[1,16,2048]{2,1,0:T(8,128)(2,1)S(1)}, u32[]{:S(2)}, u32[]{:S(2)}) collective-permute-start(bf16[1,16,2048]{2,1,0:T(8,128)(2,1)S(1)} %get-tuple-element.44), channel_id=1, source_target_pairs={{0,24},{1,25},{2,26},{3,27},{4,28},{5,29},{6,30},{7,31},{8,16},{9,... | collective-permute-start | bytes 196616 | tf_op jit(solution)/shard_map/ppermute | solution.py:399
  5.0 1.1 %copy-start = (bf16[8,16,2048]{2,1,0:T(8,128)(2,1)S(1)}, bf16[8,16,2048]{2,1,0:T(8,128)(2,1)}, u32[]{:S(2)}) copy-start(bf16[8,16,2048]{2,1,0:T(8,128)(2,1)} %array.1) | copy-start | bytes 1572868
  5.3 0.7 %copy-start.3 = (f32[32]{0:T(128)S(1)}, f32[32]{0:T(128)}, u32[]{:S(2)}) copy-start(f32[32]{0:T(128)} %param.7) | copy-start | bytes 388
  6.3 4.2 %copy-start.1 = (bf16[8,16,2048]{2,1,0:T(8,128)(2,1)S(1)}, bf16[8,16,2048]{2,1,0:T(8,128)(2,1)}, u32[]{:S(2)}) copy-start(bf16[8,16,2048]{2,1,0:T(8,128)(2,1)} %array.2) | copy-start | bytes 1572868
  7.4 5.7 %collective-permute-start.2 = (bf16[5,32,128]{2,1,0:T(8,128)(2,1)S(1)}, bf16[5,32,128]{2,1,0:T(8,128)(2,1)S(1)}, u32[]{:S(2)}, u32[]{:S(2)}) collective-permute-start(bf16[5,32,128]{2,1,0:T(8,128)(2,1)S(1)} %get-tuple-element.50), channel_id=1, source_target_pairs={{0,8},{1,2},{2,1},{3,4},{4,3},{5,6},{6,5},{7,15},{8,0},{9,10},{10,... | collective-permute-start | bytes 122888 | tf_op jit(solution)/shard_map/ppermute | solution.py:399
  7.7 5.4 %collective-permute-start.3 = (bf16[5,32,128]{2,1,0:T(8,128)(2,1)S(1)}, bf16[5,32,128]{2,1,0:T(8,128)(2,1)S(1)}, u32[]{:S(2)}, u32[]{:S(2)}) collective-permute-start(bf16[5,32,128]{2,1,0:T(8,128)(2,1)S(1)} %shard_map.69), channel_id=1, source_target_pairs={{0,1},{1,0},{2,3},{3,2},{4,5},{5,4},{6,7},{7,6},{8,9},{9,8},{10,11... | collective-permute-start | bytes 122888 | tf_op jit(solution)/shard_map/ppermute | solution.py:399
  14.5 1.3 %collective-permute-start.4 = (f32[112,128]{1,0:T(8,128)S(1)}, f32[112,128]{1,0:T(8,128)S(1)}, u32[]{:S(2)}, u32[]{:S(2)}) collective-permute-start(f32[112,128]{1,0:T(8,128)S(1)} %get-tuple-element.57), channel_id=1, source_target_pairs={{0,8},{1,9},{2,10},{3,11},{4,12},{5,13},{6,14},{7,15},{8,0},{9,1},... | collective-permute-start | bytes 172040 | tf_op jit(solution)/shard_map/ppermute | solution.py:399
  15.8 3.4 %collective-permute-start.5 = (bf16[112,128]{1,0:T(8,128)(2,1)S(1)}, bf16[112,128]{1,0:T(8,128)(2,1)S(1)}, u32[]{:S(2)}, u32[]{:S(2)}) collective-permute-start(bf16[112,128]{1,0:T(8,128)(2,1)S(1)} %shard_map.73.a), channel_id=1, source_target_pairs={{0,24},{1,25},{2,26},{3,27},{4,28},{5,29},{6,30},{7,31},{8,16},{9,... | collective-permute-start | bytes 86024 | tf_op jit(solution)/shard_map/ppermute | solution.py:399
  17.6 5.0 %collective-permute-start.7 = (bf16[32,1024]{1,0:T(8,128)(2,1)S(1)}, bf16[32,1024]{1,0:T(8,128)(2,1)S(1)}, u32[]{:S(2)}, u32[]{:S(2)}) collective-permute-start(bf16[32,1024]{1,0:T(8,128)(2,1)S(1)} %get-tuple-element.62), channel_id=1, source_target_pairs={{0,8},{1,9},{2,10},{3,11},{4,12},{5,13},{6,14},{7,15},{8,0},{9,1},... | collective-permute-start | bytes 196616 | tf_op jit(solution)/shard_map/ppermute | solution.py:399
  18.0 4.6 %collective-permute-start.8 = (bf16[32,1024]{1,0:T(8,128)(2,1)S(1)}, bf16[32,1024]{1,0:T(8,128)(2,1)S(1)}, u32[]{:S(2)}, u32[]{:S(2)}) collective-permute-start(bf16[32,1024]{1,0:T(8,128)(2,1)S(1)} %get-tuple-element.63), channel_id=1, source_target_pairs={{0,24},{1,25},{2,26},{3,27},{4,28},{5,29},{6,30},{7,31},{8,16},{9,... | collective-permute-start | bytes 196616 | tf_op jit(solution)/shard_map/ppermute | solution.py:399
  19.2 3.4 %collective-permute-start.6 = (bf16[112,128]{1,0:T(8,128)(2,1)S(1)}, bf16[112,128]{1,0:T(8,128)(2,1)S(1)}, u32[]{:S(2)}, u32[]{:S(2)}) collective-permute-start(bf16[112,128]{1,0:T(8,128)(2,1)S(1)} %shard_map.74.a), channel_id=1, source_target_pairs={{0,9},{1,8},{2,11},{3,10},{4,13},{5,12},{6,15},{7,14},{8,1},{9,0},... | collective-permute-start | bytes 86024 | tf_op jit(solution)/shard_map/ppermute | solution.py:399
  22.6 3.4 %collective-permute-start.9 = (bf16[112,128]{1,0:T(8,128)(2,1)S(1)}, bf16[112,128]{1,0:T(8,128)(2,1)S(1)}, u32[]{:S(2)}, u32[]{:S(2)}) collective-permute-start(bf16[112,128]{1,0:T(8,128)(2,1)S(1)} %shard_map.75.a), channel_id=1, source_target_pairs={{0,10},{1,11},{2,8},{3,9},{4,14},{5,15},{6,12},{7,13},{8,2},{9,3},... | collective-permute-start | bytes 86024 | tf_op jit(solution)/shard_map/ppermute | solution.py:399
  24.3 4.1 %collective-permute-start.12 = (bf16[5,32,128]{2,1,0:T(8,128)(2,1)S(1)}, bf16[5,32,128]{2,1,0:T(8,128)(2,1)S(1)}, u32[]{:S(2)}, u32[]{:S(2)}) collective-permute-start(bf16[5,32,128]{2,1,0:T(8,128)(2,1)S(1)} %shard_map.79), channel_id=1, source_target_pairs={{0,1},{1,0},{2,3},{3,2},{4,5},{5,4},{6,7},{7,6},{8,9},{9,8},{10,11... | collective-permute-start | bytes 122888 | tf_op jit(solution)/shard_map/ppermute | solution.py:399
  25.8 2.6 %collective-permute-start.11 = (bf16[5,32,128]{2,1,0:T(8,128)(2,1)S(1)}, bf16[5,32,128]{2,1,0:T(8,128)(2,1)S(1)}, u32[]{:S(2)}, u32[]{:S(2)}) collective-permute-start(bf16[5,32,128]{2,1,0:T(8,128)(2,1)S(1)} %get-tuple-element.72), channel_id=1, source_target_pairs={{0,8},{1,2},{2,1},{3,4},{4,3},{5,6},{6,5},{7,15},{8,0},{9,10},{10,... | collective-permute-start | bytes 122888 | tf_op jit(solution)/shard_map/ppermute | solution.py:399
  26.0 4.3 %collective-permute-start.10 = (bf16[112,128]{1,0:T(8,128)(2,1)S(1)}, bf16[112,128]{1,0:T(8,128)(2,1)S(1)}, u32[]{:S(2)}, u32[]{:S(2)}) collective-permute-start(bf16[112,128]{1,0:T(8,128)(2,1)S(1)} %shard_map.77.a), channel_id=1, source_target_pairs={{0,12},{1,13},{2,14},{3,15},{4,8},{5,9},{6,10},{7,11},{8,4},{9,5},... | collective-permute-start | bytes 86024 | tf_op jit(solution)/shard_map/ppermute | solution.py:399
  30.3 1.3 %collective-permute-start.13 = (f32[112,128]{1,0:T(8,128)S(1)}, f32[112,128]{1,0:T(8,128)S(1)}, u32[]{:S(2)}, u32[]{:S(2)}) collective-permute-start(f32[112,128]{1,0:T(8,128)S(1)} %shard_map.81.refs_0_), channel_id=1, source_target_pairs={{0,8},{1,9},{2,10},{3,11},{4,12},{5,13},{6,14},{7,15},{8,0},{9,1},... | collective-permute-start | bytes 172040 | tf_op jit(solution)/shard_map/ppermute | solution.py:399

commit v6 on v5

--- a/solution.py
+++ b/solution.py
@@ -11,7 +11,9 @@
 Z = 64
 T = 128
 ROW = 8 * T
-HALF = 112
+HALF = 128
+FIRST = 104
+BIAS = 112
 F32 = jnp.float32
 BF16 = jnp.bfloat16
 VMEM_LIMIT = 48 * 1024 * 1024
@@ -300,10 +302,14 @@
         near2, moved2, far2, plain2 = rows[27 + at]
         last = pltpu.roll((near2, near2, plain2)[dz], (3 * C, C, 3 * C)[dz], 1)
         out = jnp.where(group == 0, near, jnp.where(group == 1, moved, jnp.where(group == 2, far, last)))
-        wire[8 * i : 8 * i + 8] = out
+        at = 8 * i if 8 * i < FIRST else 8 * i - FIRST + HALF
+        wire[at : at + 8] = out
     total = jnp.concatenate([total[:C] + total[C:], jnp.zeros((T - C, T), F32)], axis=0)
     total = jnp.sum(total.T, axis=0, keepdims=True)
-    wire[216:] = jnp.broadcast_to(total, (8, T))
+    total = jnp.where(lax.broadcasted_iota(jnp.int32, (16, T), 0) == 0, total, 0.0)
+    wire[FIRST:BIAS] = jnp.zeros((8, T), F32)
+    wire[BIAS:HALF] = total
+    wire[HALF + BIAS :] = total
     for half in range(2):
 
         @pl.when(my_half() == half)
@@ -362,7 +368,14 @@
 
 
 def add_body(a, b, out):
-    out[...] = (a[...].astype(F32) + b[...].astype(F32)).astype(out.dtype)
+    total = a[...].astype(F32) + b[...].astype(F32)
+    out[:BIAS] = total[:BIAS].astype(out.dtype)
+    last = total[BIAS:]
+    row = lax.broadcasted_iota(jnp.int32, (16, T), 0)
+    both = last + pltpu.roll(last, 15, 0)
+    rounded = both.astype(out.dtype).astype(F32)
+    rest = pltpu.roll(both - rounded, 1, 0)
+    out[BIAS:] = jnp.where(row == 0, rounded, jnp.where(row == 1, rest, 0.0)).astype(out.dtype)
 
 
 def add(a, b, dtype, cost=100_000):
@@ -377,11 +390,12 @@
             for row in range(0, 288, 8):
                 for dz in range(3):
                     at, group = (row, dz) if row < 216 else (row - 216 + 72 * dz, 3)
-                    part = halves_of[at // HALF][at % HALF : at % HALF + 8]
+                    which, at = (0, at) if at < FIRST else (1, at - FIRST)
+                    part = halves_of[which][at : at + 8]
                     moved = part if group == 0 else pltpu.roll(part, T - group * C, 1)
                     block, inside = divmod(row, C)
                     filters[block * 3 + dz, inside : inside + 8, :] = moved[:, :C] * scale
-            biases[...] = halves_of[1][216 - HALF : 217 - HALF, :C] * scale
+            biases[...] = halves_of[0][BIAS : BIAS + 1, :C] * scale
 
 
 def finish(own, other, scale):

time: 32.7 us -> 32.9 us (level)
  no operation moved by 1% of the time
where the time goes in v6:
time: 32.9 us; the launch traced here: 32.7 us
  starting transfers between devices  15.5 us (47%)
  Pallas kernels  8 us (24%)
  waiting for transfers between devices  5.68 us (17%)
  local copies, waits for them, and re-layouts  2.61 us (8%)
  between operations  0.88 us (3%)
    ppermute x14, starting transfers between devices, permute(): return lax.ppermute(array, ('gx', 'gy'), pairs)  15.5 us
    pallas_call x17, Pallas kernels, call(): pl.pallas_call(body, out_shape=jax.tree.map(lambda a: like(a.dtype, *a.sh...  8 us
    ppermute x14, waiting for transfers between devices, permute(): return lax.ppermute(array, ('gx', 'gy'), pairs)  5.68 us
    dynamic_slice x1, local copies, waits for them, and re-layouts, shards(): xeven = lax.dynamic_slice_in_dim(volume, up, 1, 0)  0.94 us
  transfers between devices with their start and end apart: 14, of which 7 were waited for; matrix products, arithmetic and copies ran while one was open for 3% of the time, Pallas kernels for 16%

profile of v6, /device:TPU:0, one launch (start us, length us, event | category | flops | bytes accessed | tf_op | source)
XLA Modules:
  0.0 32.7 jit_solution(8157465504264247989)
XLA Ops:
  0.6 0.0 copy-start.2
  0.7 0.9 %constant_dynamic-slice_fusion = (bf16[1,16,2048]{2,1,0:T(8,128)(2,1)S(1)}, bf16[1,16,2048]{2,1,0:T(8,128)(2,1)S(1)}) fusion(bf16[8,16,2048]{2,1,0:T(8,128)(2,1)} %array.1, s32[]{:T(128)S(6)} %select_n.15, s32[]{:T(128)S(6)} %select_n.14), kind=kLoop, calls=%fused_computation.7 | loop fusion | bytes 262152 | tf_op jit(solution)/shard_map/dynamic_slice | solution.py:442
  1.6 0.5 %collective-permute-start = (bf16[1,16,2048]{2,1,0:T(8,128)(2,1)S(1)}, bf16[1,16,2048]{2,1,0:T(8,128)(2,1)S(1)}, u32[]{:S(2)}, u32[]{:S(2)}) collective-permute-start(bf16[1,16,2048]{2,1,0:T(8,128)(2,1)S(1)} %get-tuple-element.43), channel_id=1, source_target_pairs={{0,8},{1,9},{2,10},{3,11},{4,12},{5,13},{6,14},{7,15},{8,0},{9,1},... | collective-permute-start | bytes 196616 | tf_op jit(solution)/shard_map/ppermute | solution.py:413
  2.1 2.6 %collective-permute-start.1 = (bf16[1,16,2048]{2,1,0:T(8,128)(2,1)S(1)}, bf16[1,16,2048]{2,1,0:T(8,128)(2,1)S(1)}, u32[]{:S(2)}, u32[]{:S(2)}) collective-permute-start(bf16[1,16,2048]{2,1,0:T(8,128)(2,1)S(1)} %get-tuple-element.44), channel_id=1, source_target_pairs={{0,24},{1,25},{2,26},{3,27},{4,28},{5,29},{6,30},{7,31},{8,16},{9,... | collective-permute-start | bytes 196616 | tf_op jit(solution)/shard_map/ppermute | solution.py:413
  4.8 0.0 copy-done.2
  4.8 0.2 copy.9
  5.0 0.0 copy-start
  5.0 0.2 reshape.25
  5.2 0.1 pad_bitcast_fusion.3
  5.3 0.0 copy-start.3
  5.3 0.6 %copy-done.3 = f32[32]{0:T(128)S(1)} copy-done((f32[32]{0:T(128)S(1)}, f32[32]{0:T(128)}, u32[]{:S(2)}) %copy-start.3) | copy-done | bytes 152
  6.0 0.1 broadcast_in_dim.2.refs_1_.bias
  6.0 0.0 copy-done
  6.0 0.3 shard_map.67.field.vx
  6.3 0.0 copy-start.1
  6.4 0.0 collective-permute-done.xeven
  6.4 0.8 %collective-permute-done.1.xodd = bf16[1,16,2048]{2,1,0:T(8,128)(2,1)S(1)} collective-permute-done((bf16[1,16,2048]{2,1,0:T(8,128)(2,1)S(1)}, bf16[1,16,2048]{2,1,0:T(8,128)(2,1)S(1)}, u32[]{:S(2)}, u32[]{:S(2)}) %collective-permute-start.1) | collective-permute-done | bytes 65568 | tf_op jit(solution)/shard_map/ppermute | solution.py:413
  7.1 0.2 shard_map.68
  7.4 0.2 collective-permute-start.2
  7.6 0.1 shard_map.69
  7.7 2.9 %collective-permute-start.3 = (bf16[5,32,128]{2,1,0:T(8,128)(2,1)S(1)}, bf16[5,32,128]{2,1,0:T(8,128)(2,1)S(1)}, u32[]{:S(2)}, u32[]{:S(2)}) collective-permute-start(bf16[5,32,128]{2,1,0:T(8,128)(2,1)S(1)} %shard_map.69), channel_id=1, source_target_pairs={{0,1},{1,0},{2,3},{3,2},{4,5},{5,4},{6,7},{7,6},{8,9},{9,8},{10,11... | collective-permute-start | bytes 122888 | tf_op jit(solution)/shard_map/ppermute | solution.py:413
  10.6 0.0 copy-done.1
  10.6 0.3 shard_map.70.gx
  10.9 2.2 %shard_map.71 = (bf16[8,32,768]{2,1,0:T(8,128)(2,1)S(1)}, f32[64,128]{1,0:T(8,128)S(1)}, f32[384,192]{1,0:T(8,128)S(1)}) custom-call(bf16[8,32,1024]{2,1,0:T(8,128)(2,1)S(1)} %shard_map.67.field.vx, bf16[8,32,1024]{2,1,0:T(8,128)(2,1)S(1)} %shard_map.70.gx, bf16[32,1024]{1,0:T(8,128)(2,1)S(1)} %get-tuple-element.48.xlow, ...), custom_call_target="tpu_custom_call" | custom-call | flops 1000000 | bytes 2064384 | tf_op jit(solution)/shard_map/pallas_call | solution.py:26
  13.0 0.0 collective-permute-done.2.yodd
  13.1 0.0 collective-permute-done.3.yeven
  13.1 1.4 %shard_map.72 = (bf16[8,32,256]{2,1,0:T(8,128)(2,1)S(1)}, f32[128,128]{1,0:T(8,128)S(1)}, f32[128,128]{1,0:T(8,128)S(1)}) custom-call(bf16[8,32,1024]{2,1,0:T(8,128)(2,1)S(1)} %shard_map.67.field.vx, bf16[8,32,1024]{2,1,0:T(8,128)(2,1)S(1)} %shard_map.70.gx, bf16[32,1024]{1,0:T(8,128)(2,1)S(1)} %get-tuple-element.48.xlow, ...), custom_call_target="tpu_custom_call" | custom-call | flops 700000000 | bytes 2015232 | tf_op jit(solution)/shard_map/pallas_call | solution.py:26
  14.5 0.1 collective-permute-start.4
  14.6 1.2 %collective-permute-done.4.b = f32[128,128]{1,0:T(8,128)S(1)} collective-permute-done((f32[128,128]{1,0:T(8,128)S(1)}, f32[128,128]{1,0:T(8,128)S(1)}, u32[]{:S(2)}, u32[]{:S(2)}) %collective-permute-start.4) | collective-permute-done | bytes 65568 | tf_op jit(solution)/shard_map/ppermute | solution.py:413
  15.8 1.3 %collective-permute-start.5 = (bf16[128,128]{1,0:T(8,128)(2,1)S(1)}, bf16[128,128]{1,0:T(8,128)(2,1)S(1)}, u32[]{:S(2)}, u32[]{:S(2)}) collective-permute-start(bf16[128,128]{1,0:T(8,128)(2,1)S(1)} %shard_map.73.a), channel_id=1, source_target_pairs={{0,24},{1,25},{2,26},{3,27},{4,28},{5,29},{6,30},{7,31},{8,16},{9,... | collective-permute-start | bytes 98312 | tf_op jit(solution)/shard_map/ppermute | solution.py:413
  17.2 0.2 copy.11
  17.4 0.2 reshape.27
  17.6 0.4 %collective-permute-start.7 = (bf16[32,1024]{1,0:T(8,128)(2,1)S(1)}, bf16[32,1024]{1,0:T(8,128)(2,1)S(1)}, u32[]{:S(2)}, u32[]{:S(2)}) collective-permute-start(bf16[32,1024]{1,0:T(8,128)(2,1)S(1)} %get-tuple-element.62), channel_id=1, source_target_pairs={{0,8},{1,9},{2,10},{3,11},{4,12},{5,13},{6,14},{7,15},{8,0},{9,1},... | collective-permute-start | bytes 196616 | tf_op jit(solution)/shard_map/ppermute | solution.py:413
  18.0 0.3 collective-permute-start.8
  18.3 1.0 %collective-permute-done.5.b = bf16[128,128]{1,0:T(8,128)(2,1)S(1)} collective-permute-done((bf16[128,128]{1,0:T(8,128)(2,1)S(1)}, bf16[128,128]{1,0:T(8,128)(2,1)S(1)}, u32[]{:S(2)}, u32[]{:S(2)}) %collective-permute-start.5) | collective-permute-done | bytes 32800 | tf_op jit(solution)/shard_map/ppermute | solution.py:413
  19.3 1.3 %collective-permute-start.6 = (bf16[128,128]{1,0:T(8,128)(2,1)S(1)}, bf16[128,128]{1,0:T(8,128)(2,1)S(1)}, u32[]{:S(2)}, u32[]{:S(2)}) collective-permute-start(bf16[128,128]{1,0:T(8,128)(2,1)S(1)} %shard_map.74.a), channel_id=1, source_target_pairs={{0,9},{1,8},{2,11},{3,10},{4,13},{5,12},{6,15},{7,14},{8,1},{9,0},... | collective-permute-start | bytes 98312 | tf_op jit(solution)/shard_map/ppermute | solution.py:413
  20.6 0.1 pad_bitcast_fusion.1
  20.7 2.0 %collective-permute-done.6.b = bf16[128,128]{1,0:T(8,128)(2,1)S(1)} collective-permute-done((bf16[128,128]{1,0:T(8,128)(2,1)S(1)}, bf16[128,128]{1,0:T(8,128)(2,1)S(1)}, u32[]{:S(2)}, u32[]{:S(2)}) %collective-permute-start.6) | collective-permute-done | bytes 32800 | tf_op jit(solution)/shard_map/ppermute | solution.py:413
  22.7 0.0 collective-permute-done.7.xeven
  22.7 0.0 collective-permute-done.8.xodd
  22.7 1.4 %collective-permute-start.9 = (bf16[128,128]{1,0:T(8,128)(2,1)S(1)}, bf16[128,128]{1,0:T(8,128)(2,1)S(1)}, u32[]{:S(2)}, u32[]{:S(2)}) collective-permute-start(bf16[128,128]{1,0:T(8,128)(2,1)S(1)} %shard_map.75.a), channel_id=1, source_target_pairs={{0,10},{1,11},{2,8},{3,9},{4,14},{5,15},{6,12},{7,13},{8,2},{9,3},... | collective-permute-start | bytes 98312 | tf_op jit(solution)/shard_map/ppermute | solution.py:413
  24.2 0.1 shard_map.78
  24.3 0.1 shard_map.79
  24.4 1.6 %collective-permute-start.12 = (bf16[5,32,128]{2,1,0:T(8,128)(2,1)S(1)}, bf16[5,32,128]{2,1,0:T(8,128)(2,1)S(1)}, u32[]{:S(2)}, u32[]{:S(2)}) collective-permute-start(bf16[5,32,128]{2,1,0:T(8,128)(2,1)S(1)} %shard_map.79), channel_id=1, source_target_pairs={{0,1},{1,0},{2,3},{3,2},{4,5},{5,4},{6,7},{7,6},{8,9},{9,8},{10,11... | collective-permute-start | bytes 122888 | tf_op jit(solution)/shard_map/ppermute | solution.py:413
  26.0 0.1 collective-permute-start.11
  26.0 0.1 collective-permute-done.9.b
  26.1 2.4 %collective-permute-start.10 = (bf16[128,128]{1,0:T(8,128)(2,1)S(1)}, bf16[128,128]{1,0:T(8,128)(2,1)S(1)}, u32[]{:S(2)}, u32[]{:S(2)}) collective-permute-start(bf16[128,128]{1,0:T(8,128)(2,1)S(1)} %shard_map.77.a), channel_id=1, source_target_pairs={{0,12},{1,13},{2,14},{3,15},{4,8},{5,9},{6,10},{7,11},{8,4},{9,5},... | collective-permute-start | bytes 98312 | tf_op jit(solution)/shard_map/ppermute | solution.py:413
  28.6 0.0 collective-permute-done.12.yeven
  28.6 0.0 collective-permute-done.11.yodd
  28.6 1.4 %shard_map.80.block = bf16[8,16,2048]{2,1,0:T(8,128)(2,1)S(1)} custom-call(bf16[8,32,768]{2,1,0:T(8,128)(2,1)S(1)} %get-tuple-element.66.mid.gmid, bf16[8,32,256]{2,1,0:T(8,128)(2,1)S(1)} %get-tuple-element.67.edge.field.gedge, bf16[32,1024]{1,0:T(8,128)(2,1)S(1)} %get-tuple-element.70.xlow, bf16[32,1024]{1,0:T(8,128)(2,1)S(1)} %get-tuple-element.71.xhigh, ...), custom_call_target="tpu_custom_call" | custom-call | flops 1000000000 | bytes 1409024 | tf_op jit(solution)/shard_map/pallas_call | solution.py:26
  30.0 0.5 %collective-permute-done.10.b = bf16[128,128]{1,0:T(8,128)(2,1)S(1)} collective-permute-done((bf16[128,128]{1,0:T(8,128)(2,1)S(1)}, bf16[128,128]{1,0:T(8,128)(2,1)S(1)}, u32[]{:S(2)}, u32[]{:S(2)}) %collective-permute-start.10) | collective-permute-done | bytes 32800 | tf_op jit(solution)/shard_map/ppermute | solution.py:413
  30.5 0.4 %collective-permute-start.13 = (f32[128,128]{1,0:T(8,128)S(1)}, f32[128,128]{1,0:T(8,128)S(1)}, u32[]{:S(2)}, u32[]{:S(2)}) collective-permute-start(f32[128,128]{1,0:T(8,128)S(1)} %shard_map.81.refs_0_), channel_id=1, source_target_pairs={{0,8},{1,9},{2,10},{3,11},{4,12},{5,13},{6,14},{7,15},{8,0},{9,1},... | collective-permute-start | bytes 196616 | tf_op jit(solution)/shard_map/ppermute | solution.py:413
  30.9 0.8 %shard_map.82 = bf16[8,16,2048]{2,1,0:T(8,128)(2,1)} custom-call(bf16[8,16,2048]{2,1,0:T(8,128)(2,1)S(1)} %shard_map.80.block), custom_call_target="tpu_custom_call" | custom-call | flops 100000 | bytes 1048576 | tf_op jit(solution)/shard_map/pallas_call | solution.py:26
  31.7 0.1 collective-permute-done.13.refs_1_
  31.8 0.9 %shard_map.83 = (f32[27,32,32]{2,1,0:T(8,128)}, f32[1,32]{1,0:T(1,128)}) custom-call(f32[128,128]{1,0:T(8,128)S(1)} %shard_map.81.refs_0_, f32[128,128]{1,0:T(8,128)S(1)} %collective-permute-done.13.refs_1_), custom_call_target="tpu_custom_call" | custom-call | flops 100000 | bytes 241792 | tf_op jit(solution)/shard_map/pallas_call | solution.py:26
  (11 shorter events, 0.2 us)
Async XLA Ops:
  0.6 4.1 %copy-start.2 = (bf16[3,3,3,32,32]{4,3,2,1,0:T(8,128)(2,1)S(1)}, bf16[3,3,3,32,32]{4,3,2,1,0:T(8,128)(2,1)}, u32[]{:S(2)}) copy-start(bf16[3,3,3,32,32]{4,3,2,1,0:T(8,128)(2,1)} %param.6) | copy-start | bytes 165892
  1.6 4.8 %collective-permute-start = (bf16[1,16,2048]{2,1,0:T(8,128)(2,1)S(1)}, bf16[1,16,2048]{2,1,0:T(8,128)(2,1)S(1)}, u32[]{:S(2)}, u32[]{:S(2)}) collective-permute-start(bf16[1,16,2048]{2,1,0:T(8,128)(2,1)S(1)} %get-tuple-element.43), channel_id=1, source_target_pairs={{0,8},{1,9},{2,10},{3,11},{4,12},{5,13},{6,14},{7,15},{8,0},{9,1},... | collective-permute-start | bytes 196616 | tf_op jit(solution)/shard_map/ppermute | solution.py:413
  2.1 5.0 %collective-permute-start.1 = (bf16[1,16,2048]{2,1,0:T(8,128)(2,1)S(1)}, bf16[1,16,2048]{2,1,0:T(8,128)(2,1)S(1)}, u32[]{:S(2)}, u32[]{:S(2)}) collective-permute-start(bf16[1,16,2048]{2,1,0:T(8,128)(2,1)S(1)} %get-tuple-element.44), channel_id=1, source_target_pairs={{0,24},{1,25},{2,26},{3,27},{4,28},{5,29},{6,30},{7,31},{8,16},{9,... | collective-permute-start | bytes 196616 | tf_op jit(solution)/shard_map/ppermute | solution.py:413
  5.0 1.1 %copy-start = (bf16[8,16,2048]{2,1,0:T(8,128)(2,1)S(1)}, bf16[8,16,2048]{2,1,0:T(8,128)(2,1)}, u32[]{:S(2)}) copy-start(bf16[8,16,2048]{2,1,0:T(8,128)(2,1)} %array.1) | copy-start | bytes 1572868
  5.3 0.7 %copy-start.3 = (f32[32]{0:T(128)S(1)}, f32[32]{0:T(128)}, u32[]{:S(2)}) copy-start(f32[32]{0:T(128)} %param.7) | copy-start | bytes 388
  6.3 4.2 %copy-start.1 = (bf16[8,16,2048]{2,1,0:T(8,128)(2,1)S(1)}, bf16[8,16,2048]{2,1,0:T(8,128)(2,1)}, u32[]{:S(2)}) copy-start(bf16[8,16,2048]{2,1,0:T(8,128)(2,1)} %array.2) | copy-start | bytes 1572868
  7.4 5.7 %collective-permute-start.2 = (bf16[5,32,128]{2,1,0:T(8,128)(2,1)S(1)}, bf16[5,32,128]{2,1,0:T(8,128)(2,1)S(1)}, u32[]{:S(2)}, u32[]{:S(2)}) collective-permute-start(bf16[5,32,128]{2,1,0:T(8,128)(2,1)S(1)} %get-tuple-element.50), channel_id=1, source_target_pairs={{0,8},{1,2},{2,1},{3,4},{4,3},{5,6},{6,5},{7,15},{8,0},{9,10},{10,... | collective-permute-start | bytes 122888 | tf_op jit(solution)/shard_map/ppermute | solution.py:413
  7.7 5.4 %collective-permute-start.3 = (bf16[5,32,128]{2,1,0:T(8,128)(2,1)S(1)}, bf16[5,32,128]{2,1,0:T(8,128)(2,1)S(1)}, u32[]{:S(2)}, u32[]{:S(2)}) collective-permute-start(bf16[5,32,128]{2,1,0:T(8,128)(2,1)S(1)} %shard_map.69), channel_id=1, source_target_pairs={{0,1},{1,0},{2,3},{3,2},{4,5},{5,4},{6,7},{7,6},{8,9},{9,8},{10,11... | collective-permute-start | bytes 122888 | tf_op jit(solution)/shard_map/ppermute | solution.py:413
  14.5 1.3 %collective-permute-start.4 = (f32[128,128]{1,0:T(8,128)S(1)}, f32[128,128]{1,0:T(8,128)S(1)}, u32[]{:S(2)}, u32[]{:S(2)}) collective-permute-start(f32[128,128]{1,0:T(8,128)S(1)} %get-tuple-element.57), channel_id=1, source_target_pairs={{0,8},{1,9},{2,10},{3,11},{4,12},{5,13},{6,14},{7,15},{8,0},{9,1},... | collective-permute-start | bytes 196616 | tf_op jit(solution)/shard_map/ppermute | solution.py:413
  15.8 3.4 %collective-permute-start.5 = (bf16[128,128]{1,0:T(8,128)(2,1)S(1)}, bf16[128,128]{1,0:T(8,128)(2,1)S(1)}, u32[]{:S(2)}, u32[]{:S(2)}) collective-permute-start(bf16[128,128]{1,0:T(8,128)(2,1)S(1)} %shard_map.73.a), channel_id=1, source_target_pairs={{0,24},{1,25},{2,26},{3,27},{4,28},{5,29},{6,30},{7,31},{8,16},{9,... | collective-permute-start | bytes 98312 | tf_op jit(solution)/shard_map/ppermute | solution.py:413
  17.6 5.1 %collective-permute-start.7 = (bf16[32,1024]{1,0:T(8,128)(2,1)S(1)}, bf16[32,1024]{1,0:T(8,128)(2,1)S(1)}, u32[]{:S(2)}, u32[]{:S(2)}) collective-permute-start(bf16[32,1024]{1,0:T(8,128)(2,1)S(1)} %get-tuple-element.62), channel_id=1, source_target_pairs={{0,8},{1,9},{2,10},{3,11},{4,12},{5,13},{6,14},{7,15},{8,0},{9,1},... | collective-permute-start | bytes 196616 | tf_op jit(solution)/shard_map/ppermute | solution.py:413
  18.0 4.7 %collective-permute-start.8 = (bf16[32,1024]{1,0:T(8,128)(2,1)S(1)}, bf16[32,1024]{1,0:T(8,128)(2,1)S(1)}, u32[]{:S(2)}, u32[]{:S(2)}) collective-permute-start(bf16[32,1024]{1,0:T(8,128)(2,1)S(1)} %get-tuple-element.63), channel_id=1, source_target_pairs={{0,24},{1,25},{2,26},{3,27},{4,28},{5,29},{6,30},{7,31},{8,16},{9,... | collective-permute-start | bytes 196616 | tf_op jit(solution)/shard_map/ppermute | solution.py:413
  19.3 3.4 %collective-permute-start.6 = (bf16[128,128]{1,0:T(8,128)(2,1)S(1)}, bf16[128,128]{1,0:T(8,128)(2,1)S(1)}, u32[]{:S(2)}, u32[]{:S(2)}) collective-permute-start(bf16[128,128]{1,0:T(8,128)(2,1)S(1)} %shard_map.74.a), channel_id=1, source_target_pairs={{0,9},{1,8},{2,11},{3,10},{4,13},{5,12},{6,15},{7,14},{8,1},{9,0},... | collective-permute-start | bytes 98312 | tf_op jit(solution)/shard_map/ppermute | solution.py:413
  22.7 3.4 %collective-permute-start.9 = (bf16[128,128]{1,0:T(8,128)(2,1)S(1)}, bf16[128,128]{1,0:T(8,128)(2,1)S(1)}, u32[]{:S(2)}, u32[]{:S(2)}) collective-permute-start(bf16[128,128]{1,0:T(8,128)(2,1)S(1)} %shard_map.75.a), channel_id=1, source_target_pairs={{0,10},{1,11},{2,8},{3,9},{4,14},{5,15},{6,12},{7,13},{8,2},{9,3},... | collective-permute-start | bytes 98312 | tf_op jit(solution)/shard_map/ppermute | solution.py:413
  24.4 4.2 %collective-permute-start.12 = (bf16[5,32,128]{2,1,0:T(8,128)(2,1)S(1)}, bf16[5,32,128]{2,1,0:T(8,128)(2,1)S(1)}, u32[]{:S(2)}, u32[]{:S(2)}) collective-permute-start(bf16[5,32,128]{2,1,0:T(8,128)(2,1)S(1)} %shard_map.79), channel_id=1, source_target_pairs={{0,1},{1,0},{2,3},{3,2},{4,5},{5,4},{6,7},{7,6},{8,9},{9,8},{10,11... | collective-permute-start | bytes 122888 | tf_op jit(solution)/shard_map/ppermute | solution.py:413
  26.0 2.6 %collective-permute-start.11 = (bf16[5,32,128]{2,1,0:T(8,128)(2,1)S(1)}, bf16[5,32,128]{2,1,0:T(8,128)(2,1)S(1)}, u32[]{:S(2)}, u32[]{:S(2)}) collective-permute-start(bf16[5,32,128]{2,1,0:T(8,128)(2,1)S(1)} %get-tuple-element.72), channel_id=1, source_target_pairs={{0,8},{1,2},{2,1},{3,4},{4,3},{5,6},{6,5},{7,15},{8,0},{9,10},{10,... | collective-permute-start | bytes 122888 | tf_op jit(solution)/shard_map/ppermute | solution.py:413
  26.1 4.3 %collective-permute-start.10 = (bf16[128,128]{1,0:T(8,128)(2,1)S(1)}, bf16[128,128]{1,0:T(8,128)(2,1)S(1)}, u32[]{:S(2)}, u32[]{:S(2)}) collective-permute-start(bf16[128,128]{1,0:T(8,128)(2,1)S(1)} %shard_map.77.a), channel_id=1, source_target_pairs={{0,12},{1,13},{2,14},{3,15},{4,8},{5,9},{6,10},{7,11},{8,4},{9,5},... | collective-permute-start | bytes 98312 | tf_op jit(solution)/shard_map/ppermute | solution.py:413
  30.5 1.3 %collective-permute-start.13 = (f32[128,128]{1,0:T(8,128)S(1)}, f32[128,128]{1,0:T(8,128)S(1)}, u32[]{:S(2)}, u32[]{:S(2)}) collective-permute-start(f32[128,128]{1,0:T(8,128)S(1)} %shard_map.81.refs_0_), channel_id=1, source_target_pairs={{0,8},{1,9},{2,10},{3,11},{4,12},{5,13},{6,14},{7,15},{8,0},{9,1},... | collective-permute-start | bytes 196616 | tf_op jit(solution)/shard_map/ppermute | solution.py:413

commit v7 on v5

--- a/solution.py
+++ b/solution.py
@@ -87,6 +87,10 @@
     @pl.when(lax.axis_index(axis) == lax.axis_size(axis) - 1)
     def _():
         high[...] = jnp.zeros_like(high)
+
+
+def scales():
+    return 1.0 + lax.broadcasted_iota(jnp.int32, (8, T), 0).astype(F32) * 0.125
 
 
 def my_half():
@@ -303,7 +307,7 @@
         wire[8 * i : 8 * i + 8] = out
     total = jnp.concatenate([total[:C] + total[C:], jnp.zeros((T - C, T), F32)], axis=0)
     total = jnp.sum(total.T, axis=0, keepdims=True)
-    wire[216:] = jnp.broadcast_to(total, (8, T))
+    wire[216:] = total * scales()
     for half in range(2):
 
         @pl.when(my_half() == half)
@@ -381,7 +385,8 @@
                     moved = part if group == 0 else pltpu.roll(part, T - group * C, 1)
                     block, inside = divmod(row, C)
                     filters[block * 3 + dz, inside : inside + 8, :] = moved[:, :C] * scale
-            biases[...] = halves_of[1][216 - HALF : 217 - HALF, :C] * scale
+            eight = halves_of[1][216 - HALF :] / scales()
+            biases[...] = jnp.sum(eight, axis=0, keepdims=True)[:, :C] * (scale / 8)
 
 
 def finish(own, other, scale):

time: 32.7 us -> 32.7 us (level)
  no operation moved by 1% of the time
where the time goes in v7:
time: 32.7 us; the launch traced here: 32.5 us
  starting transfers between devices  15.5 us (47%)
  Pallas kernels  7.96 us (24%)
  waiting for transfers between devices  5.51 us (17%)
  local copies, waits for them, and re-layouts  2.61 us (8%)
  between operations  0.9 us (3%)
    ppermute x14, starting transfers between devices, permute(): return lax.ppermute(array, ('gx', 'gy'), pairs)  15.5 us
    pallas_call x17, Pallas kernels, call(): pl.pallas_call(body, out_shape=jax.tree.map(lambda a: like(a.dtype, *a.sh...  7.96 us
    ppermute x14, waiting for transfers between devices, permute(): return lax.ppermute(array, ('gx', 'gy'), pairs)  5.51 us
    dynamic_slice x1, local copies, waits for them, and re-layouts, shards(): xeven = lax.dynamic_slice_in_dim(volume, up, 1, 0)  0.94 us
  transfers between devices with their start and end apart: 14, of which 7 were waited for; matrix products, arithmetic and copies ran while one was open for 3% of the time, Pallas kernels for 16%

profile of v7, /device:TPU:0, one launch (start us, length us, event | category | flops | bytes accessed | tf_op | source)
XLA Modules:
  0.0 32.5 jit_solution(7018068774056260264)
XLA Ops:
  0.6 0.0 copy-start.2
  0.7 0.9 %constant_dynamic-slice_fusion = (bf16[1,16,2048]{2,1,0:T(8,128)(2,1)S(1)}, bf16[1,16,2048]{2,1,0:T(8,128)(2,1)S(1)}) fusion(bf16[8,16,2048]{2,1,0:T(8,128)(2,1)} %array.1, s32[]{:T(128)S(6)} %select_n.15, s32[]{:T(128)S(6)} %select_n.14), kind=kLoop, calls=%fused_computation.7 | loop fusion | bytes 262152 | tf_op jit(solution)/shard_map/dynamic_slice | solution.py:433
  1.6 0.5 %collective-permute-start = (bf16[1,16,2048]{2,1,0:T(8,128)(2,1)S(1)}, bf16[1,16,2048]{2,1,0:T(8,128)(2,1)S(1)}, u32[]{:S(2)}, u32[]{:S(2)}) collective-permute-start(bf16[1,16,2048]{2,1,0:T(8,128)(2,1)S(1)} %get-tuple-element.43), channel_id=1, source_target_pairs={{0,8},{1,9},{2,10},{3,11},{4,12},{5,13},{6,14},{7,15},{8,0},{9,1},... | collective-permute-start | bytes 196616 | tf_op jit(solution)/shard_map/ppermute | solution.py:404
  2.1 2.6 %collective-permute-start.1 = (bf16[1,16,2048]{2,1,0:T(8,128)(2,1)S(1)}, bf16[1,16,2048]{2,1,0:T(8,128)(2,1)S(1)}, u32[]{:S(2)}, u32[]{:S(2)}) collective-permute-start(bf16[1,16,2048]{2,1,0:T(8,128)(2,1)S(1)} %get-tuple-element.44), channel_id=1, source_target_pairs={{0,24},{1,25},{2,26},{3,27},{4,28},{5,29},{6,30},{7,31},{8,16},{9,... | collective-permute-start | bytes 196616 | tf_op jit(solution)/shard_map/ppermute | solution.py:404
  4.8 0.0 copy-done.2
  4.8 0.2 copy.9
  5.0 0.0 copy-start
  5.0 0.2 reshape.25
  5.2 0.1 pad_bitcast_fusion.3
  5.3 0.0 copy-start.3
  5.3 0.6 %copy-done.3 = f32[32]{0:T(128)S(1)} copy-done((f32[32]{0:T(128)S(1)}, f32[32]{0:T(128)}, u32[]{:S(2)}) %copy-start.3) | copy-done | bytes 152
  6.0 0.1 broadcast_in_dim.2.refs_1_.bias
  6.0 0.0 copy-done
  6.0 0.3 shard_map.67.field.vx
  6.3 0.0 copy-start.1
  6.4 0.0 collective-permute-done.xeven
  6.4 0.8 %collective-permute-done.1.xodd = bf16[1,16,2048]{2,1,0:T(8,128)(2,1)S(1)} collective-permute-done((bf16[1,16,2048]{2,1,0:T(8,128)(2,1)S(1)}, bf16[1,16,2048]{2,1,0:T(8,128)(2,1)S(1)}, u32[]{:S(2)}, u32[]{:S(2)}) %collective-permute-start.1) | collective-permute-done | bytes 65568 | tf_op jit(solution)/shard_map/ppermute | solution.py:404
  7.1 0.2 shard_map.68
  7.4 0.2 collective-permute-start.2
  7.6 0.1 shard_map.69
  7.7 2.9 %collective-permute-start.3 = (bf16[5,32,128]{2,1,0:T(8,128)(2,1)S(1)}, bf16[5,32,128]{2,1,0:T(8,128)(2,1)S(1)}, u32[]{:S(2)}, u32[]{:S(2)}) collective-permute-start(bf16[5,32,128]{2,1,0:T(8,128)(2,1)S(1)} %shard_map.69), channel_id=1, source_target_pairs={{0,1},{1,0},{2,3},{3,2},{4,5},{5,4},{6,7},{7,6},{8,9},{9,8},{10,11... | collective-permute-start | bytes 122888 | tf_op jit(solution)/shard_map/ppermute | solution.py:404
  10.6 0.0 copy-done.1
  10.6 0.3 shard_map.70.gx
  10.9 2.2 %shard_map.71 = (bf16[8,32,768]{2,1,0:T(8,128)(2,1)S(1)}, f32[64,128]{1,0:T(8,128)S(1)}, f32[384,192]{1,0:T(8,128)S(1)}) custom-call(bf16[8,32,1024]{2,1,0:T(8,128)(2,1)S(1)} %shard_map.67.field.vx, bf16[8,32,1024]{2,1,0:T(8,128)(2,1)S(1)} %shard_map.70.gx, bf16[32,1024]{1,0:T(8,128)(2,1)S(1)} %get-tuple-element.48.xlow, ...), custom_call_target="tpu_custom_call" | custom-call | flops 1000000 | bytes 2064384 | tf_op jit(solution)/shard_map/pallas_call | solution.py:24
  13.0 0.0 collective-permute-done.2.yodd
  13.1 0.0 collective-permute-done.3.yeven
  13.1 1.4 %shard_map.72 = (bf16[8,32,256]{2,1,0:T(8,128)(2,1)S(1)}, f32[112,128]{1,0:T(8,128)S(1)}, f32[112,128]{1,0:T(8,128)S(1)}) custom-call(bf16[8,32,1024]{2,1,0:T(8,128)(2,1)S(1)} %shard_map.67.field.vx, bf16[8,32,1024]{2,1,0:T(8,128)(2,1)S(1)} %shard_map.70.gx, bf16[32,1024]{1,0:T(8,128)(2,1)S(1)} %get-tuple-element.48.xlow, ...), custom_call_target="tpu_custom_call" | custom-call | flops 700000000 | bytes 1998848 | tf_op jit(solution)/shard_map/pallas_call | solution.py:24
  14.5 0.1 collective-permute-start.4
  14.6 1.2 %collective-permute-done.4.b = f32[112,128]{1,0:T(8,128)S(1)} collective-permute-done((f32[112,128]{1,0:T(8,128)S(1)}, f32[112,128]{1,0:T(8,128)S(1)}, u32[]{:S(2)}, u32[]{:S(2)}) %collective-permute-start.4) | collective-permute-done | bytes 57376 | tf_op jit(solution)/shard_map/ppermute | solution.py:404
  15.8 1.3 %collective-permute-start.5 = (bf16[112,128]{1,0:T(8,128)(2,1)S(1)}, bf16[112,128]{1,0:T(8,128)(2,1)S(1)}, u32[]{:S(2)}, u32[]{:S(2)}) collective-permute-start(bf16[112,128]{1,0:T(8,128)(2,1)S(1)} %shard_map.73.a), channel_id=1, source_target_pairs={{0,24},{1,25},{2,26},{3,27},{4,28},{5,29},{6,30},{7,31},{8,16},{9,... | collective-permute-start | bytes 86024 | tf_op jit(solution)/shard_map/ppermute | solution.py:404
  17.2 0.2 copy.11
  17.3 0.2 reshape.27
  17.6 0.4 %collective-permute-start.7 = (bf16[32,1024]{1,0:T(8,128)(2,1)S(1)}, bf16[32,1024]{1,0:T(8,128)(2,1)S(1)}, u32[]{:S(2)}, u32[]{:S(2)}) collective-permute-start(bf16[32,1024]{1,0:T(8,128)(2,1)S(1)} %get-tuple-element.62), channel_id=1, source_target_pairs={{0,8},{1,9},{2,10},{3,11},{4,12},{5,13},{6,14},{7,15},{8,0},{9,1},... | collective-permute-start | bytes 196616 | tf_op jit(solution)/shard_map/ppermute | solution.py:404
  18.0 0.3 collective-permute-start.8
  18.3 0.9 %collective-permute-done.5.b = bf16[112,128]{1,0:T(8,128)(2,1)S(1)} collective-permute-done((bf16[112,128]{1,0:T(8,128)(2,1)S(1)}, bf16[112,128]{1,0:T(8,128)(2,1)S(1)}, u32[]{:S(2)}, u32[]{:S(2)}) %collective-permute-start.5) | collective-permute-done | bytes 28704 | tf_op jit(solution)/shard_map/ppermute | solution.py:404
  19.2 1.3 %collective-permute-start.6 = (bf16[112,128]{1,0:T(8,128)(2,1)S(1)}, bf16[112,128]{1,0:T(8,128)(2,1)S(1)}, u32[]{:S(2)}, u32[]{:S(2)}) collective-permute-start(bf16[112,128]{1,0:T(8,128)(2,1)S(1)} %shard_map.74.a), channel_id=1, source_target_pairs={{0,9},{1,8},{2,11},{3,10},{4,13},{5,12},{6,15},{7,14},{8,1},{9,0},... | collective-permute-start | bytes 86024 | tf_op jit(solution)/shard_map/ppermute | solution.py:404
  20.5 0.1 pad_bitcast_fusion.1
  20.6 2.0 %collective-permute-done.6.b = bf16[112,128]{1,0:T(8,128)(2,1)S(1)} collective-permute-done((bf16[112,128]{1,0:T(8,128)(2,1)S(1)}, bf16[112,128]{1,0:T(8,128)(2,1)S(1)}, u32[]{:S(2)}, u32[]{:S(2)}) %collective-permute-start.6) | collective-permute-done | bytes 28704 | tf_op jit(solution)/shard_map/ppermute | solution.py:404
  22.6 0.0 collective-permute-done.7.xeven
  22.6 0.0 collective-permute-done.8.xodd
  22.6 1.4 %collective-permute-start.9 = (bf16[112,128]{1,0:T(8,128)(2,1)S(1)}, bf16[112,128]{1,0:T(8,128)(2,1)S(1)}, u32[]{:S(2)}, u32[]{:S(2)}) collective-permute-start(bf16[112,128]{1,0:T(8,128)(2,1)S(1)} %shard_map.75.a), channel_id=1, source_target_pairs={{0,10},{1,11},{2,8},{3,9},{4,14},{5,15},{6,12},{7,13},{8,2},{9,3},... | collective-permute-start | bytes 86024 | tf_op jit(solution)/shard_map/ppermute | solution.py:404
  24.0 0.1 shard_map.78
  24.2 0.1 shard_map.79
  24.3 1.6 %collective-permute-start.12 = (bf16[5,32,128]{2,1,0:T(8,128)(2,1)S(1)}, bf16[5,32,128]{2,1,0:T(8,128)(2,1)S(1)}, u32[]{:S(2)}, u32[]{:S(2)}) collective-permute-start(bf16[5,32,128]{2,1,0:T(8,128)(2,1)S(1)} %shard_map.79), channel_id=1, source_target_pairs={{0,1},{1,0},{2,3},{3,2},{4,5},{5,4},{6,7},{7,6},{8,9},{9,8},{10,11... | collective-permute-start | bytes 122888 | tf_op jit(solution)/shard_map/ppermute | solution.py:404
  25.8 0.1 collective-permute-start.11
  25.9 0.1 collective-permute-done.9.b
  26.0 2.4 %collective-permute-start.10 = (bf16[112,128]{1,0:T(8,128)(2,1)S(1)}, bf16[112,128]{1,0:T(8,128)(2,1)S(1)}, u32[]{:S(2)}, u32[]{:S(2)}) collective-permute-start(bf16[112,128]{1,0:T(8,128)(2,1)S(1)} %shard_map.77.a), channel_id=1, source_target_pairs={{0,12},{1,13},{2,14},{3,15},{4,8},{5,9},{6,10},{7,11},{8,4},{9,5},... | collective-permute-start | bytes 86024 | tf_op jit(solution)/shard_map/ppermute | solution.py:404
  28.4 0.0 collective-permute-done.12.yeven
  28.4 0.0 collective-permute-done.11.yodd
  28.4 1.4 %shard_map.80.block = bf16[8,16,2048]{2,1,0:T(8,128)(2,1)S(1)} custom-call(bf16[8,32,768]{2,1,0:T(8,128)(2,1)S(1)} %get-tuple-element.66.mid.gmid, bf16[8,32,256]{2,1,0:T(8,128)(2,1)S(1)} %get-tuple-element.67.edge.field.gedge, bf16[32,1024]{1,0:T(8,128)(2,1)S(1)} %get-tuple-element.70.xlow, bf16[32,1024]{1,0:T(8,128)(2,1)S(1)} %get-tuple-element.71.xhigh, ...), custom_call_target="tpu_custom_call" | custom-call | flops 1000000000 | bytes 1409024 | tf_op jit(solution)/shard_map/pallas_call | solution.py:24
  29.8 0.5 %collective-permute-done.10.b = bf16[112,128]{1,0:T(8,128)(2,1)S(1)} collective-permute-done((bf16[112,128]{1,0:T(8,128)(2,1)S(1)}, bf16[112,128]{1,0:T(8,128)(2,1)S(1)}, u32[]{:S(2)}, u32[]{:S(2)}) %collective-permute-start.10) | collective-permute-done | bytes 28704 | tf_op jit(solution)/shard_map/ppermute | solution.py:404
  30.3 0.4 %collective-permute-start.13 = (f32[112,128]{1,0:T(8,128)S(1)}, f32[112,128]{1,0:T(8,128)S(1)}, u32[]{:S(2)}, u32[]{:S(2)}) collective-permute-start(f32[112,128]{1,0:T(8,128)S(1)} %shard_map.81.refs_0_), channel_id=1, source_target_pairs={{0,8},{1,9},{2,10},{3,11},{4,12},{5,13},{6,14},{7,15},{8,0},{9,1},... | collective-permute-start | bytes 172040 | tf_op jit(solution)/shard_map/ppermute | solution.py:404
  30.7 0.8 %shard_map.82 = bf16[8,16,2048]{2,1,0:T(8,128)(2,1)} custom-call(bf16[8,16,2048]{2,1,0:T(8,128)(2,1)S(1)} %shard_map.80.block), custom_call_target="tpu_custom_call" | custom-call | flops 100000 | bytes 1048576 | tf_op jit(solution)/shard_map/pallas_call | solution.py:24
  31.5 0.1 collective-permute-done.13.refs_1_
  31.6 0.9 %shard_map.83 = (f32[27,32,32]{2,1,0:T(8,128)}, f32[1,32]{1,0:T(1,128)}) custom-call(f32[112,128]{1,0:T(8,128)S(1)} %shard_map.81.refs_0_, f32[112,128]{1,0:T(8,128)S(1)} %collective-permute-done.13.refs_1_), custom_call_target="tpu_custom_call" | custom-call | flops 100000 | bytes 225408 | tf_op jit(solution)/shard_map/pallas_call | solution.py:24
  (11 shorter events, 0.2 us)
Async XLA Ops:
  0.6 4.1 %copy-start.2 = (bf16[3,3,3,32,32]{4,3,2,1,0:T(8,128)(2,1)S(1)}, bf16[3,3,3,32,32]{4,3,2,1,0:T(8,128)(2,1)}, u32[]{:S(2)}) copy-start(bf16[3,3,3,32,32]{4,3,2,1,0:T(8,128)(2,1)} %param.6) | copy-start | bytes 165892
  1.6 4.8 %collective-permute-start = (bf16[1,16,2048]{2,1,0:T(8,128)(2,1)S(1)}, bf16[1,16,2048]{2,1,0:T(8,128)(2,1)S(1)}, u32[]{:S(2)}, u32[]{:S(2)}) collective-permute-start(bf16[1,16,2048]{2,1,0:T(8,128)(2,1)S(1)} %get-tuple-element.43), channel_id=1, source_target_pairs={{0,8},{1,9},{2,10},{3,11},{4,12},{5,13},{6,14},{7,15},{8,0},{9,1},... | collective-permute-start | bytes 196616 | tf_op jit(solution)/shard_map/ppermute | solution.py:404
  2.1 5.0 %collective-permute-start.1 = (bf16[1,16,2048]{2,1,0:T(8,128)(2,1)S(1)}, bf16[1,16,2048]{2,1,0:T(8,128)(2,1)S(1)}, u32[]{:S(2)}, u32[]{:S(2)}) collective-permute-start(bf16[1,16,2048]{2,1,0:T(8,128)(2,1)S(1)} %get-tuple-element.44), channel_id=1, source_target_pairs={{0,24},{1,25},{2,26},{3,27},{4,28},{5,29},{6,30},{7,31},{8,16},{9,... | collective-permute-start | bytes 196616 | tf_op jit(solution)/shard_map/ppermute | solution.py:404
  5.0 1.1 %copy-start = (bf16[8,16,2048]{2,1,0:T(8,128)(2,1)S(1)}, bf16[8,16,2048]{2,1,0:T(8,128)(2,1)}, u32[]{:S(2)}) copy-start(bf16[8,16,2048]{2,1,0:T(8,128)(2,1)} %array.1) | copy-start | bytes 1572868
  5.3 0.7 %copy-start.3 = (f32[32]{0:T(128)S(1)}, f32[32]{0:T(128)}, u32[]{:S(2)}) copy-start(f32[32]{0:T(128)} %param.7) | copy-start | bytes 388
  6.3 4.2 %copy-start.1 = (bf16[8,16,2048]{2,1,0:T(8,128)(2,1)S(1)}, bf16[8,16,2048]{2,1,0:T(8,128)(2,1)}, u32[]{:S(2)}) copy-start(bf16[8,16,2048]{2,1,0:T(8,128)(2,1)} %array.2) | copy-start | bytes 1572868
  7.4 5.7 %collective-permute-start.2 = (bf16[5,32,128]{2,1,0:T(8,128)(2,1)S(1)}, bf16[5,32,128]{2,1,0:T(8,128)(2,1)S(1)}, u32[]{:S(2)}, u32[]{:S(2)}) collective-permute-start(bf16[5,32,128]{2,1,0:T(8,128)(2,1)S(1)} %get-tuple-element.50), channel_id=1, source_target_pairs={{0,8},{1,2},{2,1},{3,4},{4,3},{5,6},{6,5},{7,15},{8,0},{9,10},{10,... | collective-permute-start | bytes 122888 | tf_op jit(solution)/shard_map/ppermute | solution.py:404
  7.7 5.4 %collective-permute-start.3 = (bf16[5,32,128]{2,1,0:T(8,128)(2,1)S(1)}, bf16[5,32,128]{2,1,0:T(8,128)(2,1)S(1)}, u32[]{:S(2)}, u32[]{:S(2)}) collective-permute-start(bf16[5,32,128]{2,1,0:T(8,128)(2,1)S(1)} %shard_map.69), channel_id=1, source_target_pairs={{0,1},{1,0},{2,3},{3,2},{4,5},{5,4},{6,7},{7,6},{8,9},{9,8},{10,11... | collective-permute-start | bytes 122888 | tf_op jit(solution)/shard_map/ppermute | solution.py:404
  14.5 1.3 %collective-permute-start.4 = (f32[112,128]{1,0:T(8,128)S(1)}, f32[112,128]{1,0:T(8,128)S(1)}, u32[]{:S(2)}, u32[]{:S(2)}) collective-permute-start(f32[112,128]{1,0:T(8,128)S(1)} %get-tuple-element.57), channel_id=1, source_target_pairs={{0,8},{1,9},{2,10},{3,11},{4,12},{5,13},{6,14},{7,15},{8,0},{9,1},... | collective-permute-start | bytes 172040 | tf_op jit(solution)/shard_map/ppermute | solution.py:404
  15.8 3.4 %collective-permute-start.5 = (bf16[112,128]{1,0:T(8,128)(2,1)S(1)}, bf16[112,128]{1,0:T(8,128)(2,1)S(1)}, u32[]{:S(2)}, u32[]{:S(2)}) collective-permute-start(bf16[112,128]{1,0:T(8,128)(2,1)S(1)} %shard_map.73.a), channel_id=1, source_target_pairs={{0,24},{1,25},{2,26},{3,27},{4,28},{5,29},{6,30},{7,31},{8,16},{9,... | collective-permute-start | bytes 86024 | tf_op jit(solution)/shard_map/ppermute | solution.py:404
  17.6 5.0 %collective-permute-start.7 = (bf16[32,1024]{1,0:T(8,128)(2,1)S(1)}, bf16[32,1024]{1,0:T(8,128)(2,1)S(1)}, u32[]{:S(2)}, u32[]{:S(2)}) collective-permute-start(bf16[32,1024]{1,0:T(8,128)(2,1)S(1)} %get-tuple-element.62), channel_id=1, source_target_pairs={{0,8},{1,9},{2,10},{3,11},{4,12},{5,13},{6,14},{7,15},{8,0},{9,1},... | collective-permute-start | bytes 196616 | tf_op jit(solution)/shard_map/ppermute | solution.py:404
  18.0 4.6 %collective-permute-start.8 = (bf16[32,1024]{1,0:T(8,128)(2,1)S(1)}, bf16[32,1024]{1,0:T(8,128)(2,1)S(1)}, u32[]{:S(2)}, u32[]{:S(2)}) collective-permute-start(bf16[32,1024]{1,0:T(8,128)(2,1)S(1)} %get-tuple-element.63), channel_id=1, source_target_pairs={{0,24},{1,25},{2,26},{3,27},{4,28},{5,29},{6,30},{7,31},{8,16},{9,... | collective-permute-start | bytes 196616 | tf_op jit(solution)/shard_map/ppermute | solution.py:404
  19.2 3.4 %collective-permute-start.6 = (bf16[112,128]{1,0:T(8,128)(2,1)S(1)}, bf16[112,128]{1,0:T(8,128)(2,1)S(1)}, u32[]{:S(2)}, u32[]{:S(2)}) collective-permute-start(bf16[112,128]{1,0:T(8,128)(2,1)S(1)} %shard_map.74.a), channel_id=1, source_target_pairs={{0,9},{1,8},{2,11},{3,10},{4,13},{5,12},{6,15},{7,14},{8,1},{9,0},... | collective-permute-start | bytes 86024 | tf_op jit(solution)/shard_map/ppermute | solution.py:404
  22.6 3.4 %collective-permute-start.9 = (bf16[112,128]{1,0:T(8,128)(2,1)S(1)}, bf16[112,128]{1,0:T(8,128)(2,1)S(1)}, u32[]{:S(2)}, u32[]{:S(2)}) collective-permute-start(bf16[112,128]{1,0:T(8,128)(2,1)S(1)} %shard_map.75.a), channel_id=1, source_target_pairs={{0,10},{1,11},{2,8},{3,9},{4,14},{5,15},{6,12},{7,13},{8,2},{9,3},... | collective-permute-start | bytes 86024 | tf_op jit(solution)/shard_map/ppermute | solution.py:404
  24.3 4.1 %collective-permute-start.12 = (bf16[5,32,128]{2,1,0:T(8,128)(2,1)S(1)}, bf16[5,32,128]{2,1,0:T(8,128)(2,1)S(1)}, u32[]{:S(2)}, u32[]{:S(2)}) collective-permute-start(bf16[5,32,128]{2,1,0:T(8,128)(2,1)S(1)} %shard_map.79), channel_id=1, source_target_pairs={{0,1},{1,0},{2,3},{3,2},{4,5},{5,4},{6,7},{7,6},{8,9},{9,8},{10,11... | collective-permute-start | bytes 122888 | tf_op jit(solution)/shard_map/ppermute | solution.py:404
  25.8 2.6 %collective-permute-start.11 = (bf16[5,32,128]{2,1,0:T(8,128)(2,1)S(1)}, bf16[5,32,128]{2,1,0:T(8,128)(2,1)S(1)}, u32[]{:S(2)}, u32[]{:S(2)}) collective-permute-start(bf16[5,32,128]{2,1,0:T(8,128)(2,1)S(1)} %get-tuple-element.72), channel_id=1, source_target_pairs={{0,8},{1,2},{2,1},{3,4},{4,3},{5,6},{6,5},{7,15},{8,0},{9,10},{10,... | collective-permute-start | bytes 122888 | tf_op jit(solution)/shard_map/ppermute | solution.py:404
  26.0 4.3 %collective-permute-start.10 = (bf16[112,128]{1,0:T(8,128)(2,1)S(1)}, bf16[112,128]{1,0:T(8,128)(2,1)S(1)}, u32[]{:S(2)}, u32[]{:S(2)}) collective-permute-start(bf16[112,128]{1,0:T(8,128)(2,1)S(1)} %shard_map.77.a), channel_id=1, source_target_pairs={{0,12},{1,13},{2,14},{3,15},{4,8},{5,9},{6,10},{7,11},{8,4},{9,5},... | collective-permute-start | bytes 86024 | tf_op jit(solution)/shard_map/ppermute | solution.py:404
  30.3 1.3 %collective-permute-start.13 = (f32[112,128]{1,0:T(8,128)S(1)}, f32[112,128]{1,0:T(8,128)S(1)}, u32[]{:S(2)}, u32[]{:S(2)}) collective-permute-start(f32[112,128]{1,0:T(8,128)S(1)} %shard_map.81.refs_0_), channel_id=1, source_target_pairs={{0,8},{1,9},{2,10},{3,11},{4,12},{5,13},{6,14},{7,15},{8,0},{9,1},... | collective-permute-start | bytes 172040 | tf_op jit(solution)/shard_map/ppermute | solution.py:404

commit v8 on v7

--- a/solution.py
+++ b/solution.py
@@ -434,7 +434,7 @@
     xodd = lax.dynamic_slice_in_dim(volume, 7 - up, 1, 0)
     xodd, xeven, bias = barrier((xodd, xeven, bias))
     offset = jnp.broadcast_to(bias[:, None], (C, T))
-    vx = pack(volume, wf, offset)
+    vx = pack(volume, wf, wd, offset)
     xodd = swap_x(xodd, 1)
     xeven = swap_x(xeven, 0)
     yodd, xlow, xhigh = odd_edge(vx, xeven, xodd)

time: 32.7 us -> 34.3 us (1.049)
  waiting for transfers between devices: 5.51 us -> 7.14 us
    ppermute x14, waiting for transfers between devices: 5.51 us -> 7.14 us  [permute(): return lax.ppermute(array, ('gx', 'gy'), pairs)]
  transfers between devices with their start and end apart: 14 -> 14, of which waited for: 7 -> 7; matrix products, arithmetic and copies ran while one was open for 3% -> 3% of each run, Pallas kernels for 16% -> 15%
where the time goes in v8:
time: 34.3 us; the launch traced here: 34.1 us
  starting transfers between devices  15.5 us (45%)
  Pallas kernels  7.91 us (23%)
  waiting for transfers between devices  7.14 us (21%)
  local copies, waits for them, and re-layouts  2.61 us (8%)
  between operations  0.9 us (3%)
    ppermute x14, starting transfers between devices, permute(): return lax.ppermute(array, ('gx', 'gy'), pairs)  15.5 us
    pallas_call x17, Pallas kernels, call(): pl.pallas_call(body, out_shape=jax.tree.map(lambda a: like(a.dtype, *a.sh...  7.91 us
    ppermute x14, waiting for transfers between devices, permute(): return lax.ppermute(array, ('gx', 'gy'), pairs)  7.14 us
    dynamic_slice x1, local copies, waits for them, and re-layouts, shards(): xeven = lax.dynamic_slice_in_dim(volume, up, 1, 0)  0.94 us
  transfers between devices with their start and end apart: 14, of which 7 were waited for; matrix products, arithmetic and copies ran while one was open for 3% of the time, Pallas kernels for 15%

profile of v8, /device:TPU:0, one launch (start us, length us, event | category | flops | bytes accessed | tf_op | source)
XLA Modules:
  0.0 34.1 jit_solution(7842728055809089049)
XLA Ops:
  0.6 0.0 copy-start.2
  0.7 0.9 %constant_dynamic-slice_fusion = (bf16[1,16,2048]{2,1,0:T(8,128)(2,1)S(1)}, bf16[1,16,2048]{2,1,0:T(8,128)(2,1)S(1)}) fusion(bf16[8,16,2048]{2,1,0:T(8,128)(2,1)} %array.1, s32[]{:T(128)S(6)} %select_n.15, s32[]{:T(128)S(6)} %select_n.14), kind=kLoop, calls=%fused_computation.7 | loop fusion | bytes 262152 | tf_op jit(solution)/shard_map/dynamic_slice | solution.py:433
  1.6 0.5 %collective-permute-start = (bf16[1,16,2048]{2,1,0:T(8,128)(2,1)S(1)}, bf16[1,16,2048]{2,1,0:T(8,128)(2,1)S(1)}, u32[]{:S(2)}, u32[]{:S(2)}) collective-permute-start(bf16[1,16,2048]{2,1,0:T(8,128)(2,1)S(1)} %get-tuple-element.43), channel_id=1, source_target_pairs={{0,8},{1,9},{2,10},{3,11},{4,12},{5,13},{6,14},{7,15},{8,0},{9,1},... | collective-permute-start | bytes 196616 | tf_op jit(solution)/shard_map/ppermute | solution.py:404
  2.1 2.6 %collective-permute-start.1 = (bf16[1,16,2048]{2,1,0:T(8,128)(2,1)S(1)}, bf16[1,16,2048]{2,1,0:T(8,128)(2,1)S(1)}, u32[]{:S(2)}, u32[]{:S(2)}) collective-permute-start(bf16[1,16,2048]{2,1,0:T(8,128)(2,1)S(1)} %get-tuple-element.44), channel_id=1, source_target_pairs={{0,24},{1,25},{2,26},{3,27},{4,28},{5,29},{6,30},{7,31},{8,16},{9,... | collective-permute-start | bytes 196616 | tf_op jit(solution)/shard_map/ppermute | solution.py:404
  4.8 0.0 copy-done.2
  4.8 0.2 copy.11
  5.0 0.2 reshape.27
  5.1 0.1 pad_bitcast_fusion.1
  5.3 0.2 copy.9
  5.5 0.0 copy-start
  5.5 0.2 reshape.25
  5.7 0.1 pad_bitcast_fusion.3
  5.8 0.0 copy-start.3
  5.9 0.6 %copy-done.3 = f32[32]{0:T(128)S(1)} copy-done((f32[32]{0:T(128)S(1)}, f32[32]{0:T(128)}, u32[]{:S(2)}) %copy-start.3) | copy-done | bytes 152
  6.5 0.1 broadcast_in_dim.2.refs_2_.bias
  6.6 0.0 copy-done
  6.6 0.3 shard_map.67.field.vx
  6.9 0.0 copy-start.1
  6.9 0.0 collective-permute-done.xeven
  6.9 0.2 collective-permute-done.1.xodd
  7.1 0.2 shard_map.68
  7.4 0.2 collective-permute-start.2
  7.6 0.1 shard_map.69
  7.7 2.9 %collective-permute-start.3 = (bf16[5,32,128]{2,1,0:T(8,128)(2,1)S(1)}, bf16[5,32,128]{2,1,0:T(8,128)(2,1)S(1)}, u32[]{:S(2)}, u32[]{:S(2)}) collective-permute-start(bf16[5,32,128]{2,1,0:T(8,128)(2,1)S(1)} %shard_map.69), channel_id=1, source_target_pairs={{0,1},{1,0},{2,3},{3,2},{4,5},{5,4},{6,7},{7,6},{8,9},{9,8},{10,11... | collective-permute-start | bytes 122888 | tf_op jit(solution)/shard_map/ppermute | solution.py:404
  10.6 0.0 copy-done.1
  10.6 0.3 shard_map.70.gx
  10.9 2.1 %shard_map.71 = (bf16[8,32,768]{2,1,0:T(8,128)(2,1)S(1)}, f32[64,128]{1,0:T(8,128)S(1)}, f32[384,192]{1,0:T(8,128)S(1)}) custom-call(bf16[8,32,1024]{2,1,0:T(8,128)(2,1)S(1)} %shard_map.67.field.vx, bf16[8,32,1024]{2,1,0:T(8,128)(2,1)S(1)} %shard_map.70.gx, bf16[32,1024]{1,0:T(8,128)(2,1)S(1)} %get-tuple-element.48.xlow, ...), custom_call_target="tpu_custom_call" | custom-call | flops 1000000 | bytes 2064384 | tf_op jit(solution)/shard_map/pallas_call | solution.py:24
  13.0 0.0 collective-permute-done.2.yodd
  13.0 0.0 collective-permute-done.3.yeven
  13.0 1.4 %shard_map.72 = (bf16[8,32,256]{2,1,0:T(8,128)(2,1)S(1)}, f32[112,128]{1,0:T(8,128)S(1)}, f32[112,128]{1,0:T(8,128)S(1)}) custom-call(bf16[8,32,1024]{2,1,0:T(8,128)(2,1)S(1)} %shard_map.67.field.vx, bf16[8,32,1024]{2,1,0:T(8,128)(2,1)S(1)} %shard_map.70.gx, bf16[32,1024]{1,0:T(8,128)(2,1)S(1)} %get-tuple-element.48.xlow, ...), custom_call_target="tpu_custom_call" | custom-call | flops 700000000 | bytes 1998848 | tf_op jit(solution)/shard_map/pallas_call | solution.py:24
  14.5 0.1 collective-permute-start.4
  14.6 1.2 %collective-permute-done.4.b = f32[112,128]{1,0:T(8,128)S(1)} collective-permute-done((f32[112,128]{1,0:T(8,128)S(1)}, f32[112,128]{1,0:T(8,128)S(1)}, u32[]{:S(2)}, u32[]{:S(2)}) %collective-permute-start.4) | collective-permute-done | bytes 57376 | tf_op jit(solution)/shard_map/ppermute | solution.py:404
  15.8 0.2 collective-permute-start.7
  16.1 1.5 %collective-permute-start.8 = (bf16[32,1024]{1,0:T(8,128)(2,1)S(1)}, bf16[32,1024]{1,0:T(8,128)(2,1)S(1)}, u32[]{:S(2)}, u32[]{:S(2)}) collective-permute-start(bf16[32,1024]{1,0:T(8,128)(2,1)S(1)} %get-tuple-element.63), channel_id=1, source_target_pairs={{0,24},{1,25},{2,26},{3,27},{4,28},{5,29},{6,30},{7,31},{8,16},{9,... | collective-permute-start | bytes 196616 | tf_op jit(solution)/shard_map/ppermute | solution.py:404
  17.5 0.3 collective-permute-start.5
  17.8 3.0 %collective-permute-done.5.b = bf16[112,128]{1,0:T(8,128)(2,1)S(1)} collective-permute-done((bf16[112,128]{1,0:T(8,128)(2,1)S(1)}, bf16[112,128]{1,0:T(8,128)(2,1)S(1)}, u32[]{:S(2)}, u32[]{:S(2)}) %collective-permute-start.5) | collective-permute-done | bytes 28704 | tf_op jit(solution)/shard_map/ppermute | solution.py:404
  20.8 1.3 %collective-permute-start.6 = (bf16[112,128]{1,0:T(8,128)(2,1)S(1)}, bf16[112,128]{1,0:T(8,128)(2,1)S(1)}, u32[]{:S(2)}, u32[]{:S(2)}) collective-permute-start(bf16[112,128]{1,0:T(8,128)(2,1)S(1)} %shard_map.74.a), channel_id=1, source_target_pairs={{0,9},{1,8},{2,11},{3,10},{4,13},{5,12},{6,15},{7,14},{8,1},{9,0},... | collective-permute-start | bytes 86024 | tf_op jit(solution)/shard_map/ppermute | solution.py:404
  22.2 2.0 %collective-permute-done.6.b = bf16[112,128]{1,0:T(8,128)(2,1)S(1)} collective-permute-done((bf16[112,128]{1,0:T(8,128)(2,1)S(1)}, bf16[112,128]{1,0:T(8,128)(2,1)S(1)}, u32[]{:S(2)}, u32[]{:S(2)}) %collective-permute-start.6) | collective-permute-done | bytes 28704 | tf_op jit(solution)/shard_map/ppermute | solution.py:404
  24.2 0.0 collective-permute-done.7.xeven
  24.2 0.0 collective-permute-done.8.xodd
  24.2 1.4 %collective-permute-start.9 = (bf16[112,128]{1,0:T(8,128)(2,1)S(1)}, bf16[112,128]{1,0:T(8,128)(2,1)S(1)}, u32[]{:S(2)}, u32[]{:S(2)}) collective-permute-start(bf16[112,128]{1,0:T(8,128)(2,1)S(1)} %shard_map.75.a), channel_id=1, source_target_pairs={{0,10},{1,11},{2,8},{3,9},{4,14},{5,15},{6,12},{7,13},{8,2},{9,3},... | collective-permute-start | bytes 86024 | tf_op jit(solution)/shard_map/ppermute | solution.py:404
  25.6 0.1 shard_map.78
  25.7 0.1 shard_map.79
  25.8 1.6 %collective-permute-start.12 = (bf16[5,32,128]{2,1,0:T(8,128)(2,1)S(1)}, bf16[5,32,128]{2,1,0:T(8,128)(2,1)S(1)}, u32[]{:S(2)}, u32[]{:S(2)}) collective-permute-start(bf16[5,32,128]{2,1,0:T(8,128)(2,1)S(1)} %shard_map.79), channel_id=1, source_target_pairs={{0,1},{1,0},{2,3},{3,2},{4,5},{5,4},{6,7},{7,6},{8,9},{9,8},{10,11... | collective-permute-start | bytes 122888 | tf_op jit(solution)/shard_map/ppermute | solution.py:404
  27.4 0.1 collective-permute-start.11
  27.5 0.1 collective-permute-done.9.b
  27.6 2.4 %collective-permute-start.10 = (bf16[112,128]{1,0:T(8,128)(2,1)S(1)}, bf16[112,128]{1,0:T(8,128)(2,1)S(1)}, u32[]{:S(2)}, u32[]{:S(2)}) collective-permute-start(bf16[112,128]{1,0:T(8,128)(2,1)S(1)} %shard_map.77.a), channel_id=1, source_target_pairs={{0,12},{1,13},{2,14},{3,15},{4,8},{5,9},{6,10},{7,11},{8,4},{9,5},... | collective-permute-start | bytes 86024 | tf_op jit(solution)/shard_map/ppermute | solution.py:404
  30.0 0.0 collective-permute-done.12.yeven
  30.0 0.0 collective-permute-done.11.yodd
  30.0 1.4 %shard_map.80.block = bf16[8,16,2048]{2,1,0:T(8,128)(2,1)S(1)} custom-call(bf16[8,32,768]{2,1,0:T(8,128)(2,1)S(1)} %get-tuple-element.66.mid.gmid, bf16[8,32,256]{2,1,0:T(8,128)(2,1)S(1)} %get-tuple-element.67.edge.field.gedge, bf16[32,1024]{1,0:T(8,128)(2,1)S(1)} %get-tuple-element.70.xlow, bf16[32,1024]{1,0:T(8,128)(2,1)S(1)} %get-tuple-element.71.xhigh, ...), custom_call_target="tpu_custom_call" | custom-call | flops 1000000000 | bytes 1409024 | tf_op jit(solution)/shard_map/pallas_call | solution.py:24
  31.4 0.4 %collective-permute-done.10.b = bf16[112,128]{1,0:T(8,128)(2,1)S(1)} collective-permute-done((bf16[112,128]{1,0:T(8,128)(2,1)S(1)}, bf16[112,128]{1,0:T(8,128)(2,1)S(1)}, u32[]{:S(2)}, u32[]{:S(2)}) %collective-permute-start.10) | collective-permute-done | bytes 28704 | tf_op jit(solution)/shard_map/ppermute | solution.py:404
  31.9 0.4 %collective-permute-start.13 = (f32[112,128]{1,0:T(8,128)S(1)}, f32[112,128]{1,0:T(8,128)S(1)}, u32[]{:S(2)}, u32[]{:S(2)}) collective-permute-start(f32[112,128]{1,0:T(8,128)S(1)} %shard_map.81.refs_0_), channel_id=1, source_target_pairs={{0,8},{1,9},{2,10},{3,11},{4,12},{5,13},{6,14},{7,15},{8,0},{9,1},... | collective-permute-start | bytes 172040 | tf_op jit(solution)/shard_map/ppermute | solution.py:404
  32.3 0.8 %shard_map.82 = bf16[8,16,2048]{2,1,0:T(8,128)(2,1)} custom-call(bf16[8,16,2048]{2,1,0:T(8,128)(2,1)S(1)} %shard_map.80.block), custom_call_target="tpu_custom_call" | custom-call | flops 100000 | bytes 1048576 | tf_op jit(solution)/shard_map/pallas_call | solution.py:24
  33.1 0.1 collective-permute-done.13.refs_1_
  33.2 0.9 %shard_map.83 = (f32[27,32,32]{2,1,0:T(8,128)}, f32[1,32]{1,0:T(1,128)}) custom-call(f32[112,128]{1,0:T(8,128)S(1)} %shard_map.81.refs_0_, f32[112,128]{1,0:T(8,128)S(1)} %collective-permute-done.13.refs_1_), custom_call_target="tpu_custom_call" | custom-call | flops 100000 | bytes 225408 | tf_op jit(solution)/shard_map/pallas_call | solution.py:24
  (11 shorter events, 0.2 us)
Async XLA Ops:
  0.6 4.1 %copy-start.2 = (bf16[3,3,3,32,32]{4,3,2,1,0:T(8,128)(2,1)S(1)}, bf16[3,3,3,32,32]{4,3,2,1,0:T(8,128)(2,1)}, u32[]{:S(2)}) copy-start(bf16[3,3,3,32,32]{4,3,2,1,0:T(8,128)(2,1)} %param.6) | copy-start | bytes 165892
  1.6 5.3 %collective-permute-start = (bf16[1,16,2048]{2,1,0:T(8,128)(2,1)S(1)}, bf16[1,16,2048]{2,1,0:T(8,128)(2,1)S(1)}, u32[]{:S(2)}, u32[]{:S(2)}) collective-permute-start(bf16[1,16,2048]{2,1,0:T(8,128)(2,1)S(1)} %get-tuple-element.43), channel_id=1, source_target_pairs={{0,8},{1,9},{2,10},{3,11},{4,12},{5,13},{6,14},{7,15},{8,0},{9,1},... | collective-permute-start | bytes 196616 | tf_op jit(solution)/shard_map/ppermute | solution.py:404
  2.1 5.0 %collective-permute-start.1 = (bf16[1,16,2048]{2,1,0:T(8,128)(2,1)S(1)}, bf16[1,16,2048]{2,1,0:T(8,128)(2,1)S(1)}, u32[]{:S(2)}, u32[]{:S(2)}) collective-permute-start(bf16[1,16,2048]{2,1,0:T(8,128)(2,1)S(1)} %get-tuple-element.44), channel_id=1, source_target_pairs={{0,24},{1,25},{2,26},{3,27},{4,28},{5,29},{6,30},{7,31},{8,16},{9,... | collective-permute-start | bytes 196616 | tf_op jit(solution)/shard_map/ppermute | solution.py:404
  5.5 1.1 %copy-start = (bf16[8,16,2048]{2,1,0:T(8,128)(2,1)S(1)}, bf16[8,16,2048]{2,1,0:T(8,128)(2,1)}, u32[]{:S(2)}) copy-start(bf16[8,16,2048]{2,1,0:T(8,128)(2,1)} %array.1) | copy-start | bytes 1572868
  5.8 0.7 %copy-start.3 = (f32[32]{0:T(128)S(1)}, f32[32]{0:T(128)}, u32[]{:S(2)}) copy-start(f32[32]{0:T(128)} %param.7) | copy-start | bytes 388
  6.9 3.7 %copy-start.1 = (bf16[8,16,2048]{2,1,0:T(8,128)(2,1)S(1)}, bf16[8,16,2048]{2,1,0:T(8,128)(2,1)}, u32[]{:S(2)}) copy-start(bf16[8,16,2048]{2,1,0:T(8,128)(2,1)} %array.2) | copy-start | bytes 1572868
  7.4 5.6 %collective-permute-start.2 = (bf16[5,32,128]{2,1,0:T(8,128)(2,1)S(1)}, bf16[5,32,128]{2,1,0:T(8,128)(2,1)S(1)}, u32[]{:S(2)}, u32[]{:S(2)}) collective-permute-start(bf16[5,32,128]{2,1,0:T(8,128)(2,1)S(1)} %get-tuple-element.50), channel_id=1, source_target_pairs={{0,8},{1,2},{2,1},{3,4},{4,3},{5,6},{6,5},{7,15},{8,0},{9,10},{10,... | collective-permute-start | bytes 122888 | tf_op jit(solution)/shard_map/ppermute | solution.py:404
  7.7 5.4 %collective-permute-start.3 = (bf16[5,32,128]{2,1,0:T(8,128)(2,1)S(1)}, bf16[5,32,128]{2,1,0:T(8,128)(2,1)S(1)}, u32[]{:S(2)}, u32[]{:S(2)}) collective-permute-start(bf16[5,32,128]{2,1,0:T(8,128)(2,1)S(1)} %shard_map.69), channel_id=1, source_target_pairs={{0,1},{1,0},{2,3},{3,2},{4,5},{5,4},{6,7},{7,6},{8,9},{9,8},{10,11... | collective-permute-start | bytes 122888 | tf_op jit(solution)/shard_map/ppermute | solution.py:404
  14.5 1.3 %collective-permute-start.4 = (f32[112,128]{1,0:T(8,128)S(1)}, f32[112,128]{1,0:T(8,128)S(1)}, u32[]{:S(2)}, u32[]{:S(2)}) collective-permute-start(f32[112,128]{1,0:T(8,128)S(1)} %get-tuple-element.57), channel_id=1, source_target_pairs={{0,8},{1,9},{2,10},{3,11},{4,12},{5,13},{6,14},{7,15},{8,0},{9,1},... | collective-permute-start | bytes 172040 | tf_op jit(solution)/shard_map/ppermute | solution.py:404
  15.8 8.4 %collective-permute-start.7 = (bf16[32,1024]{1,0:T(8,128)(2,1)S(1)}, bf16[32,1024]{1,0:T(8,128)(2,1)S(1)}, u32[]{:S(2)}, u32[]{:S(2)}) collective-permute-start(bf16[32,1024]{1,0:T(8,128)(2,1)S(1)} %get-tuple-element.62), channel_id=1, source_target_pairs={{0,8},{1,9},{2,10},{3,11},{4,12},{5,13},{6,14},{7,15},{8,0},{9,1},... | collective-permute-start | bytes 196616 | tf_op jit(solution)/shard_map/ppermute | solution.py:404
  16.1 8.2 %collective-permute-start.8 = (bf16[32,1024]{1,0:T(8,128)(2,1)S(1)}, bf16[32,1024]{1,0:T(8,128)(2,1)S(1)}, u32[]{:S(2)}, u32[]{:S(2)}) collective-permute-start(bf16[32,1024]{1,0:T(8,128)(2,1)S(1)} %get-tuple-element.63), channel_id=1, source_target_pairs={{0,24},{1,25},{2,26},{3,27},{4,28},{5,29},{6,30},{7,31},{8,16},{9,... | collective-permute-start | bytes 196616 | tf_op jit(solution)/shard_map/ppermute | solution.py:404
  17.5 3.3 %collective-permute-start.5 = (bf16[112,128]{1,0:T(8,128)(2,1)S(1)}, bf16[112,128]{1,0:T(8,128)(2,1)S(1)}, u32[]{:S(2)}, u32[]{:S(2)}) collective-permute-start(bf16[112,128]{1,0:T(8,128)(2,1)S(1)} %shard_map.73.a), channel_id=1, source_target_pairs={{0,24},{1,25},{2,26},{3,27},{4,28},{5,29},{6,30},{7,31},{8,16},{9,... | collective-permute-start | bytes 86024 | tf_op jit(solution)/shard_map/ppermute | solution.py:404
  20.8 3.4 %collective-permute-start.6 = (bf16[112,128]{1,0:T(8,128)(2,1)S(1)}, bf16[112,128]{1,0:T(8,128)(2,1)S(1)}, u32[]{:S(2)}, u32[]{:S(2)}) collective-permute-start(bf16[112,128]{1,0:T(8,128)(2,1)S(1)} %shard_map.74.a), channel_id=1, source_target_pairs={{0,9},{1,8},{2,11},{3,10},{4,13},{5,12},{6,15},{7,14},{8,1},{9,0},... | collective-permute-start | bytes 86024 | tf_op jit(solution)/shard_map/ppermute | solution.py:404
  24.2 3.4 %collective-permute-start.9 = (bf16[112,128]{1,0:T(8,128)(2,1)S(1)}, bf16[112,128]{1,0:T(8,128)(2,1)S(1)}, u32[]{:S(2)}, u32[]{:S(2)}) collective-permute-start(bf16[112,128]{1,0:T(8,128)(2,1)S(1)} %shard_map.75.a), channel_id=1, source_target_pairs={{0,10},{1,11},{2,8},{3,9},{4,14},{5,15},{6,12},{7,13},{8,2},{9,3},... | collective-permute-start | bytes 86024 | tf_op jit(solution)/shard_map/ppermute | solution.py:404
  25.8 4.2 %collective-permute-start.12 = (bf16[5,32,128]{2,1,0:T(8,128)(2,1)S(1)}, bf16[5,32,128]{2,1,0:T(8,128)(2,1)S(1)}, u32[]{:S(2)}, u32[]{:S(2)}) collective-permute-start(bf16[5,32,128]{2,1,0:T(8,128)(2,1)S(1)} %shard_map.79), channel_id=1, source_target_pairs={{0,1},{1,0},{2,3},{3,2},{4,5},{5,4},{6,7},{7,6},{8,9},{9,8},{10,11... | collective-permute-start | bytes 122888 | tf_op jit(solution)/shard_map/ppermute | solution.py:404
  27.4 2.6 %collective-permute-start.11 = (bf16[5,32,128]{2,1,0:T(8,128)(2,1)S(1)}, bf16[5,32,128]{2,1,0:T(8,128)(2,1)S(1)}, u32[]{:S(2)}, u32[]{:S(2)}) collective-permute-start(bf16[5,32,128]{2,1,0:T(8,128)(2,1)S(1)} %get-tuple-element.72), channel_id=1, source_target_pairs={{0,8},{1,2},{2,1},{3,4},{4,3},{5,6},{6,5},{7,15},{8,0},{9,10},{10,... | collective-permute-start | bytes 122888 | tf_op jit(solution)/shard_map/ppermute | solution.py:404
  27.6 4.3 %collective-permute-start.10 = (bf16[112,128]{1,0:T(8,128)(2,1)S(1)}, bf16[112,128]{1,0:T(8,128)(2,1)S(1)}, u32[]{:S(2)}, u32[]{:S(2)}) collective-permute-start(bf16[112,128]{1,0:T(8,128)(2,1)S(1)} %shard_map.77.a), channel_id=1, source_target_pairs={{0,12},{1,13},{2,14},{3,15},{4,8},{5,9},{6,10},{7,11},{8,4},{9,5},... | collective-permute-start | bytes 86024 | tf_op jit(solution)/shard_map/ppermute | solution.py:404
  31.9 1.3 %collective-permute-start.13 = (f32[112,128]{1,0:T(8,128)S(1)}, f32[112,128]{1,0:T(8,128)S(1)}, u32[]{:S(2)}, u32[]{:S(2)}) collective-permute-start(f32[112,128]{1,0:T(8,128)S(1)} %shard_map.81.refs_0_), channel_id=1, source_target_pairs={{0,8},{1,9},{2,10},{3,11},{4,12},{5,13},{6,14},{7,15},{8,0},{9,1},... | collective-permute-start | bytes 172040 | tf_op jit(solution)/shard_map/ppermute | solution.py:404

commit v9 on v7

--- a/solution.py
+++ b/solution.py
@@ -76,7 +76,7 @@
 
 
 def is_even(axis):
-    return lax.axis_index(axis) % 2 == 0
+    return (lax.axis_index(axis) & 1) == 0
 
 
 def clear_ends(axis, low, high):
@@ -97,8 +97,8 @@
     total = 0
     for axis in ("gx", "gy"):
         for b in range(lax.axis_size(axis).bit_length() - 1):
-            total = total + lax.axis_index(axis) // (1 << b)
-    return total % 2
+            total = total + (lax.axis_index(axis) >> b)
+    return total & 1
 
 
 def faces(field, even, odd):

time: 32.7 us -> 32.6 us (level)
  no operation moved by 1% of the time
where the time goes in v9:
time: 32.6 us; the launch traced here: 32.5 us
  starting transfers between devices  15.5 us (48%)
  Pallas kernels  7.94 us (24%)
  waiting for transfers between devices  5.53 us (17%)
  local copies, waits for them, and re-layouts  2.61 us (8%)
  between operations  0.9 us (3%)
    ppermute x14, starting transfers between devices, permute(): return lax.ppermute(array, ('gx', 'gy'), pairs)  15.5 us
    pallas_call x17, Pallas kernels, call(): pl.pallas_call(body, out_shape=jax.tree.map(lambda a: like(a.dtype, *a.sh...  7.94 us
    ppermute x14, waiting for transfers between devices, permute(): return lax.ppermute(array, ('gx', 'gy'), pairs)  5.53 us
    dynamic_slice x1, local copies, waits for them, and re-layouts, shards(): xeven = lax.dynamic_slice_in_dim(volume, up, 1, 0)  0.94 us
  transfers between devices with their start and end apart: 14, of which 7 were waited for; matrix products, arithmetic and copies ran while one was open for 3% of the time, Pallas kernels for 16%

profile of v9, /device:TPU:0, one launch (start us, length us, event | category | flops | bytes accessed | tf_op | source)
XLA Modules:
  0.0 32.5 jit_solution(6418766134471098487)
XLA Ops:
  0.6 0.0 copy-start.2
  0.7 0.9 %constant_dynamic-slice_fusion = (bf16[1,16,2048]{2,1,0:T(8,128)(2,1)S(1)}, bf16[1,16,2048]{2,1,0:T(8,128)(2,1)S(1)}) fusion(bf16[8,16,2048]{2,1,0:T(8,128)(2,1)} %array.1, s32[]{:T(128)S(6)} %select_n.15, s32[]{:T(128)S(6)} %select_n.14), kind=kLoop, calls=%fused_computation.7 | loop fusion | bytes 262152 | tf_op jit(solution)/shard_map/dynamic_slice | solution.py:433
  1.6 0.5 %collective-permute-start = (bf16[1,16,2048]{2,1,0:T(8,128)(2,1)S(1)}, bf16[1,16,2048]{2,1,0:T(8,128)(2,1)S(1)}, u32[]{:S(2)}, u32[]{:S(2)}) collective-permute-start(bf16[1,16,2048]{2,1,0:T(8,128)(2,1)S(1)} %get-tuple-element.43), channel_id=1, source_target_pairs={{0,8},{1,9},{2,10},{3,11},{4,12},{5,13},{6,14},{7,15},{8,0},{9,1},... | collective-permute-start | bytes 196616 | tf_op jit(solution)/shard_map/ppermute | solution.py:404
  2.1 2.6 %collective-permute-start.1 = (bf16[1,16,2048]{2,1,0:T(8,128)(2,1)S(1)}, bf16[1,16,2048]{2,1,0:T(8,128)(2,1)S(1)}, u32[]{:S(2)}, u32[]{:S(2)}) collective-permute-start(bf16[1,16,2048]{2,1,0:T(8,128)(2,1)S(1)} %get-tuple-element.44), channel_id=1, source_target_pairs={{0,24},{1,25},{2,26},{3,27},{4,28},{5,29},{6,30},{7,31},{8,16},{9,... | collective-permute-start | bytes 196616 | tf_op jit(solution)/shard_map/ppermute | solution.py:404
  4.8 0.0 copy-done.2
  4.8 0.2 copy.9
  5.0 0.0 copy-start
  5.0 0.2 reshape.25
  5.2 0.1 pad_bitcast_fusion.3
  5.3 0.0 copy-start.3
  5.3 0.6 %copy-done.3 = f32[32]{0:T(128)S(1)} copy-done((f32[32]{0:T(128)S(1)}, f32[32]{0:T(128)}, u32[]{:S(2)}) %copy-start.3) | copy-done | bytes 152
  6.0 0.1 broadcast_in_dim.2.refs_1_.bias
  6.0 0.0 copy-done
  6.0 0.3 shard_map.67.field.vx
  6.3 0.0 copy-start.1
  6.4 0.0 collective-permute-done.xeven
  6.4 0.8 %collective-permute-done.1.xodd = bf16[1,16,2048]{2,1,0:T(8,128)(2,1)S(1)} collective-permute-done((bf16[1,16,2048]{2,1,0:T(8,128)(2,1)S(1)}, bf16[1,16,2048]{2,1,0:T(8,128)(2,1)S(1)}, u32[]{:S(2)}, u32[]{:S(2)}) %collective-permute-start.1) | collective-permute-done | bytes 65568 | tf_op jit(solution)/shard_map/ppermute | solution.py:404
  7.1 0.2 shard_map.68
  7.4 0.2 collective-permute-start.2
  7.6 0.1 shard_map.69
  7.7 2.9 %collective-permute-start.3 = (bf16[5,32,128]{2,1,0:T(8,128)(2,1)S(1)}, bf16[5,32,128]{2,1,0:T(8,128)(2,1)S(1)}, u32[]{:S(2)}, u32[]{:S(2)}) collective-permute-start(bf16[5,32,128]{2,1,0:T(8,128)(2,1)S(1)} %shard_map.69), channel_id=1, source_target_pairs={{0,1},{1,0},{2,3},{3,2},{4,5},{5,4},{6,7},{7,6},{8,9},{9,8},{10,11... | collective-permute-start | bytes 122888 | tf_op jit(solution)/shard_map/ppermute | solution.py:404
  10.6 0.0 copy-done.1
  10.6 0.3 shard_map.70.gx
  10.9 2.2 %shard_map.71 = (bf16[8,32,768]{2,1,0:T(8,128)(2,1)S(1)}, f32[64,128]{1,0:T(8,128)S(1)}, f32[384,192]{1,0:T(8,128)S(1)}) custom-call(bf16[8,32,1024]{2,1,0:T(8,128)(2,1)S(1)} %shard_map.67.field.vx, bf16[8,32,1024]{2,1,0:T(8,128)(2,1)S(1)} %shard_map.70.gx, bf16[32,1024]{1,0:T(8,128)(2,1)S(1)} %get-tuple-element.48.xlow, ...), custom_call_target="tpu_custom_call" | custom-call | flops 1000000 | bytes 2064384 | tf_op jit(solution)/shard_map/pallas_call | solution.py:24
  13.0 0.0 collective-permute-done.2.yodd
  13.1 0.0 collective-permute-done.3.yeven
  13.1 1.4 %shard_map.72 = (bf16[8,32,256]{2,1,0:T(8,128)(2,1)S(1)}, f32[112,128]{1,0:T(8,128)S(1)}, f32[112,128]{1,0:T(8,128)S(1)}) custom-call(bf16[8,32,1024]{2,1,0:T(8,128)(2,1)S(1)} %shard_map.67.field.vx, bf16[8,32,1024]{2,1,0:T(8,128)(2,1)S(1)} %shard_map.70.gx, bf16[32,1024]{1,0:T(8,128)(2,1)S(1)} %get-tuple-element.48.xlow, ...), custom_call_target="tpu_custom_call" | custom-call | flops 700000000 | bytes 1998848 | tf_op jit(solution)/shard_map/pallas_call | solution.py:24
  14.5 0.1 collective-permute-start.4
  14.6 1.2 %collective-permute-done.4.b = f32[112,128]{1,0:T(8,128)S(1)} collective-permute-done((f32[112,128]{1,0:T(8,128)S(1)}, f32[112,128]{1,0:T(8,128)S(1)}, u32[]{:S(2)}, u32[]{:S(2)}) %collective-permute-start.4) | collective-permute-done | bytes 57376 | tf_op jit(solution)/shard_map/ppermute | solution.py:404
  15.8 1.3 %collective-permute-start.5 = (bf16[112,128]{1,0:T(8,128)(2,1)S(1)}, bf16[112,128]{1,0:T(8,128)(2,1)S(1)}, u32[]{:S(2)}, u32[]{:S(2)}) collective-permute-start(bf16[112,128]{1,0:T(8,128)(2,1)S(1)} %shard_map.73.a), channel_id=1, source_target_pairs={{0,24},{1,25},{2,26},{3,27},{4,28},{5,29},{6,30},{7,31},{8,16},{9,... | collective-permute-start | bytes 86024 | tf_op jit(solution)/shard_map/ppermute | solution.py:404
  17.2 0.2 copy.11
  17.3 0.2 reshape.27
  17.6 0.4 %collective-permute-start.7 = (bf16[32,1024]{1,0:T(8,128)(2,1)S(1)}, bf16[32,1024]{1,0:T(8,128)(2,1)S(1)}, u32[]{:S(2)}, u32[]{:S(2)}) collective-permute-start(bf16[32,1024]{1,0:T(8,128)(2,1)S(1)} %get-tuple-element.62), channel_id=1, source_target_pairs={{0,8},{1,9},{2,10},{3,11},{4,12},{5,13},{6,14},{7,15},{8,0},{9,1},... | collective-permute-start | bytes 196616 | tf_op jit(solution)/shard_map/ppermute | solution.py:404
  18.0 0.3 collective-permute-start.8
  18.3 0.9 %collective-permute-done.5.b = bf16[112,128]{1,0:T(8,128)(2,1)S(1)} collective-permute-done((bf16[112,128]{1,0:T(8,128)(2,1)S(1)}, bf16[112,128]{1,0:T(8,128)(2,1)S(1)}, u32[]{:S(2)}, u32[]{:S(2)}) %collective-permute-start.5) | collective-permute-done | bytes 28704 | tf_op jit(solution)/shard_map/ppermute | solution.py:404
  19.2 1.3 %collective-permute-start.6 = (bf16[112,128]{1,0:T(8,128)(2,1)S(1)}, bf16[112,128]{1,0:T(8,128)(2,1)S(1)}, u32[]{:S(2)}, u32[]{:S(2)}) collective-permute-start(bf16[112,128]{1,0:T(8,128)(2,1)S(1)} %shard_map.74.a), channel_id=1, source_target_pairs={{0,9},{1,8},{2,11},{3,10},{4,13},{5,12},{6,15},{7,14},{8,1},{9,0},... | collective-permute-start | bytes 86024 | tf_op jit(solution)/shard_map/ppermute | solution.py:404
  20.5 0.1 pad_bitcast_fusion.1
  20.6 2.0 %collective-permute-done.6.b = bf16[112,128]{1,0:T(8,128)(2,1)S(1)} collective-permute-done((bf16[112,128]{1,0:T(8,128)(2,1)S(1)}, bf16[112,128]{1,0:T(8,128)(2,1)S(1)}, u32[]{:S(2)}, u32[]{:S(2)}) %collective-permute-start.6) | collective-permute-done | bytes 28704 | tf_op jit(solution)/shard_map/ppermute | solution.py:404
  22.6 0.0 collective-permute-done.7.xeven
  22.6 0.0 collective-permute-done.8.xodd
  22.6 1.4 %collective-permute-start.9 = (bf16[112,128]{1,0:T(8,128)(2,1)S(1)}, bf16[112,128]{1,0:T(8,128)(2,1)S(1)}, u32[]{:S(2)}, u32[]{:S(2)}) collective-permute-start(bf16[112,128]{1,0:T(8,128)(2,1)S(1)} %shard_map.75.a), channel_id=1, source_target_pairs={{0,10},{1,11},{2,8},{3,9},{4,14},{5,15},{6,12},{7,13},{8,2},{9,3},... | collective-permute-start | bytes 86024 | tf_op jit(solution)/shard_map/ppermute | solution.py:404
  24.0 0.1 shard_map.78
  24.2 0.1 shard_map.79
  24.3 1.5 %collective-permute-start.12 = (bf16[5,32,128]{2,1,0:T(8,128)(2,1)S(1)}, bf16[5,32,128]{2,1,0:T(8,128)(2,1)S(1)}, u32[]{:S(2)}, u32[]{:S(2)}) collective-permute-start(bf16[5,32,128]{2,1,0:T(8,128)(2,1)S(1)} %shard_map.79), channel_id=1, source_target_pairs={{0,1},{1,0},{2,3},{3,2},{4,5},{5,4},{6,7},{7,6},{8,9},{9,8},{10,11... | collective-permute-start | bytes 122888 | tf_op jit(solution)/shard_map/ppermute | solution.py:404
  25.8 0.1 collective-permute-start.11
  25.9 0.1 collective-permute-done.9.b
  26.0 2.4 %collective-permute-start.10 = (bf16[112,128]{1,0:T(8,128)(2,1)S(1)}, bf16[112,128]{1,0:T(8,128)(2,1)S(1)}, u32[]{:S(2)}, u32[]{:S(2)}) collective-permute-start(bf16[112,128]{1,0:T(8,128)(2,1)S(1)} %shard_map.77.a), channel_id=1, source_target_pairs={{0,12},{1,13},{2,14},{3,15},{4,8},{5,9},{6,10},{7,11},{8,4},{9,5},... | collective-permute-start | bytes 86024 | tf_op jit(solution)/shard_map/ppermute | solution.py:404
  28.4 0.0 collective-permute-done.12.yeven
  28.4 0.0 collective-permute-done.11.yodd
  28.4 1.4 %shard_map.80.block = bf16[8,16,2048]{2,1,0:T(8,128)(2,1)S(1)} custom-call(bf16[8,32,768]{2,1,0:T(8,128)(2,1)S(1)} %get-tuple-element.66.mid.gmid, bf16[8,32,256]{2,1,0:T(8,128)(2,1)S(1)} %get-tuple-element.67.edge.field.gedge, bf16[32,1024]{1,0:T(8,128)(2,1)S(1)} %get-tuple-element.70.xlow, bf16[32,1024]{1,0:T(8,128)(2,1)S(1)} %get-tuple-element.71.xhigh, ...), custom_call_target="tpu_custom_call" | custom-call | flops 1000000000 | bytes 1409024 | tf_op jit(solution)/shard_map/pallas_call | solution.py:24
  29.8 0.5 %collective-permute-done.10.b = bf16[112,128]{1,0:T(8,128)(2,1)S(1)} collective-permute-done((bf16[112,128]{1,0:T(8,128)(2,1)S(1)}, bf16[112,128]{1,0:T(8,128)(2,1)S(1)}, u32[]{:S(2)}, u32[]{:S(2)}) %collective-permute-start.10) | collective-permute-done | bytes 28704 | tf_op jit(solution)/shard_map/ppermute | solution.py:404
  30.2 0.4 %collective-permute-start.13 = (f32[112,128]{1,0:T(8,128)S(1)}, f32[112,128]{1,0:T(8,128)S(1)}, u32[]{:S(2)}, u32[]{:S(2)}) collective-permute-start(f32[112,128]{1,0:T(8,128)S(1)} %shard_map.81.refs_0_), channel_id=1, source_target_pairs={{0,8},{1,9},{2,10},{3,11},{4,12},{5,13},{6,14},{7,15},{8,0},{9,1},... | collective-permute-start | bytes 172040 | tf_op jit(solution)/shard_map/ppermute | solution.py:404
  30.7 0.8 %shard_map.82 = bf16[8,16,2048]{2,1,0:T(8,128)(2,1)} custom-call(bf16[8,16,2048]{2,1,0:T(8,128)(2,1)S(1)} %shard_map.80.block), custom_call_target="tpu_custom_call" | custom-call | flops 100000 | bytes 1048576 | tf_op jit(solution)/shard_map/pallas_call | solution.py:24
  31.5 0.1 collective-permute-done.13.refs_1_
  31.6 0.9 %shard_map.83 = (f32[27,32,32]{2,1,0:T(8,128)}, f32[1,32]{1,0:T(1,128)}) custom-call(f32[112,128]{1,0:T(8,128)S(1)} %shard_map.81.refs_0_, f32[112,128]{1,0:T(8,128)S(1)} %collective-permute-done.13.refs_1_), custom_call_target="tpu_custom_call" | custom-call | flops 100000 | bytes 225408 | tf_op jit(solution)/shard_map/pallas_call | solution.py:24
  (11 shorter events, 0.2 us)
Async XLA Ops:
  0.6 4.1 %copy-start.2 = (bf16[3,3,3,32,32]{4,3,2,1,0:T(8,128)(2,1)S(1)}, bf16[3,3,3,32,32]{4,3,2,1,0:T(8,128)(2,1)}, u32[]{:S(2)}) copy-start(bf16[3,3,3,32,32]{4,3,2,1,0:T(8,128)(2,1)} %param.6) | copy-start | bytes 165892
  1.6 4.8 %collective-permute-start = (bf16[1,16,2048]{2,1,0:T(8,128)(2,1)S(1)}, bf16[1,16,2048]{2,1,0:T(8,128)(2,1)S(1)}, u32[]{:S(2)}, u32[]{:S(2)}) collective-permute-start(bf16[1,16,2048]{2,1,0:T(8,128)(2,1)S(1)} %get-tuple-element.43), channel_id=1, source_target_pairs={{0,8},{1,9},{2,10},{3,11},{4,12},{5,13},{6,14},{7,15},{8,0},{9,1},... | collective-permute-start | bytes 196616 | tf_op jit(solution)/shard_map/ppermute | solution.py:404
  2.1 5.0 %collective-permute-start.1 = (bf16[1,16,2048]{2,1,0:T(8,128)(2,1)S(1)}, bf16[1,16,2048]{2,1,0:T(8,128)(2,1)S(1)}, u32[]{:S(2)}, u32[]{:S(2)}) collective-permute-start(bf16[1,16,2048]{2,1,0:T(8,128)(2,1)S(1)} %get-tuple-element.44), channel_id=1, source_target_pairs={{0,24},{1,25},{2,26},{3,27},{4,28},{5,29},{6,30},{7,31},{8,16},{9,... | collective-permute-start | bytes 196616 | tf_op jit(solution)/shard_map/ppermute | solution.py:404
  5.0 1.1 %copy-start = (bf16[8,16,2048]{2,1,0:T(8,128)(2,1)S(1)}, bf16[8,16,2048]{2,1,0:T(8,128)(2,1)}, u32[]{:S(2)}) copy-start(bf16[8,16,2048]{2,1,0:T(8,128)(2,1)} %array.1) | copy-start | bytes 1572868
  5.3 0.7 %copy-start.3 = (f32[32]{0:T(128)S(1)}, f32[32]{0:T(128)}, u32[]{:S(2)}) copy-start(f32[32]{0:T(128)} %param.7) | copy-start | bytes 388
  6.3 4.2 %copy-start.1 = (bf16[8,16,2048]{2,1,0:T(8,128)(2,1)S(1)}, bf16[8,16,2048]{2,1,0:T(8,128)(2,1)}, u32[]{:S(2)}) copy-start(bf16[8,16,2048]{2,1,0:T(8,128)(2,1)} %array.2) | copy-start | bytes 1572868
  7.4 5.7 %collective-permute-start.2 = (bf16[5,32,128]{2,1,0:T(8,128)(2,1)S(1)}, bf16[5,32,128]{2,1,0:T(8,128)(2,1)S(1)}, u32[]{:S(2)}, u32[]{:S(2)}) collective-permute-start(bf16[5,32,128]{2,1,0:T(8,128)(2,1)S(1)} %get-tuple-element.50), channel_id=1, source_target_pairs={{0,8},{1,2},{2,1},{3,4},{4,3},{5,6},{6,5},{7,15},{8,0},{9,10},{10,... | collective-permute-start | bytes 122888 | tf_op jit(solution)/shard_map/ppermute | solution.py:404
  7.7 5.4 %collective-permute-start.3 = (bf16[5,32,128]{2,1,0:T(8,128)(2,1)S(1)}, bf16[5,32,128]{2,1,0:T(8,128)(2,1)S(1)}, u32[]{:S(2)}, u32[]{:S(2)}) collective-permute-start(bf16[5,32,128]{2,1,0:T(8,128)(2,1)S(1)} %shard_map.69), channel_id=1, source_target_pairs={{0,1},{1,0},{2,3},{3,2},{4,5},{5,4},{6,7},{7,6},{8,9},{9,8},{10,11... | collective-permute-start | bytes 122888 | tf_op jit(solution)/shard_map/ppermute | solution.py:404
  14.5 1.3 %collective-permute-start.4 = (f32[112,128]{1,0:T(8,128)S(1)}, f32[112,128]{1,0:T(8,128)S(1)}, u32[]{:S(2)}, u32[]{:S(2)}) collective-permute-start(f32[112,128]{1,0:T(8,128)S(1)} %get-tuple-element.57), channel_id=1, source_target_pairs={{0,8},{1,9},{2,10},{3,11},{4,12},{5,13},{6,14},{7,15},{8,0},{9,1},... | collective-permute-start | bytes 172040 | tf_op jit(solution)/shard_map/ppermute | solution.py:404
  15.8 3.4 %collective-permute-start.5 = (bf16[112,128]{1,0:T(8,128)(2,1)S(1)}, bf16[112,128]{1,0:T(8,128)(2,1)S(1)}, u32[]{:S(2)}, u32[]{:S(2)}) collective-permute-start(bf16[112,128]{1,0:T(8,128)(2,1)S(1)} %shard_map.73.a), channel_id=1, source_target_pairs={{0,24},{1,25},{2,26},{3,27},{4,28},{5,29},{6,30},{7,31},{8,16},{9,... | collective-permute-start | bytes 86024 | tf_op jit(solution)/shard_map/ppermute | solution.py:404
  17.6 5.0 %collective-permute-start.7 = (bf16[32,1024]{1,0:T(8,128)(2,1)S(1)}, bf16[32,1024]{1,0:T(8,128)(2,1)S(1)}, u32[]{:S(2)}, u32[]{:S(2)}) collective-permute-start(bf16[32,1024]{1,0:T(8,128)(2,1)S(1)} %get-tuple-element.62), channel_id=1, source_target_pairs={{0,8},{1,9},{2,10},{3,11},{4,12},{5,13},{6,14},{7,15},{8,0},{9,1},... | collective-permute-start | bytes 196616 | tf_op jit(solution)/shard_map/ppermute | solution.py:404
  18.0 4.6 %collective-permute-start.8 = (bf16[32,1024]{1,0:T(8,128)(2,1)S(1)}, bf16[32,1024]{1,0:T(8,128)(2,1)S(1)}, u32[]{:S(2)}, u32[]{:S(2)}) collective-permute-start(bf16[32,1024]{1,0:T(8,128)(2,1)S(1)} %get-tuple-element.63), channel_id=1, source_target_pairs={{0,24},{1,25},{2,26},{3,27},{4,28},{5,29},{6,30},{7,31},{8,16},{9,... | collective-permute-start | bytes 196616 | tf_op jit(solution)/shard_map/ppermute | solution.py:404
  19.2 3.4 %collective-permute-start.6 = (bf16[112,128]{1,0:T(8,128)(2,1)S(1)}, bf16[112,128]{1,0:T(8,128)(2,1)S(1)}, u32[]{:S(2)}, u32[]{:S(2)}) collective-permute-start(bf16[112,128]{1,0:T(8,128)(2,1)S(1)} %shard_map.74.a), channel_id=1, source_target_pairs={{0,9},{1,8},{2,11},{3,10},{4,13},{5,12},{6,15},{7,14},{8,1},{9,0},... | collective-permute-start | bytes 86024 | tf_op jit(solution)/shard_map/ppermute | solution.py:404
  22.6 3.4 %collective-permute-start.9 = (bf16[112,128]{1,0:T(8,128)(2,1)S(1)}, bf16[112,128]{1,0:T(8,128)(2,1)S(1)}, u32[]{:S(2)}, u32[]{:S(2)}) collective-permute-start(bf16[112,128]{1,0:T(8,128)(2,1)S(1)} %shard_map.75.a), channel_id=1, source_target_pairs={{0,10},{1,11},{2,8},{3,9},{4,14},{5,15},{6,12},{7,13},{8,2},{9,3},... | collective-permute-start | bytes 86024 | tf_op jit(solution)/shard_map/ppermute | solution.py:404
  24.3 4.1 %collective-permute-start.12 = (bf16[5,32,128]{2,1,0:T(8,128)(2,1)S(1)}, bf16[5,32,128]{2,1,0:T(8,128)(2,1)S(1)}, u32[]{:S(2)}, u32[]{:S(2)}) collective-permute-start(bf16[5,32,128]{2,1,0:T(8,128)(2,1)S(1)} %shard_map.79), channel_id=1, source_target_pairs={{0,1},{1,0},{2,3},{3,2},{4,5},{5,4},{6,7},{7,6},{8,9},{9,8},{10,11... | collective-permute-start | bytes 122888 | tf_op jit(solution)/shard_map/ppermute | solution.py:404
  25.8 2.6 %collective-permute-start.11 = (bf16[5,32,128]{2,1,0:T(8,128)(2,1)S(1)}, bf16[5,32,128]{2,1,0:T(8,128)(2,1)S(1)}, u32[]{:S(2)}, u32[]{:S(2)}) collective-permute-start(bf16[5,32,128]{2,1,0:T(8,128)(2,1)S(1)} %get-tuple-element.72), channel_id=1, source_target_pairs={{0,8},{1,2},{2,1},{3,4},{4,3},{5,6},{6,5},{7,15},{8,0},{9,10},{10,... | collective-permute-start | bytes 122888 | tf_op jit(solution)/shard_map/ppermute | solution.py:404
  26.0 4.3 %collective-permute-start.10 = (bf16[112,128]{1,0:T(8,128)(2,1)S(1)}, bf16[112,128]{1,0:T(8,128)(2,1)S(1)}, u32[]{:S(2)}, u32[]{:S(2)}) collective-permute-start(bf16[112,128]{1,0:T(8,128)(2,1)S(1)} %shard_map.77.a), channel_id=1, source_target_pairs={{0,12},{1,13},{2,14},{3,15},{4,8},{5,9},{6,10},{7,11},{8,4},{9,5},... | collective-permute-start | bytes 86024 | tf_op jit(solution)/shard_map/ppermute | solution.py:404
  30.2 1.3 %collective-permute-start.13 = (f32[112,128]{1,0:T(8,128)S(1)}, f32[112,128]{1,0:T(8,128)S(1)}, u32[]{:S(2)}, u32[]{:S(2)}) collective-permute-start(f32[112,128]{1,0:T(8,128)S(1)} %shard_map.81.refs_0_), channel_id=1, source_target_pairs={{0,8},{1,9},{2,10},{3,11},{4,12},{5,13},{6,14},{7,15},{8,0},{9,1},... | collective-permute-start | bytes 172040 | tf_op jit(solution)/shard_map/ppermute | solution.py:404
